TPU v7x, 512 devices: a whole 4x8x8 slice. The times are simulated.
512 devices in a mesh: grp: 16 (over z_lo, x), layer: 32 (over y, z_hi, core).
Axes of the slice: x: 4, y: 8, z: 8 (z_hi: 2, z_lo: 4; z = z_hi * 4 + z_lo), core: 2. Of those that a mesh axis runs over, the one named last changes fastest.
Arguments:
- grads: bfloat16 [32, 3072, 4096], P('layer', 'grp'), may hold values from -6 to 6
- in_factor: float32 [32, 64, 64], P('layer'), may hold values from -0.02 to 3, as said below
- out_factor: float32 [32, 64, 64], P('layer'), may hold values from -0.02 to 3, as said below
Outputs:
- scores: float32 [3072, 9, 192], P('grp', None, 'layer')
Inputs may be any that keep to these rules, and one draw needn't show every extreme that they name: `in_factor`: each layer's matrix is symmetric, and every diagonal entry exceeds the sum of magnitudes of the other entries of its row. `out_factor`: each layer's matrix is symmetric, and every diagonal entry exceeds the sum of magnitudes of the other entries of its row.
All inputs are finite; a program needn't handle non-finite values.
Results may differ from a plain program's by a relative error of at most 0.00034.
Values may be sent and summed in bfloat16 or wider, within the bound.
No kernel may reach another device: no remote copies, remote signals or barrier semaphores. Data moves between devices by JAX's collectives and lax.ppermute only.
A program may use at most 64 MiB of HBM per device.

v0:
```python
import math

import jax
import jax.numpy as jnp
from jax import lax
from jax.sharding import PartitionSpec as P


def shifted(value, axis, steps):
    count = lax.axis_size(axis)
    pairs = [(source, (source + steps) % count) for source in range(count)]
    return lax.ppermute(value, axis, pairs)


def cross_block(left_rows, right_rows):
    return lax.dot_general(
        left_rows, right_rows, (((1,), (1,)), ((), ())), preferred_element_type=jnp.float32
    )


def per_device(grads, in_factor, out_factor):
    layers_here, rows, width = grads.shape
    k_in = in_factor.shape[1]
    k_out = out_factor.shape[1]
    groups = lax.axis_size("grp")
    half_span = groups // 2
    factor = 1.0 / math.sqrt(layers_here * lax.axis_size("layer") * width)
    matrix = grads.astype(jnp.float32).reshape(layers_here, rows, k_out, k_in)
    left = jnp.einsum("lpo,lboi->lbpi", out_factor, matrix, precision=lax.Precision.HIGHEST)
    right = jnp.einsum("lbpi,liq->lbpq", left, in_factor, precision=lax.Precision.HIGHEST)
    weighted = right.astype(jnp.bfloat16).transpose(1, 0, 2, 3).reshape(rows, layers_here * width)
    plain = grads.transpose(1, 0, 2).reshape(rows, layers_here * width)
    blocks = [cross_block(weighted, plain)]
    current = plain
    for offset in range(1, half_span + 1):
        current = shifted(current, "grp", -1)
        blocks.append(cross_block(weighted, current))
    whole = lax.psum_scatter(jnp.stack(blocks, axis=1), "layer", scatter_dimension=2, tiled=True)
    summed = [whole[:, offset] for offset in range(len(blocks))]
    band = jnp.stack(summed, axis=1)
    return band * factor


def solution(mesh):
    in_specs = (P("layer", "grp", None), P("layer", None, None), P("layer", None, None))
    out_specs = P("grp", None, "layer")
    return jax.shard_map(
        per_device, mesh=mesh, in_specs=in_specs, out_specs=out_specs, check_vma=False
    )
```

profile of v0, /device:TPU:2, one launch (start us, length us, event | category | flops | bytes accessed | tf_op | source)
XLA Modules:
  0.0 477.9 jit_solution(4910496777213760540)
XLA Ops:
  6.5 7.9 %collective-permute-start = (bf16[192,4096]{1,0:T(8,128)(2,1)}, bf16[192,4096]{1,0:T(8,128)(2,1)S(1)}, u32[]{:S(2)}, u32[]{:S(2)}) collective-permute-start(bf16[192,4096]{1,0:T(8,128)(2,1)} %bitcast.83), channel_id=1, source_target_pairs={{0,480},{32,0},{64,32},{96,64},{128,96},{160,128},{192,160},{224,1... | collective-permute-start | bytes 4718600 | tf_op jit(solution)/shard_map/ppermute | solution.py:12
  14.5 30.4 %collective-permute-done = bf16[192,4096]{1,0:T(8,128)(2,1)S(1)} collective-permute-done((bf16[192,4096]{1,0:T(8,128)(2,1)}, bf16[192,4096]{1,0:T(8,128)(2,1)S(1)}, u32[]{:S(2)}, u32[]{:S(2)}) %collective-permute-start) | collective-permute-done | bytes 1572896 | tf_op jit(solution)/shard_map/ppermute | solution.py:12
  44.9 8.2 %collective-permute-start.1 = (bf16[192,4096]{1,0:T(8,128)(2,1)S(1)}, bf16[192,4096]{1,0:T(8,128)(2,1)S(1)}, u32[]{:S(2)}, u32[]{:S(2)}) collective-permute-start(bf16[192,4096]{1,0:T(8,128)(2,1)S(1)} %collective-permute-done), channel_id=1, source_target_pairs={{0,480},{32,0},{64,32},{96,64},{128,96},{160,128},{192,160},{224,1... | collective-permute-start | bytes 4718600 | tf_op jit(solution)/shard_map/ppermute | solution.py:12
  53.1 32.8 %collective-permute-done.1 = bf16[192,4096]{1,0:T(8,128)(2,1)S(1)} collective-permute-done((bf16[192,4096]{1,0:T(8,128)(2,1)S(1)}, bf16[192,4096]{1,0:T(8,128)(2,1)S(1)}, u32[]{:S(2)}, u32[]{:S(2)}) %collective-permute-start.1) | collective-permute-done | bytes 1572896 | tf_op jit(solution)/shard_map/ppermute | solution.py:12
  85.9 8.2 %collective-permute-start.2 = (bf16[192,4096]{1,0:T(8,128)(2,1)S(1)}, bf16[192,4096]{1,0:T(8,128)(2,1)S(1)}, u32[]{:S(2)}, u32[]{:S(2)}) collective-permute-start(bf16[192,4096]{1,0:T(8,128)(2,1)S(1)} %collective-permute-done.1), channel_id=1, source_target_pairs={{0,480},{32,0},{64,32},{96,64},{128,96},{160,128},{192,160},{224,1... | collective-permute-start | bytes 4718600 | tf_op jit(solution)/shard_map/ppermute | solution.py:12
  94.1 31.8 %collective-permute-done.2 = bf16[192,4096]{1,0:T(8,128)(2,1)S(1)} collective-permute-done((bf16[192,4096]{1,0:T(8,128)(2,1)S(1)}, bf16[192,4096]{1,0:T(8,128)(2,1)S(1)}, u32[]{:S(2)}, u32[]{:S(2)}) %collective-permute-start.2) | collective-permute-done | bytes 1572896 | tf_op jit(solution)/shard_map/ppermute | solution.py:12
  125.9 8.3 %collective-permute-start.3 = (bf16[192,4096]{1,0:T(8,128)(2,1)S(1)}, bf16[192,4096]{1,0:T(8,128)(2,1)S(1)}, u32[]{:S(2)}, u32[]{:S(2)}) collective-permute-start(bf16[192,4096]{1,0:T(8,128)(2,1)S(1)} %collective-permute-done.2), channel_id=1, source_target_pairs={{0,480},{32,0},{64,32},{96,64},{128,96},{160,128},{192,160},{224,1... | collective-permute-start | bytes 4718600 | tf_op jit(solution)/shard_map/ppermute | solution.py:12
  134.2 30.9 %collective-permute-done.3 = bf16[192,4096]{1,0:T(8,128)(2,1)S(1)} collective-permute-done((bf16[192,4096]{1,0:T(8,128)(2,1)S(1)}, bf16[192,4096]{1,0:T(8,128)(2,1)S(1)}, u32[]{:S(2)}, u32[]{:S(2)}) %collective-permute-start.3) | collective-permute-done | bytes 1572896 | tf_op jit(solution)/shard_map/ppermute | solution.py:12
  165.2 8.3 %collective-permute-start.4 = (bf16[192,4096]{1,0:T(8,128)(2,1)S(1)}, bf16[192,4096]{1,0:T(8,128)(2,1)}, u32[]{:S(2)}, u32[]{:S(2)}) collective-permute-start(bf16[192,4096]{1,0:T(8,128)(2,1)S(1)} %collective-permute-done.3), channel_id=1, source_target_pairs={{0,480},{32,0},{64,32},{96,64},{128,96},{160,128},{192,160},{224,1... | collective-permute-start | bytes 4718600 | tf_op jit(solution)/shard_map/ppermute | solution.py:12
  173.4 30.0 %collective-permute-done.4 = bf16[192,4096]{1,0:T(8,128)(2,1)} collective-permute-done((bf16[192,4096]{1,0:T(8,128)(2,1)S(1)}, bf16[192,4096]{1,0:T(8,128)(2,1)}, u32[]{:S(2)}, u32[]{:S(2)}) %collective-permute-start.4) | collective-permute-done | bytes 1572896 | tf_op jit(solution)/shard_map/ppermute | solution.py:12
  203.5 8.3 %collective-permute-start.5 = (bf16[192,4096]{1,0:T(8,128)(2,1)}, bf16[192,4096]{1,0:T(8,128)(2,1)}, u32[]{:S(2)}, u32[]{:S(2)}) collective-permute-start(bf16[192,4096]{1,0:T(8,128)(2,1)} %collective-permute-done.4), channel_id=1, source_target_pairs={{0,480},{32,0},{64,32},{96,64},{128,96},{160,128},{192,160},{224,1... | collective-permute-start | bytes 4718600 | tf_op jit(solution)/shard_map/ppermute | solution.py:12
  211.8 3.2 copy.19
  214.9 26.2 %collective-permute-done.5 = bf16[192,4096]{1,0:T(8,128)(2,1)} collective-permute-done((bf16[192,4096]{1,0:T(8,128)(2,1)}, bf16[192,4096]{1,0:T(8,128)(2,1)}, u32[]{:S(2)}, u32[]{:S(2)}) %collective-permute-start.5) | collective-permute-done | bytes 1572896 | tf_op jit(solution)/shard_map/ppermute | solution.py:12
  241.1 8.4 %collective-permute-start.6 = (bf16[192,4096]{1,0:T(8,128)(2,1)}, bf16[192,4096]{1,0:T(8,128)(2,1)S(1)}, u32[]{:S(2)}, u32[]{:S(2)}) collective-permute-start(bf16[192,4096]{1,0:T(8,128)(2,1)} %collective-permute-done.5), channel_id=1, source_target_pairs={{0,480},{32,0},{64,32},{96,64},{128,96},{160,128},{192,160},{224,1... | collective-permute-start | bytes 4718600 | tf_op jit(solution)/shard_map/ppermute | solution.py:12
  249.6 2.7 convolution_bitcast_fusion
  252.3 5.8 %fusion.3 = bf16[192,64,64]{0,2,1:T(8,128)(2,1)S(1)} fusion(f32[192,64,64]{0,1,2:T(8,128)S(1)} %convolution_bitcast_fusion, f32[1,64,64]{2,1,0:T(8,128)S(1)} %copy-done.10), kind=kOutput, calls=%fused_computation.4 | convolution fusion | flops 604766208 | bytes 4734976 | tf_op jit(solution)/shard_map/lbpi,liq->lbpq/dot_general | solution.py:30
  261.8 16.2 %collective-permute-done.6 = bf16[192,4096]{1,0:T(8,128)(2,1)S(1)} collective-permute-done((bf16[192,4096]{1,0:T(8,128)(2,1)}, bf16[192,4096]{1,0:T(8,128)(2,1)S(1)}, u32[]{:S(2)}, u32[]{:S(2)}) %collective-permute-start.6) | collective-permute-done | bytes 1572896 | tf_op jit(solution)/shard_map/ppermute | solution.py:12
  278.0 8.5 %collective-permute-start.7 = (bf16[192,4096]{1,0:T(8,128)(2,1)S(1)}, bf16[192,4096]{1,0:T(8,128)(2,1)S(1)}, u32[]{:S(2)}, u32[]{:S(2)}) collective-permute-start(bf16[192,4096]{1,0:T(8,128)(2,1)S(1)} %collective-permute-done.6), channel_id=1, source_target_pairs={{0,480},{32,0},{64,32},{96,64},{128,96},{160,128},{192,160},{224,1... | collective-permute-start | bytes 4718600 | tf_op jit(solution)/shard_map/ppermute | solution.py:12
  288.2 2.3 fusion.9
  290.5 2.3 fusion.8
  293.6 19.9 %collective-permute-done.7 = bf16[192,4096]{1,0:T(8,128)(2,1)S(1)} collective-permute-done((bf16[192,4096]{1,0:T(8,128)(2,1)S(1)}, bf16[192,4096]{1,0:T(8,128)(2,1)S(1)}, u32[]{:S(2)}, u32[]{:S(2)}) %collective-permute-start.7) | collective-permute-done | bytes 1572896 | tf_op jit(solution)/shard_map/ppermute | solution.py:12
  314.4 3.1 copy.23
  317.5 152.0 %reduce-scatter.2.cloned.1.call-done = f32[192,9,6]{0,1,2:T(8,128)} async-done(((f32[192,9,192]{0,1,2:T(8,128)}), f32[192,9,6]{0,1,2:T(8,128)}) %reduce-scatter.2.cloned.1.call-update) | async-done | bytes 41488 | tf_op jit(solution)/shard_map/reduce_scatter | solution.py:38
  469.5 1.6 copy_multiply_fusion
  (31 shorter events, 7.1 us)
Async XLA Ops:
  6.5 243.0 %copy-start = (f32[1,64,64]{2,1,0:T(8,128)S(1)}, f32[1,64,64]{2,1,0:T(8,128)}, u32[]{:S(2)}) copy-start(f32[1,64,64]{2,1,0:T(8,128)} %param.5) | copy-start | bytes 49156
  6.5 463.0 %reduce-scatter.2.cloned.1.call-start = ((), (), s32[]{:S(2)}) async-start(), calls=%async_computation.1 | async-start | bytes 3244032 | tf_op jit(solution)/shard_map/reduce_scatter | solution.py:38
  6.5 38.4 %collective-permute-start = (bf16[192,4096]{1,0:T(8,128)(2,1)}, bf16[192,4096]{1,0:T(8,128)(2,1)S(1)}, u32[]{:S(2)}, u32[]{:S(2)}) collective-permute-start(bf16[192,4096]{1,0:T(8,128)(2,1)} %bitcast.83), channel_id=1, source_target_pairs={{0,480},{32,0},{64,32},{96,64},{128,96},{160,128},{192,160},{224,1... | collective-permute-start | bytes 4718600 | tf_op jit(solution)/shard_map/ppermute | solution.py:12
  44.9 158.5 %copy-start.2 = (bf16[192,4096]{1,0:T(8,128)(2,1)}, bf16[192,4096]{1,0:T(8,128)(2,1)S(1)}, u32[]{:S(2)}) copy-start(bf16[192,4096]{1,0:T(8,128)(2,1)S(1)} %collective-permute-done) | copy-start | bytes 4718596
  44.9 41.0 %collective-permute-start.1 = (bf16[192,4096]{1,0:T(8,128)(2,1)S(1)}, bf16[192,4096]{1,0:T(8,128)(2,1)S(1)}, u32[]{:S(2)}, u32[]{:S(2)}) collective-permute-start(bf16[192,4096]{1,0:T(8,128)(2,1)S(1)} %collective-permute-done), channel_id=1, source_target_pairs={{0,480},{32,0},{64,32},{96,64},{128,96},{160,128},{192,160},{224,1... | collective-permute-start | bytes 4718600 | tf_op jit(solution)/shard_map/ppermute | solution.py:12
  85.9 117.5 %copy-start.6 = (bf16[192,4096]{1,0:T(8,128)(2,1)}, bf16[192,4096]{1,0:T(8,128)(2,1)S(1)}, u32[]{:S(2)}) copy-start(bf16[192,4096]{1,0:T(8,128)(2,1)S(1)} %collective-permute-done.1) | copy-start | bytes 4718596
  85.9 40.0 %collective-permute-start.2 = (bf16[192,4096]{1,0:T(8,128)(2,1)S(1)}, bf16[192,4096]{1,0:T(8,128)(2,1)S(1)}, u32[]{:S(2)}, u32[]{:S(2)}) collective-permute-start(bf16[192,4096]{1,0:T(8,128)(2,1)S(1)} %collective-permute-done.1), channel_id=1, source_target_pairs={{0,480},{32,0},{64,32},{96,64},{128,96},{160,128},{192,160},{224,1... | collective-permute-start | bytes 4718600 | tf_op jit(solution)/shard_map/ppermute | solution.py:12
  125.9 77.5 %copy-start.4 = (bf16[192,4096]{1,0:T(8,128)(2,1)}, bf16[192,4096]{1,0:T(8,128)(2,1)S(1)}, u32[]{:S(2)}) copy-start(bf16[192,4096]{1,0:T(8,128)(2,1)S(1)} %collective-permute-done.2) | copy-start | bytes 4718596
  125.9 39.2 %collective-permute-start.3 = (bf16[192,4096]{1,0:T(8,128)(2,1)S(1)}, bf16[192,4096]{1,0:T(8,128)(2,1)S(1)}, u32[]{:S(2)}, u32[]{:S(2)}) collective-permute-start(bf16[192,4096]{1,0:T(8,128)(2,1)S(1)} %collective-permute-done.2), channel_id=1, source_target_pairs={{0,480},{32,0},{64,32},{96,64},{128,96},{160,128},{192,160},{224,1... | collective-permute-start | bytes 4718600 | tf_op jit(solution)/shard_map/ppermute | solution.py:12
  165.1 38.3 %copy-start.8 = (bf16[192,4096]{1,0:T(8,128)(2,1)}, bf16[192,4096]{1,0:T(8,128)(2,1)S(1)}, u32[]{:S(2)}) copy-start(bf16[192,4096]{1,0:T(8,128)(2,1)S(1)} %collective-permute-done.3) | copy-start | bytes 4718596
  165.2 38.3 %collective-permute-start.4 = (bf16[192,4096]{1,0:T(8,128)(2,1)S(1)}, bf16[192,4096]{1,0:T(8,128)(2,1)}, u32[]{:S(2)}, u32[]{:S(2)}) collective-permute-start(bf16[192,4096]{1,0:T(8,128)(2,1)S(1)} %collective-permute-done.3), channel_id=1, source_target_pairs={{0,480},{32,0},{64,32},{96,64},{128,96},{160,128},{192,160},{224,1... | collective-permute-start | bytes 4718600 | tf_op jit(solution)/shard_map/ppermute | solution.py:12
  203.5 37.7 %collective-permute-start.5 = (bf16[192,4096]{1,0:T(8,128)(2,1)}, bf16[192,4096]{1,0:T(8,128)(2,1)}, u32[]{:S(2)}, u32[]{:S(2)}) collective-permute-start(bf16[192,4096]{1,0:T(8,128)(2,1)} %collective-permute-done.4), channel_id=1, source_target_pairs={{0,480},{32,0},{64,32},{96,64},{128,96},{160,128},{192,160},{224,1... | collective-permute-start | bytes 4718600 | tf_op jit(solution)/shard_map/ppermute | solution.py:12
  241.1 36.9 %collective-permute-start.6 = (bf16[192,4096]{1,0:T(8,128)(2,1)}, bf16[192,4096]{1,0:T(8,128)(2,1)S(1)}, u32[]{:S(2)}, u32[]{:S(2)}) collective-permute-start(bf16[192,4096]{1,0:T(8,128)(2,1)} %collective-permute-done.5), channel_id=1, source_target_pairs={{0,480},{32,0},{64,32},{96,64},{128,96},{160,128},{192,160},{224,1... | collective-permute-start | bytes 4718600 | tf_op jit(solution)/shard_map/ppermute | solution.py:12
  249.6 2.7 copy-start.10
  252.3 5.8 %copy-start.1 = (bf16[1,192,4096]{2,1,0:T(8,128)(2,1)S(1)}, bf16[1,192,4096]{2,1,0:T(8,128)(2,1)}, u32[]{:S(2)}) copy-start(bf16[1,192,4096]{2,1,0:T(8,128)(2,1)} %param.3) | copy-start | bytes 4718596
  258.1 1.4 copy-start.3
  259.5 1.4 copy-start.7
  260.9 25.6 %copy-start.5 = (bf16[192,4096]{1,0:T(8,128)(2,1)S(1)}, bf16[192,4096]{1,0:T(8,128)(2,1)}, u32[]{:S(2)}) copy-start(bf16[192,4096]{1,0:T(8,128)(2,1)} %copy-done.4) | copy-start | bytes 4718596
  261.8 25.6 %copy-start.9 = (bf16[192,4096]{1,0:T(8,128)(2,1)S(1)}, bf16[192,4096]{1,0:T(8,128)(2,1)}, u32[]{:S(2)}) copy-start(bf16[192,4096]{1,0:T(8,128)(2,1)} %copy-done.8) | copy-start | bytes 4718596
  278.0 35.5 %collective-permute-start.7 = (bf16[192,4096]{1,0:T(8,128)(2,1)S(1)}, bf16[192,4096]{1,0:T(8,128)(2,1)S(1)}, u32[]{:S(2)}, u32[]{:S(2)}) collective-permute-start(bf16[192,4096]{1,0:T(8,128)(2,1)S(1)} %collective-permute-done.6), channel_id=1, source_target_pairs={{0,480},{32,0},{64,32},{96,64},{128,96},{160,128},{192,160},{224,1... | collective-permute-start | bytes 4718600 | tf_op jit(solution)/shard_map/ppermute | solution.py:12
Sparse Core Ops, SparseCore 0:
  317.6 151.8 reduce-scatter.1
where the time goes:
time: 479 us; the launch traced here: 478 us
  waiting for transfers between devices  370 us (77%)
  starting transfers between devices  66.1 us (14%)
  matrix products  18.9 us (4%)
  between operations  13.6 us (3%)
  local copies, waits for them, and re-layouts  7.46 us (2%)
    ppermute x8, waiting for transfers between devices, shifted(): return lax.ppermute(value, axis, pairs)  218 us
    reduce_scatter x1, waiting for transfers between devices, per_device(): lax.psum_scatter(jnp.stack(blocks, axis=1), 'layer', scatter_dimension=2,...  152 us
    ppermute x8, starting transfers between devices, shifted(): return lax.ppermute(value, axis, pairs)  66.1 us
    dot_general x9, matrix products, cross_block(): lax.dot_general(left_rows, right_rows, (((1,), (1,)), ((), ())), preferre...  10.4 us
  transfers between devices with their start and end apart: 9, of which 9 were waited for; matrix products, arithmetic and copies ran while one was open for 4% of the time, Pallas kernels for 0%

commit v1 on v0

v1 whole, which is shorter than its diff:
```python
import math

import jax
import jax.numpy as jnp
from jax import lax
from jax.sharding import Mesh, PartitionSpec as P

NZ, NX, NY, NH, NC = 4, 4, 8, 2, 2


def moved(value, axis, steps):
    count = lax.axis_size(axis)
    return lax.ppermute(value, axis, [(s, (s + steps) % count) for s in range(count)])


def precondition(rows, in_mat, out_mat):
    matrix = rows.astype(jnp.float32).reshape(-1, out_mat.shape[0], in_mat.shape[0])
    left = jnp.einsum("po,boi->bpi", out_mat, matrix, precision=lax.Precision.HIGHEST)
    right = jnp.einsum("bpi,iq->bpq", left, in_mat, precision=lax.Precision.HIGHEST)
    return right.astype(jnp.bfloat16).reshape(rows.shape)


def product(plain, weighted):
    return lax.dot_general(
        plain, weighted, (((1,), (1,)), ((), ())), preferred_element_type=jnp.float32
    )


def per_device(grads, in_factor, out_factor):
    _, rows, width = grads.shape
    factor = 1.0 / math.sqrt(32 * width)
    x = lax.axis_index("x")
    plain0 = grads[0]
    plain1 = moved(plain0, "zl", -1)
    plain2 = moved(plain0, "zl", -2)
    own = precondition(plain0, in_factor[0], out_factor[0])
    weighted = [own, moved(own, "x", 1), moved(own, "x", 2), moved(own, "x", 3)]
    next_row = [product(plain1, w) for w in weighted]
    chosen = [
        jnp.where(x >= r, product(plain0, weighted[r]), product(plain2, weighted[r]))
        for r in range(1, NX)
    ]
    ends = [product(plain0, own), product(plain2, own)]
    slots = jnp.concatenate(next_row + chosen + ends, axis=1)
    lanes = 1792
    slots = jnp.pad(slots, ((0, 0), (0, lanes - slots.shape[1])))
    half = lanes // 2
    pair = jnp.stack([slots[:, :half], slots[:, half:]])
    pair = lax.all_to_all(pair, "c", 0, 0, tiled=False)
    part = (pair[0] + pair[1]).reshape(NY, rows // NY, half)
    part = lax.all_to_all(part, "y", 0, 0, tiled=False).sum(0)
    part = part.reshape(NH * NC, rows // 32, half)
    part = lax.all_to_all(part, ("zh", "c"), 0, 0, tiled=False)
    part = part.reshape(NH, NC, rows // 32, half).sum(0)
    full = part.transpose(1, 0, 2).reshape(rows // 32, lanes)[:, : 9 * rows]
    full = full.reshape(rows // 32, 9, rows) * factor
    out = [None] * 9
    out[4], out[0], out[8] = full[:, 0], full[:, 7], full[:, 8]
    for r in range(1, NX):
        both = moved(jnp.stack([full[:, r], full[:, 3 + r]]), "x", -r)
        inside = x + r < NX
        out[r] = jnp.where(inside, both[1], both[0])
        out[r + 4] = jnp.where(inside, both[0], both[1])
    return jnp.stack(out).transpose(2, 0, 1)


def solution(mesh):
    fine = Mesh(mesh.devices.reshape(NZ, NX, NY, NH, NC), ("zl", "x", "y", "zh", "c"))
    layer, group = ("y", "zh", "c"), ("zl", "x")
    in_specs = (P(layer, group, None), P(layer, None, None), P(layer, None, None))
    return jax.shard_map(
        per_device, mesh=fine, in_specs=in_specs, out_specs=P(group, None, layer), check_vma=False
    )
```

time: 479 us -> 195 us (0.41)
  the two profiles are of different devices: /device:TPU:2 before, /device:TPU:8 now
where the time goes in v1:
time: 195 us; the launch traced here: 194 us
  waiting for transfers between devices  72.3 us (37%)
  matrix products  39.5 us (20%)
  starting transfers between devices  39.2 us (20%)
  blocking collectives  32 us (16%)
  local copies, waits for them, and re-layouts  10.4 us (5%)
    ppermute x8, waiting for transfers between devices, moved(): lax.ppermute(value, axis, [(s, (s + steps) % count) for s in range(count)])  64 us
    dot_general x12, matrix products, product(): lax.dot_general(plain, weighted, (((1,), (1,)), ((), ())), preferred_elem...  31.1 us
    ppermute x8, starting transfers between devices, moved(): lax.ppermute(value, axis, [(s, (s + steps) % count) for s in range(count)])  30.5 us
    all_to_all x1, blocking collectives, per_device(): part = lax.all_to_all(part, 'y', 0, 0, tiled=False).sum(0)  27.2 us
    all_to_all x1, starting transfers between devices, per_device(): part = lax.all_to_all(part, ('zh', 'c'), 0, 0, tiled=False)  8.74 us
    all_to_all x1, waiting for transfers between devices, per_device(): part = lax.all_to_all(part, ('zh', 'c'), 0, 0, tiled=False)  8.37 us
    dot_general x1, matrix products, precondition(): jnp.einsum('bpi,iq->bpq', left, in_mat, precision=lax.Precision.HIGHEST)  5.78 us
    all_to_all x1, blocking collectives, per_device(): pair = lax.all_to_all(pair, 'c', 0, 0, tiled=False)  4.84 us
  transfers between devices with their start and end apart: 9, of which 6 were waited for; matrix products, arithmetic and copies ran while one was open for 14% of the time, Pallas kernels for 0%

profile of v1, /device:TPU:8, one launch (start us, length us, event | category | flops | bytes accessed | tf_op | source)
XLA Modules:
  0.0 194.1 jit_solution(5489101706310028127)
XLA Ops:
  0.0 8.0 %collective-permute-start = (bf16[192,4096]{1,0:T(8,128)(2,1)}, bf16[192,4096]{1,0:T(8,128)(2,1)}, u32[]{:S(2)}, u32[]{:S(2)}) collective-permute-start(bf16[192,4096]{1,0:T(8,128)(2,1)} %bitcast.92), channel_id=1, source_target_pairs={{0,384},{128,0},{256,128},{384,256},{1,385},{129,1},{257,129},{385... | collective-permute-start | bytes 4718600 | tf_op jit(solution)/shard_map/ppermute | solution.py:13
  8.0 3.2 %copy.8 = bf16[1,192,4096]{1,2,0:T(8,128)(2,1)S(1)} copy(bf16[1,192,4096]{2,1,0:T(8,128)(2,1)} %param.3) | data formatting | bytes 3145728 | tf_op args[0]
  11.2 2.7 %convolution_bitcast_fusion = f32[192,64,64]{0,1,2:T(8,128)S(1)} fusion(bf16[192,64,64]{0,2,1:T(8,128)(2,1)S(1)} %bitcast.94, f32[1,64,64]{2,1,0:T(8,128)S(1)} %copy-done), kind=kOutput, calls=%fused_computation.2 | convolution fusion | flops 603979776 | bytes 4734976 | tf_op jit(solution)/shard_map/po,boi->bpi/dot_general | solution.py:18
  13.9 5.8 %fusion.3 = bf16[192,64,64]{0,2,1:T(8,128)(2,1)S(1)} fusion(f32[192,64,64]{0,1,2:T(8,128)S(1)} %convolution_bitcast_fusion, f32[1,64,64]{2,1,0:T(8,128)S(1)} %copy-done.6), kind=kOutput, calls=%fused_computation.4 | convolution fusion | flops 604766208 | bytes 4734976 | tf_op jit(solution)/shard_map/bpi,iq->bpq/dot_general | solution.py:19
  19.7 2.8 %copy.12 = bf16[192,4096]{1,0:T(8,128)(2,1)} copy(bf16[192,4096]{0,1:T(8,128)(2,1)S(1)} %bitcast.88) | data formatting | bytes 3145728 | tf_op jit(solution)/shard_map/reshape | solution.py:20
  22.5 4.7 %collective-permute-start.3 = (bf16[192,4096]{1,0:T(8,128)(2,1)}, bf16[192,4096]{1,0:T(8,128)(2,1)}, u32[]{:S(2)}, u32[]{:S(2)}) collective-permute-start(bf16[192,4096]{1,0:T(8,128)(2,1)} %copy.12), channel_id=1, source_target_pairs={{0,96},{32,0},{64,32},{96,64},{1,97},{33,1},{65,33},{97,65},{2,98}... | collective-permute-start | bytes 4718600 | tf_op jit(solution)/shard_map/ppermute | solution.py:13
  27.2 2.7 %collective-permute-start.2 = (bf16[192,4096]{1,0:T(8,128)(2,1)}, bf16[192,4096]{1,0:T(8,128)(2,1)}, u32[]{:S(2)}, u32[]{:S(2)}) collective-permute-start(bf16[192,4096]{1,0:T(8,128)(2,1)} %copy.12), channel_id=1, source_target_pairs={{0,64},{32,96},{64,0},{96,32},{1,65},{33,97},{65,1},{97,33},{2,66}... | collective-permute-start | bytes 4718600 | tf_op jit(solution)/shard_map/ppermute | solution.py:13
  29.9 2.8 %collective-permute-start.1 = (bf16[192,4096]{1,0:T(8,128)(2,1)}, bf16[192,4096]{1,0:T(8,128)(2,1)}, u32[]{:S(2)}, u32[]{:S(2)}) collective-permute-start(bf16[192,4096]{1,0:T(8,128)(2,1)} %copy.12), channel_id=1, source_target_pairs={{0,32},{32,64},{64,96},{96,0},{1,33},{33,65},{65,97},{97,1},{2,34}... | collective-permute-start | bytes 4718600 | tf_op jit(solution)/shard_map/ppermute | solution.py:13
  34.8 2.7 %convolution_bitcast_fusion.5 = f32[192,192]{1,0:T(8,128)} fusion(bf16[192,4096]{0,1:T(8,128)(2,1)S(1)} %bitcast.89, bf16[1,192,4096]{2,1,0:T(8,128)(2,1)} %param.3), kind=kOutput, calls=%fused_computation.11 | convolution fusion | flops 301989888 | bytes 3293184 | tf_op jit(solution)/shard_map/dot_general | solution.py:24
  37.5 5.7 %collective-permute-done = bf16[192,4096]{1,0:T(8,128)(2,1)} collective-permute-done((bf16[192,4096]{1,0:T(8,128)(2,1)}, bf16[192,4096]{1,0:T(8,128)(2,1)}, u32[]{:S(2)}, u32[]{:S(2)}) %collective-permute-start) | collective-permute-done | bytes 1572896 | tf_op jit(solution)/shard_map/ppermute | solution.py:13
  43.2 51.4 %collective-permute-done.3 = bf16[192,4096]{1,0:T(8,128)(2,1)} collective-permute-done((bf16[192,4096]{1,0:T(8,128)(2,1)}, bf16[192,4096]{1,0:T(8,128)(2,1)}, u32[]{:S(2)}, u32[]{:S(2)}) %collective-permute-start.3) | collective-permute-done | bytes 1572896 | tf_op jit(solution)/shard_map/ppermute | solution.py:13
  97.1 3.2 %convolution_bitcast_fusion.2 = f32[192,192]{1,0:T(8,128)} fusion(bf16[192,4096]{1,0:T(8,128)(2,1)} %collective-permute-done.2, bf16[192,4096]{1,0:T(8,128)(2,1)} %collective-permute-done), kind=kOutput, calls=%fused_computation.8 | convolution fusion | flops 301989888 | bytes 3293184 | tf_op jit(solution)/shard_map/dot_general | solution.py:24
  100.2 3.2 %convolution_bitcast_fusion.3 = f32[192,192]{1,0:T(8,128)} fusion(bf16[192,4096]{1,0:T(8,128)(2,1)} %collective-permute-done.1, bf16[192,4096]{1,0:T(8,128)(2,1)} %collective-permute-done), kind=kOutput, calls=%fused_computation.9 | convolution fusion | flops 301989888 | bytes 3293184 | tf_op jit(solution)/shard_map/dot_general | solution.py:24
  105.4 2.9 %collective-permute-done.4 = bf16[192,4096]{1,0:T(8,128)(2,1)} collective-permute-done((bf16[192,4096]{1,0:T(8,128)(2,1)}, bf16[192,4096]{1,0:T(8,128)(2,1)}, u32[]{:S(2)}, u32[]{:S(2)}) %collective-permute-start.4) | collective-permute-done | bytes 1572896 | tf_op jit(solution)/shard_map/ppermute | solution.py:13
  114.1 2.7 %convolution_bitcast_fusion.4 = f32[192,192]{1,0:T(8,128)} fusion(bf16[192,4096]{1,0:T(8,128)(2,1)} %collective-permute-done.4, bf16[192,4096]{0,1:T(8,128)(2,1)S(1)} %bitcast.91), kind=kOutput, calls=%fused_computation.10 | convolution fusion | flops 301989888 | bytes 3293184 | tf_op jit(solution)/shard_map/dot_general | solution.py:24
  121.9 2.7 %fusion.6 = f32[192,192]{1,0:T(8,128)} fusion(f32[192,192]{0,1:T(8,128)S(1)} %fusion.18, bf16[192,4096]{1,0:T(8,128)(2,1)} %collective-permute-done.3, pred[]{:T(512)S(6)} %ge.11, bf16[1,192,4096]{2,1,0:T(8,128)(2,1)S(1)} %copy-done.2), kind=kOutput, calls=%fused_computation.14 | convolution fusion | flops 302026752 | bytes 3440641 | tf_op jit(solution)/shard_map/dot_general | solution.py:24
  124.6 2.8 %fusion.7 = f32[192,192]{1,0:T(8,128)} fusion(f32[192,192]{0,1:T(8,128)S(1)} %fusion.17, bf16[192,4096]{1,0:T(8,128)(2,1)} %collective-permute-done.2, pred[]{:T(512)S(6)} %ge.10, bf16[1,192,4096]{2,1,0:T(8,128)(2,1)S(1)} %copy-done.2), kind=kOutput, calls=%fused_computation.16 | convolution fusion | flops 302026752 | bytes 3440641 | tf_op jit(solution)/shard_map/dot_general | solution.py:24
  129.0 4.8 %all_to_all.15 = f32[2,192,896]{2,1,0:T(8,128)S(1)} all-to-all(f32[2,192,896]{2,1,0:T(8,128)S(1)} %pad_maximum_fusion), channel_id=1, replica_groups=mesh['zl'=4,'x'=4,'y'=8,'zh'=2,'c'=2] {'c'}, dimensions={0} | all-to-all | bytes 2752512 | tf_op jit(solution)/shard_map/all_to_all | solution.py:49
  133.9 27.2 %all_to_all.16 = f32[8,24,896]{2,1,0:T(8,128)S(1)} all-to-all(f32[8,24,896]{2,1,0:T(8,128)S(1)} %bitcast.95), channel_id=1, replica_groups=mesh['zl'=4,'x'=4,'y'=8,'zh'=2,'c'=2] {'y'}, dimensions={0} | all-to-all | bytes 1376256 | tf_op jit(solution)/shard_map/all_to_all | solution.py:51
  161.8 8.7 %all-to-all-start.2 = ((f32[4,6,896]{2,1,0:T(8,128)}), f32[4,6,896]{2,1,0:T(8,128)S(1)}, u32[]{:S(2)}, u32[]{:S(2)}) async-start(f32[4,6,896]{2,1,0:T(8,128)} %reshape.25), calls=%async_computation.2 | async-start | bytes 229376 | tf_op jit(solution)/shard_map/all_to_all | solution.py:53
  170.6 8.4 %all-to-all-done.2 = f32[4,6,896]{2,1,0:T(8,128)S(1)} async-done(((f32[4,6,896]{2,1,0:T(8,128)}), f32[4,6,896]{2,1,0:T(8,128)S(1)}, u32[]{:S(2)}, u32[]{:S(2)}) %all-to-all-start.2) | async-done | bytes 86048 | tf_op jit(solution)/shard_map/all_to_all | solution.py:53
  179.1 4.7 %collective-permute-start.5 = (f32[2,6,192]{2,0,1:T(2,128)S(1)}, f32[2,6,192]{2,0,1:T(2,128)S(1)}, u32[]{:S(2)}, u32[]{:S(2)}) collective-permute-start(f32[2,6,192]{2,0,1:T(2,128)S(1)} %pad_maximum_fusion.1), channel_id=1, source_target_pairs={{0,96},{32,0},{64,32},{96,64},{1,97},{33,1},{65,33},{97,65},{2,98}... | collective-permute-start | bytes 27656 | tf_op jit(solution)/shard_map/ppermute | solution.py:13
  183.8 2.7 %collective-permute-start.6 = (f32[2,6,192]{2,0,1:T(2,128)S(1)}, f32[2,6,192]{2,0,1:T(2,128)S(1)}, u32[]{:S(2)}, u32[]{:S(2)}) collective-permute-start(f32[2,6,192]{2,0,1:T(2,128)S(1)} %pad_maximum_fusion.2), channel_id=1, source_target_pairs={{0,64},{32,96},{64,0},{96,32},{1,65},{33,97},{65,1},{97,33},{2,66}... | collective-permute-start | bytes 27656 | tf_op jit(solution)/shard_map/ppermute | solution.py:13
  186.6 2.8 %collective-permute-start.7 = (f32[2,6,192]{2,0,1:T(2,128)S(1)}, f32[2,6,192]{2,0,1:T(2,128)S(1)}, u32[]{:S(2)}, u32[]{:S(2)}) collective-permute-start(f32[2,6,192]{2,0,1:T(2,128)S(1)} %pad_maximum_fusion.3), channel_id=1, source_target_pairs={{0,32},{32,64},{64,96},{96,0},{1,33},{33,65},{65,97},{97,1},{2,34}... | collective-permute-start | bytes 27656 | tf_op jit(solution)/shard_map/ppermute | solution.py:13
  (45 shorter events, 24.8 us)
Async XLA Ops:
  0.0 11.2 %copy-start = (f32[1,64,64]{2,1,0:T(8,128)S(1)}, f32[1,64,64]{2,1,0:T(8,128)}, u32[]{:S(2)}) copy-start(f32[1,64,64]{2,1,0:T(8,128)} %param.5) | copy-start | bytes 49156
  0.0 43.2 %collective-permute-start = (bf16[192,4096]{1,0:T(8,128)(2,1)}, bf16[192,4096]{1,0:T(8,128)(2,1)}, u32[]{:S(2)}, u32[]{:S(2)}) collective-permute-start(bf16[192,4096]{1,0:T(8,128)(2,1)} %bitcast.92), channel_id=1, source_target_pairs={{0,384},{128,0},{256,128},{384,256},{1,385},{129,1},{257,129},{385... | collective-permute-start | bytes 4718600 | tf_op jit(solution)/shard_map/ppermute | solution.py:13
  11.2 2.7 %copy-start.6 = (f32[1,64,64]{2,1,0:T(8,128)S(1)}, f32[1,64,64]{2,1,0:T(8,128)}, u32[]{:S(2)}) copy-start(f32[1,64,64]{2,1,0:T(8,128)} %param.4) | copy-start | bytes 49156
  22.5 72.1 %collective-permute-start.3 = (bf16[192,4096]{1,0:T(8,128)(2,1)}, bf16[192,4096]{1,0:T(8,128)(2,1)}, u32[]{:S(2)}, u32[]{:S(2)}) collective-permute-start(bf16[192,4096]{1,0:T(8,128)(2,1)} %copy.12), channel_id=1, source_target_pairs={{0,96},{32,0},{64,32},{96,64},{1,97},{33,1},{65,33},{97,65},{2,98}... | collective-permute-start | bytes 4718600 | tf_op jit(solution)/shard_map/ppermute | solution.py:13
  27.2 69.9 %collective-permute-start.2 = (bf16[192,4096]{1,0:T(8,128)(2,1)}, bf16[192,4096]{1,0:T(8,128)(2,1)}, u32[]{:S(2)}, u32[]{:S(2)}) collective-permute-start(bf16[192,4096]{1,0:T(8,128)(2,1)} %copy.12), channel_id=1, source_target_pairs={{0,64},{32,96},{64,0},{96,32},{1,65},{33,97},{65,1},{97,33},{2,66}... | collective-permute-start | bytes 4718600 | tf_op jit(solution)/shard_map/ppermute | solution.py:13
  29.9 70.3 %collective-permute-start.1 = (bf16[192,4096]{1,0:T(8,128)(2,1)}, bf16[192,4096]{1,0:T(8,128)(2,1)}, u32[]{:S(2)}, u32[]{:S(2)}) collective-permute-start(bf16[192,4096]{1,0:T(8,128)(2,1)} %copy.12), channel_id=1, source_target_pairs={{0,32},{32,64},{64,96},{96,0},{1,33},{33,65},{65,97},{97,1},{2,34}... | collective-permute-start | bytes 4718600 | tf_op jit(solution)/shard_map/ppermute | solution.py:13
  32.7 75.6 %collective-permute-start.4 = (bf16[192,4096]{1,0:T(8,128)(2,1)}, bf16[192,4096]{1,0:T(8,128)(2,1)}, u32[]{:S(2)}, u32[]{:S(2)}) collective-permute-start(bf16[192,4096]{1,0:T(8,128)(2,1)} %bitcast.93), channel_id=1, source_target_pairs={{0,256},{128,384},{256,0},{384,128},{1,257},{129,385},{257,1},{385... | collective-permute-start | bytes 4718600 | tf_op jit(solution)/shard_map/ppermute | solution.py:13
  105.4 5.4 %copy-start.1 = (bf16[1,192,4096]{2,1,0:T(8,128)(2,1)S(1)}, bf16[1,192,4096]{2,1,0:T(8,128)(2,1)}, u32[]{:S(2)}) copy-start(bf16[1,192,4096]{2,1,0:T(8,128)(2,1)} %param.3) | copy-start | bytes 4718596
  119.3 2.6 %copy-start.2 = (bf16[1,192,4096]{2,1,0:T(8,128)(2,1)S(1)}, bf16[1,192,4096]{2,1,0:T(8,128)(2,1)}, u32[]{:S(2)}) copy-start(bf16[1,192,4096]{2,1,0:T(8,128)(2,1)} %param.3) | copy-start | bytes 4718596
  124.6 2.8 %copy-start.3 = (f32[192,192]{1,0:T(8,128)S(1)}, f32[192,192]{1,0:T(8,128)}, u32[]{:S(2)}) copy-start(f32[192,192]{1,0:T(8,128)} %convolution_bitcast_fusion.2) | copy-start | bytes 442372
  124.6 2.8 %copy-start.4 = (f32[192,192]{1,0:T(8,128)S(1)}, f32[192,192]{1,0:T(8,128)}, u32[]{:S(2)}) copy-start(f32[192,192]{1,0:T(8,128)} %convolution_bitcast_fusion.3) | copy-start | bytes 442372
  124.6 2.8 %copy-start.5 = (f32[192,192]{1,0:T(8,128)S(1)}, f32[192,192]{1,0:T(8,128)}, u32[]{:S(2)}) copy-start(f32[192,192]{1,0:T(8,128)} %convolution_bitcast_fusion.5) | copy-start | bytes 442372
  161.8 17.1 %all-to-all-start.2 = ((f32[4,6,896]{2,1,0:T(8,128)}), f32[4,6,896]{2,1,0:T(8,128)S(1)}, u32[]{:S(2)}, u32[]{:S(2)}) async-start(f32[4,6,896]{2,1,0:T(8,128)} %reshape.25), calls=%async_computation.2 | async-start | bytes 229376 | tf_op jit(solution)/shard_map/all_to_all | solution.py:53
  179.1 10.2 %collective-permute-start.5 = (f32[2,6,192]{2,0,1:T(2,128)S(1)}, f32[2,6,192]{2,0,1:T(2,128)S(1)}, u32[]{:S(2)}, u32[]{:S(2)}) collective-permute-start(f32[2,6,192]{2,0,1:T(2,128)S(1)} %pad_maximum_fusion.1), channel_id=1, source_target_pairs={{0,96},{32,0},{64,32},{96,64},{1,97},{33,1},{65,33},{97,65},{2,98}... | collective-permute-start | bytes 27656 | tf_op jit(solution)/shard_map/ppermute | solution.py:13
  183.8 7.1 %collective-permute-start.6 = (f32[2,6,192]{2,0,1:T(2,128)S(1)}, f32[2,6,192]{2,0,1:T(2,128)S(1)}, u32[]{:S(2)}, u32[]{:S(2)}) collective-permute-start(f32[2,6,192]{2,0,1:T(2,128)S(1)} %pad_maximum_fusion.2), channel_id=1, source_target_pairs={{0,64},{32,96},{64,0},{96,32},{1,65},{33,97},{65,1},{97,33},{2,66}... | collective-permute-start | bytes 27656 | tf_op jit(solution)/shard_map/ppermute | solution.py:13
  186.6 6.8 %collective-permute-start.7 = (f32[2,6,192]{2,0,1:T(2,128)S(1)}, f32[2,6,192]{2,0,1:T(2,128)S(1)}, u32[]{:S(2)}, u32[]{:S(2)}) collective-permute-start(f32[2,6,192]{2,0,1:T(2,128)S(1)} %pad_maximum_fusion.3), channel_id=1, source_target_pairs={{0,32},{32,64},{64,96},{96,0},{1,33},{33,65},{65,97},{97,1},{2,34}... | collective-permute-start | bytes 27656 | tf_op jit(solution)/shard_map/ppermute | solution.py:13

commit v2 on v1

v2 whole, which is shorter than its diff:
```python
import functools
import math

import jax
import jax.numpy as jnp
import numpy as np
from jax import lax
from jax.experimental import pallas as pl
from jax.experimental.pallas import tpu as pltpu
from jax.sharding import Mesh, PartitionSpec as P

NZ, NX, NY, NH, NC = 4, 4, 8, 2, 2
NL = NY * NH
ROWS = 192
OWN = ROWS // (NL * NC)
LANES = 128
PIECE = OWN * ROWS // LANES
TILE = 256
NN, NT = ((1,), (0,)), ((1,), (1,))
COST = pl.CostEstimate(flops=10**10, bytes_accessed=10**6, transcendentals=0)


def moved(value, axis, steps):
    count = lax.axis_size(axis)
    return lax.ppermute(value, axis, [(s, (s + steps) % count) for s in range(count)])


def held_kernel(value_ref, *refs):
    pass


def held(value, *others):
    anywhere = pl.BlockSpec(memory_space=pl.ANY)
    return pl.pallas_call(
        held_kernel,
        out_shape=jax.ShapeDtypeStruct(value.shape, value.dtype),
        in_specs=[anywhere] * (1 + len(others)),
        out_specs=anywhere,
        input_output_aliases={0: 0},
        cost_estimate=COST,
    )(value, *others)


def spread():
    at = np.arange(TILE)
    six = np.arange(64)
    by_four = (at[:, None] // 4 == six).astype(np.float32)
    by_last = (at[:, None] % 64 == six).astype(np.float32)
    mixed = (at[:, None] // 16 * 4 + at[:, None] % 4 == six).astype(np.float32)
    inner = (at[:, None] % 4 == at // 64).astype(np.float32)
    outer = (at[:, None] // 4 % 4 == at // 4 % 4).astype(np.float32)
    order = np.zeros((TILE, TILE), np.float32)
    order[at, at % 64 * 4 + at // 64] = 1
    return [jnp.asarray(m) for m in (by_four, by_last, mixed, inner, outer)], jnp.asarray(
        order, jnp.bfloat16
    )


def tiles_kernel(in_ref, out_ref, four_ref, last_ref, mixed_ref, im_ref, om_ref, a_ref, b_ref):
    def exact(a, b, dims):
        return lax.dot_general(
            a,
            b,
            (dims, ((), ())),
            precision=lax.Precision.HIGHEST,
            preferred_element_type=jnp.float32,
        )

    def parts(ref, matrix):
        for part in range(3):
            rounded = matrix.astype(jnp.bfloat16)
            ref[:, part * TILE : (part + 1) * TILE] = rounded
            matrix = matrix - rounded.astype(jnp.float32)

    inner = exact(exact(four_ref[...], in_ref[...], NT), last_ref[...], NT)
    parts(a_ref, inner * im_ref[...])
    outer = exact(exact(mixed_ref[...], out_ref[...], NN), mixed_ref[...], NT)
    parts(b_ref, outer * om_ref[...])


def factor_tiles(in_mat, out_mat):
    matrices, order = spread()
    shape = jax.ShapeDtypeStruct((TILE, 3 * TILE), jnp.bfloat16)
    inner, outer = pl.pallas_call(
        tiles_kernel, out_shape=(shape, shape), cost_estimate=COST
    )(in_mat, out_mat, *matrices)
    return inner, outer, order


def dot(a, b, dims):
    return lax.dot_general(a, b, (dims, ((), ())), preferred_element_type=jnp.float32)


def weigh_kernel(p_ref, inner_ref, outer_ref, order_ref, w_ref, t_ref):
    tiles = p_ref.shape[1] // TILE

    @pl.loop(0, tiles, unroll=tiles)
    def _(b):
        x = p_ref[:, pl.ds(pl.multiple_of(b * TILE, TILE), TILE)]
        t_ref[b] = dot(inner_ref[...], jnp.concatenate([x] * 3, axis=1), NT)

    @pl.loop(0, tiles, unroll=tiles)
    def _(g):
        at = pl.ds(pl.multiple_of(g * 16, 16), 16)
        x = t_ref[:, at, :].reshape(TILE, ROWS)
        high = x.astype(jnp.bfloat16)
        low = (x - high.astype(jnp.float32)).astype(jnp.bfloat16)
        left = jnp.concatenate([outer_ref[:, : 2 * TILE], outer_ref[:, :TILE]], axis=1)
        y = dot(left, jnp.concatenate([high, high, low], axis=0), NN)
        t_ref[:, at, :] = y.reshape(16, 16, ROWS)

    @pl.loop(0, tiles, unroll=tiles)
    def _(b):
        y = dot(order_ref[...], t_ref[b].astype(jnp.bfloat16), NN)
        w_ref[pl.ds(pl.multiple_of(b * TILE, TILE), TILE), :] = y.astype(jnp.bfloat16)


def weigh(rows, tiles):
    width = rows.shape[1]
    return pl.pallas_call(
        weigh_kernel,
        out_shape=jax.ShapeDtypeStruct((width, ROWS), jnp.bfloat16),
        scratch_shapes=[pltpu.VMEM((width // TILE, TILE, ROWS), jnp.float32)],
        compiler_params=pltpu.CompilerParams(vmem_limit_bytes=24 * 2**20),
        cost_estimate=COST,
    )(rows, *tiles)


def products_kernel(picks, n_p, n_w, first, place_ref, *refs):
    p_refs, w_refs = refs[:n_p], refs[n_p : n_p + n_w]
    given, (out_ref, total) = refs[n_p + n_w : -2], refs[-2:]

    def score(slot, p, w):
        total[slot] = dot(p_refs[p][...], w_refs[w][...], NN)

    for slot, (axis, least, below, reached) in enumerate(picks):
        if axis is None:
            score(slot, *reached)
        else:
            here = place_ref[axis]
            pl.when(here < least)(functools.partial(score, slot, *below))
            pl.when(here >= least)(functools.partial(score, slot, *reached))
    if given:
        out_ref[:, :, : first * PIECE] = given[0][:, :, : first * PIECE]
    for pair in range(len(picks) // 2):
        a, b = total[2 * pair], total[2 * pair + 1]
        rest = jnp.concatenate([a[:, LANES:], b[:, LANES:]], axis=1)
        for n, piece in enumerate((a[:, :LANES], b[:, :LANES], rest)):
            to = first * PIECE + (3 * pair + n) * OWN
            for chip in range(NL):
                for core in range(NC):
                    at = (chip * NC + core) * OWN
                    out_ref[core, chip, to : to + OWN] = piece[at : at + OWN]


def products(plains, weights, picks, slots, first=0, sums=None):
    place = jnp.stack([lax.axis_index("zl"), lax.axis_index("x")]).astype(jnp.int32)
    given = () if sums is None else (sums,)
    vmem = pl.BlockSpec(memory_space=pltpu.VMEM)
    height = -(-slots * PIECE // 8) * 8
    return pl.pallas_call(
        functools.partial(products_kernel, picks, len(plains), len(weights), first),
        out_shape=jax.ShapeDtypeStruct((NC, NL, height, LANES), jnp.float32),
        in_specs=[pl.BlockSpec(memory_space=pltpu.SMEM)]
        + [vmem] * (len(plains) + len(weights) + len(given)),
        out_specs=vmem,
        scratch_shapes=[pltpu.VMEM((len(picks), ROWS, ROWS), jnp.float32)],
        compiler_params=pltpu.CompilerParams(vmem_limit_bytes=24 * 2**20),
        cost_estimate=COST,
    )(place, *plains, *weights, *given)


def unpacked(part, slots):
    part = part[: slots * PIECE].reshape(slots // 2, 3, OWN, LANES)
    rest = part[:, 2].reshape(slots // 2, OWN, 2, ROWS - LANES).transpose(0, 2, 1, 3)
    return jnp.concatenate([part[:, :2], rest], axis=-1).reshape(slots, OWN, ROWS)


def per_device(grads, in_factor, out_factor):
    factor = 1.0 / math.sqrt(NL * NC * grads.shape[-1])
    z, x = lax.axis_index("zl"), lax.axis_index("x")
    tiles = factor_tiles(in_factor[0], out_factor[0])
    half = ROWS // 2
    p0 = grads[0]
    p1, p3 = moved(p0, "x", 1), moved(p0, "x", -1)
    p4 = lax.ppermute(p0, "zl", [(0, 2), (3, 1), (1, 0)])
    own = held(p0, p4)
    p5 = lax.ppermute(own, "zl", [(0, 3), (2, 1), (3, 2)])
    p2 = jnp.concatenate([moved(p1[:half], "x", 1), moved(p3[half:], "x", -1)])
    w0, w1, w2, w3, w4 = (weigh(p, tiles) for p in (p0, p1, p2, p3, p4))
    early = products(
        [own, p1, p2, p3, p4],
        [w0, w1, w2, w3, w4],
        [
            (None, 0, None, (0, 0)),
            (1, 1, (1, 0), (0, 1)),
            (None, 0, None, (0, 2)),
            (None, 0, None, (4, 0)),
            (1, 1, (4, 1), (1, 4)),
            (1, 2, (4, 2), (2, 4)),
            (1, 3, (4, 3), (3, 4)),
            (None, 0, None, (0, 4)),
        ],
        12,
    )
    sums = products(
        [p4, p5], [w0, w1, w2, w3], [(0, 1, (0, r), (1, r)) for r in range(NX)], 12, 8, early
    )
    pair = lax.all_to_all(sums, "c", 0, 0, tiled=False)
    part = pair[0] + pair[1]
    part = lax.all_to_all(part, ("y", "zh"), 0, 0, tiled=False).sum(0)
    slots = unpacked(part, 12)
    row, two, again, following = slots[:3], slots[3:7], slots[7], slots[8:]
    out = [None] * 9
    out[0], out[4] = row[0], following[0]
    across = lax.ppermute(
        jnp.concatenate([again[None], two[1:]]), "zl", [(1, 3), (2, 0)]
    )
    middle = (z == 1) | (z == 2)
    out[8] = jnp.where(middle, two[0], across[0])
    for r in range(1, NX):
        same = row[r] if r < 3 else row[1]
        back = moved(jnp.stack([following[r], jnp.where(x >= r, same, two[r])]), "x", -r)
        inside = x + r < NX
        near = row[1] if r == 3 else back[1]
        far = jnp.where(middle, back[1], across[NX - r])
        out[r] = jnp.where(inside, near, back[0])
        out[r + 4] = jnp.where(inside, back[0], far)
    return (jnp.stack(out) * factor).transpose(2, 0, 1)


def solution(mesh):
    fine = Mesh(mesh.devices.reshape(NZ, NX, NY, NH, NC), ("zl", "x", "y", "zh", "c"))
    layer, group = ("y", "zh", "c"), ("zl", "x")
    in_specs = (P(layer, group, None), P(layer, None, None), P(layer, None, None))
    return jax.shard_map(
        per_device, mesh=fine, in_specs=in_specs, out_specs=P(group, None, layer), check_vma=False
    )
```

time: 195 us -> 167 us (0.86)
  the two profiles are of different devices: /device:TPU:8 before, /device:TPU:32 now
where the time goes in v2:
time: 167 us; the launch traced here: 166 us
  waiting for transfers between devices  58.9 us (35%)
  starting transfers between devices  51.6 us (31%)
  Pallas kernels  37.3 us (22%)
  local copies, waits for them, and re-layouts  11 us (7%)
  blocking collectives  5.21 us (3%)
  other arithmetic  1.89 us (1%)
    all_to_all x1, waiting for transfers between devices, per_device(): part = lax.all_to_all(part, ('y', 'zh'), 0, 0, tiled=False).sum(0)  35.3 us
    pallas_call x5, Pallas kernels, weigh(): pl.pallas_call(weigh_kernel, out_shape=jax.ShapeDtypeStruct((width, ROWS)...  23.9 us
    ppermute x7, starting transfers between devices, moved(): lax.ppermute(value, axis, [(s, (s + steps) % count) for s in range(count)])  23 us
    ppermute x7, waiting for transfers between devices, moved(): lax.ppermute(value, axis, [(s, (s + steps) % count) for s in range(count)])  21.9 us
    all_to_all x1, starting transfers between devices, per_device(): part = lax.all_to_all(part, ('y', 'zh'), 0, 0, tiled=False).sum(0)  13 us
    pallas_call x2, Pallas kernels, products(): pl.pallas_call(functools.partial(products_kernel, picks, len(plains), len...  10.3 us
    ppermute x1, starting transfers between devices, per_device(): p5 = lax.ppermute(own, 'zl', [(0, 3), (2, 1), (3, 2)])  8.17 us
    unnamed x21, local copies, waits for them, and re-layouts  6.59 us
  transfers between devices with their start and end apart: 11, of which 4 were waited for; matrix products, arithmetic and copies ran while one was open for 3% of the time, Pallas kernels for 20%

profile of v2, /device:TPU:32, one launch (start us, length us, event | category | flops | bytes accessed | tf_op | source)
XLA Modules:
  0.0 166.3 jit_solution(10626435843060502729)
XLA Ops:
  1.4 3.4 %collective-permute-start.2 = (bf16[192,4096]{1,0:T(8,128)(2,1)S(1)}, bf16[192,4096]{1,0:T(8,128)(2,1)S(1)}, u32[]{:S(2)}, u32[]{:S(2)}) collective-permute-start(bf16[192,4096]{1,0:T(8,128)(2,1)S(1)} %bitcast.15), channel_id=1, source_target_pairs={{0,32},{32,64},{64,96},{96,0},{1,33},{33,65},{65,97},{97,1},{2,34}... | collective-permute-start | bytes 4718600 | tf_op jit(solution)/shard_map/ppermute | solution.py:25
  4.8 3.7 %collective-permute-start.4 = (bf16[192,4096]{1,0:T(8,128)(2,1)S(1)}, bf16[192,4096]{1,0:T(8,128)(2,1)}, u32[]{:S(2)}, u32[]{:S(2)}) collective-permute-start(bf16[192,4096]{1,0:T(8,128)(2,1)S(1)} %bitcast.16), channel_id=1, source_target_pairs={{0,96},{32,0},{64,32},{96,64},{1,97},{33,1},{65,33},{97,65},{2,98}... | collective-permute-start | bytes 4718600 | tf_op jit(solution)/shard_map/ppermute | solution.py:25
  8.5 6.1 %collective-permute-start = (bf16[192,4096]{1,0:T(8,128)(2,1)S(1)}, bf16[192,4096]{1,0:T(8,128)(2,1)}, u32[]{:S(2)}, u32[]{:S(2)}) collective-permute-start(bf16[192,4096]{1,0:T(8,128)(2,1)S(1)} %bitcast.17), channel_id=1, source_target_pairs={{0,256},{384,128},{128,0},{1,257},{385,129},{129,1},{2,258},{386,1... | collective-permute-start | bytes 4718600 | tf_op jit(solution)/shard_map/ppermute | solution.py:186
  14.7 3.1 %shard_map.92 = (bf16[256,768]{1,0:T(8,128)(2,1)}, bf16[256,768]{1,0:T(8,128)(2,1)}) custom-call(f32[64,64]{1,0:T(8,128)} %bitcast.29, f32[64,64]{1,0:T(8,128)} %bitcast.30, f32[256,64]{1,0:T(8,128)} %constant.34.clone.four_ref, f32[256,64]{1,0:T(8,128)} %constant.35.clone.last_ref, f32[256,64]{1,0:T(8,128)} %constant.36.clone.mixed_ref, ...), custom_call_target="tpu_custom_call" | custom-call | flops 10000000000 | bytes 1000000 | tf_op jit(solution)/shard_map/pallas_call | solution.py:84
  19.7 4.2 %shard_map.93.refs_5_.refs_2_ = bf16[4096,192]{1,0:T(8,128)(2,1)S(1)} custom-call(bf16[192,4096]{1,0:T(8,128)(2,1)S(1)} %bitcast.18, bf16[256,768]{1,0:T(8,128)(2,1)S(1)} %copy-done.5, bf16[256,768]{1,0:T(8,128)(2,1)S(1)} %copy-done.7, bf16[256,256]{1,0:T(8,128)(2,1)S(1)} %copy-done.2), custom_call_target="tpu_custom_call" | custom-call | flops 10000000000 | bytes 1000000 | tf_op jit(solution)/shard_map/pallas_call | solution.py:120
  23.9 16.7 %collective-permute-done.2.p_ref.refs_1_ = bf16[192,4096]{1,0:T(8,128)(2,1)S(1)} collective-permute-done((bf16[192,4096]{1,0:T(8,128)(2,1)S(1)}, bf16[192,4096]{1,0:T(8,128)(2,1)S(1)}, u32[]{:S(2)}, u32[]{:S(2)}) %collective-permute-start.2) | collective-permute-done | bytes 1572896 | tf_op jit(solution)/shard_map/ppermute | solution.py:25
  41.6 2.2 %collective-permute-start.3 = (bf16[96,4096]{1,0:T(8,128)(2,1)}, bf16[96,4096]{1,0:T(8,128)(2,1)}, u32[]{:S(2)}, u32[]{:S(2)}) collective-permute-start(bf16[96,4096]{1,0:T(8,128)(2,1)} %slice.145), channel_id=1, source_target_pairs={{0,32},{32,64},{64,96},{96,0},{1,33},{33,65},{65,97},{97,1},{2,34}... | collective-permute-start | bytes 2359304 | tf_op jit(solution)/shard_map/ppermute | solution.py:25
  43.8 2.2 %slice.146 = bf16[96,4096]{1,0:T(8,128)(2,1)} slice(bf16[192,4096]{1,0:T(8,128)(2,1)} %collective-permute-done.4.p_ref.refs_3_), slice={[96:192], [0:4096]} | slice | bytes 1572864 | tf_op jit(solution)/shard_map/slice | solution.py:189
  45.9 4.9 %collective-permute-start.5 = (bf16[96,4096]{1,0:T(8,128)(2,1)}, bf16[96,4096]{1,0:T(8,128)(2,1)}, u32[]{:S(2)}, u32[]{:S(2)}) collective-permute-start(bf16[96,4096]{1,0:T(8,128)(2,1)} %slice.146), channel_id=1, source_target_pairs={{0,96},{32,0},{64,32},{96,64},{1,97},{33,1},{65,33},{97,65},{2,98}... | collective-permute-start | bytes 2359304 | tf_op jit(solution)/shard_map/ppermute | solution.py:25
  50.8 8.2 %collective-permute-start.1 = (bf16[192,4096]{1,0:T(8,128)(2,1)}, bf16[192,4096]{1,0:T(8,128)(2,1)S(1)}, u32[]{:S(2)}, u32[]{:S(2)}) collective-permute-start(bf16[192,4096]{1,0:T(8,128)(2,1)} %shard_map.91.refs_0_), channel_id=1, source_target_pairs={{0,384},{256,128},{384,256},{1,385},{257,129},{385,257},{2,386},{2... | collective-permute-start | bytes 4718600 | tf_op jit(solution)/shard_map/ppermute | solution.py:188
  61.0 4.2 %shard_map.94.refs_6_.refs_3_ = bf16[4096,192]{1,0:T(8,128)(2,1)S(1)} custom-call(bf16[192,4096]{1,0:T(8,128)(2,1)S(1)} %collective-permute-done.2.p_ref.refs_1_, bf16[256,768]{1,0:T(8,128)(2,1)S(1)} %copy-done.6, bf16[256,768]{1,0:T(8,128)(2,1)S(1)} %copy-done.8, bf16[256,256]{1,0:T(8,128)(2,1)S(1)} %copy-done.2), custom_call_target="tpu_custom_call" | custom-call | flops 10000000000 | bytes 1000000 | tf_op jit(solution)/shard_map/pallas_call | solution.py:120
  65.1 5.6 %shard_map.96.refs_8_.refs_5_ = bf16[4096,192]{1,0:T(8,128)(2,1)S(1)} custom-call(bf16[192,4096]{1,0:T(8,128)(2,1)} %collective-permute-done.4.p_ref.refs_3_, bf16[256,768]{1,0:T(8,128)(2,1)S(1)} %copy-done.6, bf16[256,768]{1,0:T(8,128)(2,1)S(1)} %copy-done.8, bf16[256,256]{1,0:T(8,128)(2,1)S(1)} %copy-done.2), custom_call_target="tpu_custom_call" | custom-call | flops 10000000000 | bytes 1000000 | tf_op jit(solution)/shard_map/pallas_call | solution.py:120
  70.7 5.6 %shard_map.97.refs_9_ = bf16[4096,192]{1,0:T(8,128)(2,1)S(1)} custom-call(bf16[192,4096]{1,0:T(8,128)(2,1)} %collective-permute-done.refs_0_.p_ref.refs_4_, bf16[256,768]{1,0:T(8,128)(2,1)S(1)} %copy-done.6, bf16[256,768]{1,0:T(8,128)(2,1)S(1)} %copy-done.8, bf16[256,256]{1,0:T(8,128)(2,1)S(1)} %copy-done.2), custom_call_target="tpu_custom_call" | custom-call | flops 10000000000 | bytes 1000000 | tf_op jit(solution)/shard_map/pallas_call | solution.py:120
  78.7 4.4 %shard_map.95.refs_7_.refs_4_ = bf16[4096,192]{1,0:T(8,128)(2,1)S(1)} custom-call(bf16[192,4096]{1,0:T(8,128)(2,1)S(1)} %constant_dynamic-update-slice_fusion.p_ref.refs_2_, bf16[256,768]{1,0:T(8,128)(2,1)S(1)} %copy-done.6, bf16[256,768]{1,0:T(8,128)(2,1)S(1)} %copy-done.8, bf16[256,256]{1,0:T(8,128)(2,1)S(1)} %copy-done.2), custom_call_target="tpu_custom_call" | custom-call | flops 10000000000 | bytes 1000000 | tf_op jit(solution)/shard_map/pallas_call | solution.py:120
  83.2 6.4 %shard_map.98.refs_6_ = f32[2,16,112,128]{3,2,1,0:T(8,128)S(1)} custom-call(s32[2]{0:T(128)S(1)} %pad_add_fusion.place_ref, bf16[192,4096]{1,0:T(8,128)(2,1)S(1)} %copy-done.1, bf16[192,4096]{1,0:T(8,128)(2,1)S(1)} %collective-permute-done.2.p_ref.refs_1_, bf16[192,4096]{1,0:T(8,128)(2,1)S(1)} %constant_dynamic-update-slice_fusion.p_ref.refs_2_, ...), custom_call_target="tpu_custom_call" | custom-call | flops 10000000000 | bytes 1000000 | tf_op jit(solution)/shard_map/pallas_call | solution.py:161
  89.6 1.6 collective-permute-done.1.refs_1_
  91.2 3.9 %shard_map.99 = f32[2,16,112,128]{3,2,1,0:T(8,128)S(1)} custom-call(s32[2]{0:T(128)S(1)} %pad_add_fusion.place_ref, bf16[192,4096]{1,0:T(8,128)(2,1)} %collective-permute-done.refs_0_.p_ref.refs_4_, bf16[192,4096]{1,0:T(8,128)(2,1)S(1)} %collective-permute-done.1.refs_1_, bf16[4096,192]{1,0:T(8,128)(2,1)S(1)} %copy-done.4, ...), custom_call_target="tpu_custom_call" | custom-call | flops 10000000000 | bytes 1000000 | tf_op jit(solution)/shard_map/pallas_call | solution.py:161
  95.1 5.2 %all_to_all.10 = f32[2,16,112,128]{3,2,1,0:T(8,128)S(1)} all-to-all(f32[2,16,112,128]{3,2,1,0:T(8,128)S(1)} %shard_map.99), channel_id=1, replica_groups=mesh['zl'=4,'x'=4,'y'=8,'zh'=2,'c'=2] {'c'}, dimensions={0} | all-to-all | bytes 3670016 | tf_op jit(solution)/shard_map/all_to_all | solution.py:209
  101.4 13.0 %all-to-all-start.1 = ((f32[16,112,128]{2,1,0:T(8,128)}), f32[16,112,128]{2,1,0:T(8,128)S(1)}, u32[]{:S(2)}, u32[]{:S(2)}) async-start(f32[16,112,128]{2,1,0:T(8,128)} %fusion), calls=%async_computation.1 | async-start | bytes 1835008 | tf_op jit(solution)/shard_map/all_to_all | solution.py:211
  114.4 35.3 %all-to-all-done.1 = f32[16,112,128]{2,1,0:T(8,128)S(1)} async-done(((f32[16,112,128]{2,1,0:T(8,128)}), f32[16,112,128]{2,1,0:T(8,128)S(1)}, u32[]{:S(2)}, u32[]{:S(2)}) %all-to-all-start.1) | async-done | bytes 917536 | tf_op jit(solution)/shard_map/all_to_all | solution.py:211
  151.3 1.9 %collective-permute-start.8 = (f32[2,6,192]{2,1,0:T(8,128)S(1)}, f32[2,6,192]{2,1,0:T(8,128)S(1)}, u32[]{:S(2)}, u32[]{:S(2)}) collective-permute-start(f32[2,6,192]{2,1,0:T(8,128)S(1)} %pad_maximum_fusion.4), channel_id=1, source_target_pairs={{0,32},{32,64},{64,96},{96,0},{1,33},{33,65},{65,97},{97,1},{2,34}... | collective-permute-start | bytes 27656 | tf_op jit(solution)/shard_map/ppermute | solution.py:25
  153.2 5.1 %collective-permute-start.6 = (f32[2,6,192]{2,1,0:T(8,128)S(1)}, f32[2,6,192]{2,1,0:T(8,128)S(1)}, u32[]{:S(2)}, u32[]{:S(2)}) collective-permute-start(f32[2,6,192]{2,1,0:T(8,128)S(1)} %pad_maximum_fusion.2), channel_id=1, source_target_pairs={{0,96},{32,0},{64,32},{96,64},{1,97},{33,1},{65,33},{97,65},{2,98}... | collective-permute-start | bytes 27656 | tf_op jit(solution)/shard_map/ppermute | solution.py:25
  158.4 1.9 %collective-permute-start.7 = (f32[2,6,192]{2,1,0:T(8,128)S(1)}, f32[2,6,192]{2,1,0:T(8,128)S(1)}, u32[]{:S(2)}, u32[]{:S(2)}) collective-permute-start(f32[2,6,192]{2,1,0:T(8,128)S(1)} %pad_maximum_fusion.3), channel_id=1, source_target_pairs={{0,64},{32,96},{64,0},{96,32},{1,65},{33,97},{65,1},{97,33},{2,66}... | collective-permute-start | bytes 27656 | tf_op jit(solution)/shard_map/ppermute | solution.py:25
  160.3 5.2 %collective-permute-done.7 = f32[2,6,192]{2,1,0:T(8,128)S(1)} collective-permute-done((f32[2,6,192]{2,1,0:T(8,128)S(1)}, f32[2,6,192]{2,1,0:T(8,128)S(1)}, u32[]{:S(2)}, u32[]{:S(2)}) %collective-permute-start.7) | collective-permute-done | bytes 9248 | tf_op jit(solution)/shard_map/ppermute | solution.py:25
  (56 shorter events, 12.0 us)
Async XLA Ops:
  1.4 16.3 %copy-start = (bf16[1,192,4096]{2,1,0:T(8,128)(2,1)}, bf16[1,192,4096]{2,1,0:T(8,128)(2,1)S(1)}, u32[]{:S(2)}) copy-start(bf16[1,192,4096]{2,1,0:T(8,128)(2,1)S(1)} %copy.28) | copy-start | bytes 4718596
  1.4 39.2 %collective-permute-start.2 = (bf16[192,4096]{1,0:T(8,128)(2,1)S(1)}, bf16[192,4096]{1,0:T(8,128)(2,1)S(1)}, u32[]{:S(2)}, u32[]{:S(2)}) collective-permute-start(bf16[192,4096]{1,0:T(8,128)(2,1)S(1)} %bitcast.15), channel_id=1, source_target_pairs={{0,32},{32,64},{64,96},{96,0},{1,33},{33,65},{65,97},{97,1},{2,34}... | collective-permute-start | bytes 4718600 | tf_op jit(solution)/shard_map/ppermute | solution.py:25
  4.8 38.9 %collective-permute-start.4 = (bf16[192,4096]{1,0:T(8,128)(2,1)S(1)}, bf16[192,4096]{1,0:T(8,128)(2,1)}, u32[]{:S(2)}, u32[]{:S(2)}) collective-permute-start(bf16[192,4096]{1,0:T(8,128)(2,1)S(1)} %bitcast.16), channel_id=1, source_target_pairs={{0,96},{32,0},{64,32},{96,64},{1,97},{33,1},{65,33},{97,65},{2,98}... | collective-permute-start | bytes 4718600 | tf_op jit(solution)/shard_map/ppermute | solution.py:25
  8.5 42.3 %collective-permute-start = (bf16[192,4096]{1,0:T(8,128)(2,1)S(1)}, bf16[192,4096]{1,0:T(8,128)(2,1)}, u32[]{:S(2)}, u32[]{:S(2)}) collective-permute-start(bf16[192,4096]{1,0:T(8,128)(2,1)S(1)} %bitcast.17), channel_id=1, source_target_pairs={{0,256},{384,128},{128,0},{1,257},{385,129},{129,1},{2,258},{386,1... | collective-permute-start | bytes 4718600 | tf_op jit(solution)/shard_map/ppermute | solution.py:186
  14.7 3.1 %copy-start.2 = (bf16[256,256]{1,0:T(8,128)(2,1)S(1)}, bf16[256,256]{1,0:T(8,128)(2,1)}, u32[]{:S(2)}) copy-start(bf16[256,256]{1,0:T(8,128)(2,1)} %constant.39.clone.order_ref) | copy-start | bytes 393220
  17.7 1.0 copy-start.5
  18.7 1.0 copy-start.7
  23.9 22.0 %copy-start.3 = (bf16[4096,192]{1,0:T(8,128)(2,1)}, bf16[4096,192]{1,0:T(8,128)(2,1)S(1)}, u32[]{:S(2)}) copy-start(bf16[4096,192]{1,0:T(8,128)(2,1)S(1)} %shard_map.93.refs_5_.refs_2_) | copy-start | bytes 4718596
  41.6 34.8 %collective-permute-start.3 = (bf16[96,4096]{1,0:T(8,128)(2,1)}, bf16[96,4096]{1,0:T(8,128)(2,1)}, u32[]{:S(2)}, u32[]{:S(2)}) collective-permute-start(bf16[96,4096]{1,0:T(8,128)(2,1)} %slice.145), channel_id=1, source_target_pairs={{0,32},{32,64},{64,96},{96,0},{1,33},{33,65},{65,97},{97,1},{2,34}... | collective-permute-start | bytes 2359304 | tf_op jit(solution)/shard_map/ppermute | solution.py:25
  45.9 31.6 %collective-permute-start.5 = (bf16[96,4096]{1,0:T(8,128)(2,1)}, bf16[96,4096]{1,0:T(8,128)(2,1)}, u32[]{:S(2)}, u32[]{:S(2)}) collective-permute-start(bf16[96,4096]{1,0:T(8,128)(2,1)} %slice.146), channel_id=1, source_target_pairs={{0,96},{32,0},{64,32},{96,64},{1,97},{33,1},{65,33},{97,65},{2,98}... | collective-permute-start | bytes 2359304 | tf_op jit(solution)/shard_map/ppermute | solution.py:25
  50.8 40.4 %collective-permute-start.1 = (bf16[192,4096]{1,0:T(8,128)(2,1)}, bf16[192,4096]{1,0:T(8,128)(2,1)S(1)}, u32[]{:S(2)}, u32[]{:S(2)}) collective-permute-start(bf16[192,4096]{1,0:T(8,128)(2,1)} %shard_map.91.refs_0_), channel_id=1, source_target_pairs={{0,384},{256,128},{384,256},{1,385},{257,129},{385,257},{2,386},{2... | collective-permute-start | bytes 4718600 | tf_op jit(solution)/shard_map/ppermute | solution.py:188
  59.0 1.0 copy-start.6
  60.0 1.0 copy-start.8
  78.7 4.4 %copy-start.1 = (bf16[192,4096]{1,0:T(8,128)(2,1)S(1)}, bf16[192,4096]{1,0:T(8,128)(2,1)}, u32[]{:S(2)}) copy-start(bf16[192,4096]{1,0:T(8,128)(2,1)} %shard_map.91.refs_0_) | copy-start | bytes 4718596
  78.7 4.4 %copy-start.4 = (bf16[4096,192]{1,0:T(8,128)(2,1)S(1)}, bf16[4096,192]{1,0:T(8,128)(2,1)}, u32[]{:S(2)}) copy-start(bf16[4096,192]{1,0:T(8,128)(2,1)} %copy-done.3) | copy-start | bytes 4718596
  101.4 48.3 %all-to-all-start.1 = ((f32[16,112,128]{2,1,0:T(8,128)}), f32[16,112,128]{2,1,0:T(8,128)S(1)}, u32[]{:S(2)}, u32[]{:S(2)}) async-start(f32[16,112,128]{2,1,0:T(8,128)} %fusion), calls=%async_computation.1 | async-start | bytes 1835008 | tf_op jit(solution)/shard_map/all_to_all | solution.py:211
  150.0 15.6 %collective-permute-start.9 = (f32[4,6,192]{2,1,0:T(8,128)S(1)}, f32[4,6,192]{2,1,0:T(8,128)S(1)}, u32[]{:S(2)}, u32[]{:S(2)}) collective-permute-start(f32[4,6,192]{2,1,0:T(8,128)S(1)} %pad_maximum_fusion.1), channel_id=1, source_target_pairs={{128,384},{256,0},{129,385},{257,1},{130,386},{258,2},{131,387},{2... | collective-permute-start | bytes 55304 | tf_op jit(solution)/shard_map/ppermute | solution.py:216
  151.3 14.2 %collective-permute-start.8 = (f32[2,6,192]{2,1,0:T(8,128)S(1)}, f32[2,6,192]{2,1,0:T(8,128)S(1)}, u32[]{:S(2)}, u32[]{:S(2)}) collective-permute-start(f32[2,6,192]{2,1,0:T(8,128)S(1)} %pad_maximum_fusion.4), channel_id=1, source_target_pairs={{0,32},{32,64},{64,96},{96,0},{1,33},{33,65},{65,97},{97,1},{2,34}... | collective-permute-start | bytes 27656 | tf_op jit(solution)/shard_map/ppermute | solution.py:25
  153.2 7.1 %collective-permute-start.6 = (f32[2,6,192]{2,1,0:T(8,128)S(1)}, f32[2,6,192]{2,1,0:T(8,128)S(1)}, u32[]{:S(2)}, u32[]{:S(2)}) collective-permute-start(f32[2,6,192]{2,1,0:T(8,128)S(1)} %pad_maximum_fusion.2), channel_id=1, source_target_pairs={{0,96},{32,0},{64,32},{96,64},{1,97},{33,1},{65,33},{97,65},{2,98}... | collective-permute-start | bytes 27656 | tf_op jit(solution)/shard_map/ppermute | solution.py:25
  158.4 7.1 %collective-permute-start.7 = (f32[2,6,192]{2,1,0:T(8,128)S(1)}, f32[2,6,192]{2,1,0:T(8,128)S(1)}, u32[]{:S(2)}, u32[]{:S(2)}) collective-permute-start(f32[2,6,192]{2,1,0:T(8,128)S(1)} %pad_maximum_fusion.3), channel_id=1, source_target_pairs={{0,64},{32,96},{64,0},{96,32},{1,65},{33,97},{65,1},{97,33},{2,66}... | collective-permute-start | bytes 27656 | tf_op jit(solution)/shard_map/ppermute | solution.py:25

commit v3 on v2

--- a/solution.py
+++ b/solution.py
@@ -23,22 +23,6 @@
 def moved(value, axis, steps):
     count = lax.axis_size(axis)
     return lax.ppermute(value, axis, [(s, (s + steps) % count) for s in range(count)])
-
-
-def held_kernel(value_ref, *refs):
-    pass
-
-
-def held(value, *others):
-    anywhere = pl.BlockSpec(memory_space=pl.ANY)
-    return pl.pallas_call(
-        held_kernel,
-        out_shape=jax.ShapeDtypeStruct(value.shape, value.dtype),
-        in_specs=[anywhere] * (1 + len(others)),
-        out_specs=anywhere,
-        input_output_aliases={0: 0},
-        cost_estimate=COST,
-    )(value, *others)
 
 
 def spread():
@@ -91,8 +75,11 @@
     return lax.dot_general(a, b, (dims, ((), ())), preferred_element_type=jnp.float32)
 
 
-def weigh_kernel(p_ref, inner_ref, outer_ref, order_ref, w_ref, t_ref):
+def weigh_kernel(p_ref, inner_ref, outer_ref, order_ref, w_ref, *rest):
+    *copies, t_ref = rest
     tiles = p_ref.shape[1] // TILE
+    for copy in copies:
+        copy[...] = p_ref[...]
 
     @pl.loop(0, tiles, unroll=tiles)
     def _(b):
@@ -115,11 +102,12 @@
         w_ref[pl.ds(pl.multiple_of(b * TILE, TILE), TILE), :] = y.astype(jnp.bfloat16)
 
 
-def weigh(rows, tiles):
+def weigh(rows, tiles, copied=False):
     width = rows.shape[1]
+    out = jax.ShapeDtypeStruct((width, ROWS), jnp.bfloat16)
     return pl.pallas_call(
         weigh_kernel,
-        out_shape=jax.ShapeDtypeStruct((width, ROWS), jnp.bfloat16),
+        out_shape=(out, jax.ShapeDtypeStruct(rows.shape, rows.dtype)) if copied else out,
         scratch_shapes=[pltpu.VMEM((width // TILE, TILE, ROWS), jnp.float32)],
         compiler_params=pltpu.CompilerParams(vmem_limit_bytes=24 * 2**20),
         cost_estimate=COST,
@@ -184,10 +172,10 @@
     p0 = grads[0]
     p1, p3 = moved(p0, "x", 1), moved(p0, "x", -1)
     p4 = lax.ppermute(p0, "zl", [(0, 2), (3, 1), (1, 0)])
-    own = held(p0, p4)
+    w0, own = weigh(p0, tiles, copied=True)
     p5 = lax.ppermute(own, "zl", [(0, 3), (2, 1), (3, 2)])
     p2 = jnp.concatenate([moved(p1[:half], "x", 1), moved(p3[half:], "x", -1)])
-    w0, w1, w2, w3, w4 = (weigh(p, tiles) for p in (p0, p1, p2, p3, p4))
+    w1, w2, w3, w4 = (weigh(p, tiles) for p in (p1, p2, p3, p4))
     early = products(
         [own, p1, p2, p3, p4],
         [w0, w1, w2, w3, w4],

time: 167 us -> 158 us (0.946)
  the two profiles are of different devices: /device:TPU:32 before, /device:TPU:64 now
where the time goes in v3:
time: 158 us; the launch traced here: 157 us
  waiting for transfers between devices  56.1 us (36%)
  starting transfers between devices  50.6 us (32%)
  Pallas kernels  37.9 us (24%)
  blocking collectives  5.21 us (3%)
  local copies, waits for them, and re-layouts  5.08 us (3%)
  other arithmetic  1.89 us (1%)
    all_to_all x1, waiting for transfers between devices, per_device(): part = lax.all_to_all(part, ('y', 'zh'), 0, 0, tiled=False).sum(0)  32.2 us
    ppermute x7, starting transfers between devices, moved(): lax.ppermute(value, axis, [(s, (s + steps) % count) for s in range(count)])  23.8 us
    pallas_call x5, Pallas kernels, weigh(): pl.pallas_call(weigh_kernel, out_shape=(out, jax.ShapeDtypeStruct(rows.sh...  23.8 us
    ppermute x7, waiting for transfers between devices, moved(): lax.ppermute(value, axis, [(s, (s + steps) % count) for s in range(count)])  16.8 us
    all_to_all x1, starting transfers between devices, per_device(): part = lax.all_to_all(part, ('y', 'zh'), 0, 0, tiled=False).sum(0)  13.8 us
    pallas_call x2, Pallas kernels, products(): pl.pallas_call(functools.partial(products_kernel, picks, len(plains), len...  11 us
    ppermute x1, waiting for transfers between devices, per_device(): p5 = lax.ppermute(own, 'zl', [(0, 3), (2, 1), (3, 2)])  7.01 us
    ppermute x1, starting transfers between devices, per_device(): p4 = lax.ppermute(p0, 'zl', [(0, 2), (3, 1), (1, 0)])  6.94 us
  transfers between devices with their start and end apart: 11, of which 6 were waited for; matrix products, arithmetic and copies ran while one was open for 0% of the time, Pallas kernels for 21%

profile of v3, /device:TPU:64, one launch (start us, length us, event | category | flops | bytes accessed | tf_op | source)
XLA Modules:
  0.0 157.2 jit_solution(15799418127328264647)
XLA Ops:
  0.0 3.4 %collective-permute-start.2 = (bf16[192,4096]{1,0:T(8,128)(2,1)}, bf16[192,4096]{1,0:T(8,128)(2,1)S(1)}, u32[]{:S(2)}, u32[]{:S(2)}) collective-permute-start(bf16[192,4096]{1,0:T(8,128)(2,1)} %bitcast.15), channel_id=1, source_target_pairs={{0,32},{32,64},{64,96},{96,0},{1,33},{33,65},{65,97},{97,1},{2,34}... | collective-permute-start | bytes 4718600 | tf_op jit(solution)/shard_map/ppermute | solution.py:25
  3.4 3.7 %collective-permute-start.4 = (bf16[192,4096]{1,0:T(8,128)(2,1)}, bf16[192,4096]{1,0:T(8,128)(2,1)S(1)}, u32[]{:S(2)}, u32[]{:S(2)}) collective-permute-start(bf16[192,4096]{1,0:T(8,128)(2,1)} %bitcast.16), channel_id=1, source_target_pairs={{0,96},{32,0},{64,32},{96,64},{1,97},{33,1},{65,33},{97,65},{2,98}... | collective-permute-start | bytes 4718600 | tf_op jit(solution)/shard_map/ppermute | solution.py:25
  7.1 6.9 %collective-permute-start = (bf16[192,4096]{1,0:T(8,128)(2,1)}, bf16[192,4096]{1,0:T(8,128)(2,1)}, u32[]{:S(2)}, u32[]{:S(2)}) collective-permute-start(bf16[192,4096]{1,0:T(8,128)(2,1)} %bitcast.17), channel_id=1, source_target_pairs={{0,256},{384,128},{128,0},{1,257},{385,129},{129,1},{2,258},{386,1... | collective-permute-start | bytes 4718600 | tf_op jit(solution)/shard_map/ppermute | solution.py:174
  14.0 3.0 %shard_map.91 = (bf16[256,768]{1,0:T(8,128)(2,1)}, bf16[256,768]{1,0:T(8,128)(2,1)}) custom-call(f32[64,64]{1,0:T(8,128)} %bitcast.28, f32[64,64]{1,0:T(8,128)} %bitcast.29, f32[256,64]{1,0:T(8,128)} %constant.34.clone.four_ref, f32[256,64]{1,0:T(8,128)} %constant.35.clone.last_ref, f32[256,64]{1,0:T(8,128)} %constant.36.clone.mixed_ref, ...), custom_call_target="tpu_custom_call" | custom-call | flops 10000000000 | bytes 1000000 | tf_op jit(solution)/shard_map/pallas_call | solution.py:68
  17.1 1.4 copy-done
  20.5 5.4 %shard_map.92 = (bf16[4096,192]{1,0:T(8,128)(2,1)S(1)}, bf16[192,4096]{1,0:T(8,128)(2,1)}) custom-call(bf16[192,4096]{1,0:T(8,128)(2,1)S(1)} %bitcast.18, bf16[256,768]{1,0:T(8,128)(2,1)S(1)} %copy-done.4, bf16[256,768]{1,0:T(8,128)(2,1)S(1)} %copy-done.6, bf16[256,256]{1,0:T(8,128)(2,1)S(1)} %copy-done.1), custom_call_target="tpu_custom_call" | custom-call | flops 10000000000 | bytes 1000000 | tf_op jit(solution)/shard_map/pallas_call | solution.py:108
  28.6 10.9 %collective-permute-done.2.p_ref.refs_1_ = bf16[192,4096]{1,0:T(8,128)(2,1)S(1)} collective-permute-done((bf16[192,4096]{1,0:T(8,128)(2,1)}, bf16[192,4096]{1,0:T(8,128)(2,1)S(1)}, u32[]{:S(2)}, u32[]{:S(2)}) %collective-permute-start.2) | collective-permute-done | bytes 1572896 | tf_op jit(solution)/shard_map/ppermute | solution.py:25
  39.5 2.2 %collective-permute-start.3 = (bf16[96,4096]{1,0:T(8,128)(2,1)S(1)}, bf16[96,4096]{1,0:T(8,128)(2,1)S(1)}, u32[]{:S(2)}, u32[]{:S(2)}) collective-permute-start(bf16[96,4096]{1,0:T(8,128)(2,1)S(1)} %slice.145), channel_id=1, source_target_pairs={{0,32},{32,64},{64,96},{96,0},{1,33},{33,65},{65,97},{97,1},{2,34}... | collective-permute-start | bytes 2359304 | tf_op jit(solution)/shard_map/ppermute | solution.py:25
  41.8 5.0 %collective-permute-start.5 = (bf16[96,4096]{1,0:T(8,128)(2,1)S(1)}, bf16[96,4096]{1,0:T(8,128)(2,1)S(1)}, u32[]{:S(2)}, u32[]{:S(2)}) collective-permute-start(bf16[96,4096]{1,0:T(8,128)(2,1)S(1)} %slice.146), channel_id=1, source_target_pairs={{0,96},{32,0},{64,32},{96,64},{1,97},{33,1},{65,33},{97,65},{2,98}... | collective-permute-start | bytes 2359304 | tf_op jit(solution)/shard_map/ppermute | solution.py:25
  46.8 4.2 %shard_map.93.refs_6_.refs_3_ = bf16[4096,192]{1,0:T(8,128)(2,1)S(1)} custom-call(bf16[192,4096]{1,0:T(8,128)(2,1)S(1)} %collective-permute-done.2.p_ref.refs_1_, bf16[256,768]{1,0:T(8,128)(2,1)S(1)} %copy-done.5, bf16[256,768]{1,0:T(8,128)(2,1)S(1)} %copy-done.7, bf16[256,256]{1,0:T(8,128)(2,1)S(1)} %copy-done.1), custom_call_target="tpu_custom_call" | custom-call | flops 10000000000 | bytes 1000000 | tf_op jit(solution)/shard_map/pallas_call | solution.py:108
  51.0 4.2 %shard_map.95.refs_8_.refs_5_ = bf16[4096,192]{1,0:T(8,128)(2,1)S(1)} custom-call(bf16[192,4096]{1,0:T(8,128)(2,1)S(1)} %collective-permute-done.4.p_ref.refs_3_, bf16[256,768]{1,0:T(8,128)(2,1)S(1)} %copy-done.5, bf16[256,768]{1,0:T(8,128)(2,1)S(1)} %copy-done.7, bf16[256,256]{1,0:T(8,128)(2,1)S(1)} %copy-done.1), custom_call_target="tpu_custom_call" | custom-call | flops 10000000000 | bytes 1000000 | tf_op jit(solution)/shard_map/pallas_call | solution.py:108
  55.2 5.6 %shard_map.96.refs_9_ = bf16[4096,192]{1,0:T(8,128)(2,1)S(1)} custom-call(bf16[192,4096]{1,0:T(8,128)(2,1)} %collective-permute-done.p_ref.refs_4_.refs_0_, bf16[256,768]{1,0:T(8,128)(2,1)S(1)} %copy-done.5, bf16[256,768]{1,0:T(8,128)(2,1)S(1)} %copy-done.7, bf16[256,256]{1,0:T(8,128)(2,1)S(1)} %copy-done.1), custom_call_target="tpu_custom_call" | custom-call | flops 10000000000 | bytes 1000000 | tf_op jit(solution)/shard_map/pallas_call | solution.py:108
  62.3 4.4 %shard_map.94.refs_7_.refs_4_ = bf16[4096,192]{1,0:T(8,128)(2,1)S(1)} custom-call(bf16[192,4096]{1,0:T(8,128)(2,1)S(1)} %constant_dynamic-update-slice_fusion.p_ref.refs_2_, bf16[256,768]{1,0:T(8,128)(2,1)S(1)} %copy-done.5, bf16[256,768]{1,0:T(8,128)(2,1)S(1)} %copy-done.7, bf16[256,256]{1,0:T(8,128)(2,1)S(1)} %copy-done.1), custom_call_target="tpu_custom_call" | custom-call | flops 10000000000 | bytes 1000000 | tf_op jit(solution)/shard_map/pallas_call | solution.py:108
  66.8 6.6 %shard_map.97.refs_6_ = f32[2,16,112,128]{3,2,1,0:T(8,128)S(1)} custom-call(s32[2]{0:T(128)S(1)} %pad_add_fusion.place_ref, bf16[192,4096]{1,0:T(8,128)(2,1)} %get-tuple-element.11.refs_0_, bf16[192,4096]{1,0:T(8,128)(2,1)S(1)} %collective-permute-done.2.p_ref.refs_1_, bf16[192,4096]{1,0:T(8,128)(2,1)S(1)} %constant_dynamic-update-slice_fusion.p_ref.refs_2_, ...), custom_call_target="tpu_custom_call" | custom-call | flops 10000000000 | bytes 1000000 | tf_op jit(solution)/shard_map/pallas_call | solution.py:149
  73.4 7.0 %collective-permute-done.1.refs_1_ = bf16[192,4096]{1,0:T(8,128)(2,1)} collective-permute-done((bf16[192,4096]{1,0:T(8,128)(2,1)}, bf16[192,4096]{1,0:T(8,128)(2,1)}, u32[]{:S(2)}, u32[]{:S(2)}) %collective-permute-start.1) | collective-permute-done | bytes 1572896 | tf_op jit(solution)/shard_map/ppermute | solution.py:176
  80.4 4.5 %shard_map.98 = f32[2,16,112,128]{3,2,1,0:T(8,128)S(1)} custom-call(s32[2]{0:T(128)S(1)} %pad_add_fusion.place_ref, bf16[192,4096]{1,0:T(8,128)(2,1)} %collective-permute-done.p_ref.refs_4_.refs_0_, bf16[192,4096]{1,0:T(8,128)(2,1)} %collective-permute-done.1.refs_1_, bf16[4096,192]{1,0:T(8,128)(2,1)S(1)} %copy-done.3, ...), custom_call_target="tpu_custom_call" | custom-call | flops 10000000000 | bytes 1000000 | tf_op jit(solution)/shard_map/pallas_call | solution.py:149
  84.9 5.2 %all_to_all.10 = f32[2,16,112,128]{3,2,1,0:T(8,128)S(1)} all-to-all(f32[2,16,112,128]{3,2,1,0:T(8,128)S(1)} %shard_map.98), channel_id=1, replica_groups=mesh['zl'=4,'x'=4,'y'=8,'zh'=2,'c'=2] {'c'}, dimensions={0} | all-to-all | bytes 3670016 | tf_op jit(solution)/shard_map/all_to_all | solution.py:197
  91.1 13.8 %all-to-all-start.1 = ((f32[16,112,128]{2,1,0:T(8,128)}), f32[16,112,128]{2,1,0:T(8,128)S(1)}, u32[]{:S(2)}, u32[]{:S(2)}) async-start(f32[16,112,128]{2,1,0:T(8,128)} %fusion), calls=%async_computation.1 | async-start | bytes 1835008 | tf_op jit(solution)/shard_map/all_to_all | solution.py:199
  105.0 32.2 %all-to-all-done.1 = f32[16,112,128]{2,1,0:T(8,128)S(1)} async-done(((f32[16,112,128]{2,1,0:T(8,128)}), f32[16,112,128]{2,1,0:T(8,128)S(1)}, u32[]{:S(2)}, u32[]{:S(2)}) %all-to-all-start.1) | async-done | bytes 917536 | tf_op jit(solution)/shard_map/all_to_all | solution.py:199
  137.5 4.7 %collective-permute-start.9 = (f32[4,6,192]{2,1,0:T(8,128)S(1)}, f32[4,6,192]{2,1,0:T(8,128)S(1)}, u32[]{:S(2)}, u32[]{:S(2)}) collective-permute-start(f32[4,6,192]{2,1,0:T(8,128)S(1)} %pad_maximum_fusion.1), channel_id=1, source_target_pairs={{128,384},{256,0},{129,385},{257,1},{130,386},{258,2},{131,387},{2... | collective-permute-start | bytes 55304 | tf_op jit(solution)/shard_map/ppermute | solution.py:204
  142.2 2.2 %collective-permute-start.8 = (f32[2,6,192]{2,1,0:T(8,128)S(1)}, f32[2,6,192]{2,1,0:T(8,128)S(1)}, u32[]{:S(2)}, u32[]{:S(2)}) collective-permute-start(f32[2,6,192]{2,1,0:T(8,128)S(1)} %pad_maximum_fusion.4), channel_id=1, source_target_pairs={{0,32},{32,64},{64,96},{96,0},{1,33},{33,65},{65,97},{97,1},{2,34}... | collective-permute-start | bytes 27656 | tf_op jit(solution)/shard_map/ppermute | solution.py:25
  144.4 4.9 %collective-permute-start.6 = (f32[2,6,192]{2,1,0:T(8,128)S(1)}, f32[2,6,192]{2,1,0:T(8,128)S(1)}, u32[]{:S(2)}, u32[]{:S(2)}) collective-permute-start(f32[2,6,192]{2,1,0:T(8,128)S(1)} %pad_maximum_fusion.2), channel_id=1, source_target_pairs={{0,96},{32,0},{64,32},{96,64},{1,97},{33,1},{65,33},{97,65},{2,98}... | collective-permute-start | bytes 27656 | tf_op jit(solution)/shard_map/ppermute | solution.py:25
  149.3 2.5 %collective-permute-start.7 = (f32[2,6,192]{2,1,0:T(8,128)S(1)}, f32[2,6,192]{2,1,0:T(8,128)S(1)}, u32[]{:S(2)}, u32[]{:S(2)}) collective-permute-start(f32[2,6,192]{2,1,0:T(8,128)S(1)} %pad_maximum_fusion.3), channel_id=1, source_target_pairs={{0,64},{32,96},{64,0},{96,32},{1,65},{33,97},{65,1},{97,33},{2,66}... | collective-permute-start | bytes 27656 | tf_op jit(solution)/shard_map/ppermute | solution.py:25
  151.9 4.6 %collective-permute-done.7 = f32[2,6,192]{2,1,0:T(8,128)S(1)} collective-permute-done((f32[2,6,192]{2,1,0:T(8,128)S(1)}, f32[2,6,192]{2,1,0:T(8,128)S(1)}, u32[]{:S(2)}, u32[]{:S(2)}) %collective-permute-start.7) | collective-permute-done | bytes 9248 | tf_op jit(solution)/shard_map/ppermute | solution.py:25
  (52 shorter events, 8.2 us)
Async XLA Ops:
  0.0 39.4 %collective-permute-start.2 = (bf16[192,4096]{1,0:T(8,128)(2,1)}, bf16[192,4096]{1,0:T(8,128)(2,1)S(1)}, u32[]{:S(2)}, u32[]{:S(2)}) collective-permute-start(bf16[192,4096]{1,0:T(8,128)(2,1)} %bitcast.15), channel_id=1, source_target_pairs={{0,32},{32,64},{64,96},{96,0},{1,33},{33,65},{65,97},{97,1},{2,34}... | collective-permute-start | bytes 4718600 | tf_op jit(solution)/shard_map/ppermute | solution.py:25
  3.4 38.3 %collective-permute-start.4 = (bf16[192,4096]{1,0:T(8,128)(2,1)}, bf16[192,4096]{1,0:T(8,128)(2,1)S(1)}, u32[]{:S(2)}, u32[]{:S(2)}) collective-permute-start(bf16[192,4096]{1,0:T(8,128)(2,1)} %bitcast.16), channel_id=1, source_target_pairs={{0,96},{32,0},{64,32},{96,64},{1,97},{33,1},{65,33},{97,65},{2,98}... | collective-permute-start | bytes 4718600 | tf_op jit(solution)/shard_map/ppermute | solution.py:25
  7.1 48.2 %collective-permute-start = (bf16[192,4096]{1,0:T(8,128)(2,1)}, bf16[192,4096]{1,0:T(8,128)(2,1)}, u32[]{:S(2)}, u32[]{:S(2)}) collective-permute-start(bf16[192,4096]{1,0:T(8,128)(2,1)} %bitcast.17), channel_id=1, source_target_pairs={{0,256},{384,128},{128,0},{1,257},{385,129},{129,1},{2,258},{386,1... | collective-permute-start | bytes 4718600 | tf_op jit(solution)/shard_map/ppermute | solution.py:174
  14.0 3.1 %copy-start.1 = (bf16[256,256]{1,0:T(8,128)(2,1)S(1)}, bf16[256,256]{1,0:T(8,128)(2,1)}, u32[]{:S(2)}) copy-start(bf16[256,256]{1,0:T(8,128)(2,1)} %constant.39.clone.order_ref) | copy-start | bytes 393220
  17.1 1.4 copy-start
  18.5 1.0 copy-start.4
  19.5 1.0 copy-start.6
  25.8 1.3 copy-start.2
  27.2 53.2 %collective-permute-start.1 = (bf16[192,4096]{1,0:T(8,128)(2,1)}, bf16[192,4096]{1,0:T(8,128)(2,1)}, u32[]{:S(2)}, u32[]{:S(2)}) collective-permute-start(bf16[192,4096]{1,0:T(8,128)(2,1)} %get-tuple-element.11.refs_0_), channel_id=1, source_target_pairs={{0,384},{256,128},{384,256},{1,385},{257,129},{385,257},{2,386},{2... | collective-permute-start | bytes 4718600 | tf_op jit(solution)/shard_map/ppermute | solution.py:176
  28.5 18.3 %copy-start.5 = (bf16[256,768]{1,0:T(8,128)(2,1)S(1)}, bf16[256,768]{1,0:T(8,128)(2,1)}, u32[]{:S(2)}) copy-start(bf16[256,768]{1,0:T(8,128)(2,1)} %get-tuple-element.9.inner_ref) | copy-start | bytes 1179652
  28.5 18.3 %copy-start.7 = (bf16[256,768]{1,0:T(8,128)(2,1)S(1)}, bf16[256,768]{1,0:T(8,128)(2,1)}, u32[]{:S(2)}) copy-start(bf16[256,768]{1,0:T(8,128)(2,1)} %get-tuple-element.10.outer_ref) | copy-start | bytes 1179652
  39.5 21.5 %collective-permute-start.3 = (bf16[96,4096]{1,0:T(8,128)(2,1)S(1)}, bf16[96,4096]{1,0:T(8,128)(2,1)S(1)}, u32[]{:S(2)}, u32[]{:S(2)}) collective-permute-start(bf16[96,4096]{1,0:T(8,128)(2,1)S(1)} %slice.145), channel_id=1, source_target_pairs={{0,32},{32,64},{64,96},{96,0},{1,33},{33,65},{65,97},{97,1},{2,34}... | collective-permute-start | bytes 2359304 | tf_op jit(solution)/shard_map/ppermute | solution.py:25
  41.8 20.5 %collective-permute-start.5 = (bf16[96,4096]{1,0:T(8,128)(2,1)S(1)}, bf16[96,4096]{1,0:T(8,128)(2,1)S(1)}, u32[]{:S(2)}, u32[]{:S(2)}) collective-permute-start(bf16[96,4096]{1,0:T(8,128)(2,1)S(1)} %slice.146), channel_id=1, source_target_pairs={{0,96},{32,0},{64,32},{96,64},{1,97},{33,1},{65,33},{97,65},{2,98}... | collective-permute-start | bytes 2359304 | tf_op jit(solution)/shard_map/ppermute | solution.py:25
  62.3 4.5 %copy-start.3 = (bf16[4096,192]{1,0:T(8,128)(2,1)S(1)}, bf16[4096,192]{1,0:T(8,128)(2,1)}, u32[]{:S(2)}) copy-start(bf16[4096,192]{1,0:T(8,128)(2,1)} %copy-done.2) | copy-start | bytes 4718596
  91.1 46.1 %all-to-all-start.1 = ((f32[16,112,128]{2,1,0:T(8,128)}), f32[16,112,128]{2,1,0:T(8,128)S(1)}, u32[]{:S(2)}, u32[]{:S(2)}) async-start(f32[16,112,128]{2,1,0:T(8,128)} %fusion), calls=%async_computation.1 | async-start | bytes 1835008 | tf_op jit(solution)/shard_map/all_to_all | solution.py:199
  137.5 19.0 %collective-permute-start.9 = (f32[4,6,192]{2,1,0:T(8,128)S(1)}, f32[4,6,192]{2,1,0:T(8,128)S(1)}, u32[]{:S(2)}, u32[]{:S(2)}) collective-permute-start(f32[4,6,192]{2,1,0:T(8,128)S(1)} %pad_maximum_fusion.1), channel_id=1, source_target_pairs={{128,384},{256,0},{129,385},{257,1},{130,386},{258,2},{131,387},{2... | collective-permute-start | bytes 55304 | tf_op jit(solution)/shard_map/ppermute | solution.py:204
  142.2 14.2 %collective-permute-start.8 = (f32[2,6,192]{2,1,0:T(8,128)S(1)}, f32[2,6,192]{2,1,0:T(8,128)S(1)}, u32[]{:S(2)}, u32[]{:S(2)}) collective-permute-start(f32[2,6,192]{2,1,0:T(8,128)S(1)} %pad_maximum_fusion.4), channel_id=1, source_target_pairs={{0,32},{32,64},{64,96},{96,0},{1,33},{33,65},{65,97},{97,1},{2,34}... | collective-permute-start | bytes 27656 | tf_op jit(solution)/shard_map/ppermute | solution.py:25
  144.4 7.4 %collective-permute-start.6 = (f32[2,6,192]{2,1,0:T(8,128)S(1)}, f32[2,6,192]{2,1,0:T(8,128)S(1)}, u32[]{:S(2)}, u32[]{:S(2)}) collective-permute-start(f32[2,6,192]{2,1,0:T(8,128)S(1)} %pad_maximum_fusion.2), channel_id=1, source_target_pairs={{0,96},{32,0},{64,32},{96,64},{1,97},{33,1},{65,33},{97,65},{2,98}... | collective-permute-start | bytes 27656 | tf_op jit(solution)/shard_map/ppermute | solution.py:25
  149.3 7.1 %collective-permute-start.7 = (f32[2,6,192]{2,1,0:T(8,128)S(1)}, f32[2,6,192]{2,1,0:T(8,128)S(1)}, u32[]{:S(2)}, u32[]{:S(2)}) collective-permute-start(f32[2,6,192]{2,1,0:T(8,128)S(1)} %pad_maximum_fusion.3), channel_id=1, source_target_pairs={{0,64},{32,96},{64,0},{96,32},{1,65},{33,97},{65,1},{97,33},{2,66}... | collective-permute-start | bytes 27656 | tf_op jit(solution)/shard_map/ppermute | solution.py:25

commit v4 on v3

--- a/solution.py
+++ b/solution.py
@@ -129,7 +129,12 @@
             pl.when(here < least)(functools.partial(score, slot, *below))
             pl.when(here >= least)(functools.partial(score, slot, *reached))
     if given:
-        out_ref[:, :, : first * PIECE] = given[0][:, :, : first * PIECE]
+        before = given[0][:, :, : first * PIECE]
+        out_ref[:, :, : first * PIECE] = before
+        top = jnp.maximum(jnp.max(jnp.abs(before)), jnp.max(jnp.abs(total[...])))
+        end = (first + len(picks)) * PIECE
+        left = out_ref.shape[2] - end
+        out_ref[:, :, end:] = jnp.full((NC, NL, left, LANES), top, jnp.float32)
     for pair in range(len(picks) // 2):
         a, b = total[2 * pair], total[2 * pair + 1]
         rest = jnp.concatenate([a[:, LANES:], b[:, LANES:]], axis=1)
@@ -162,6 +167,16 @@
     part = part[: slots * PIECE].reshape(slots // 2, 3, OWN, LANES)
     rest = part[:, 2].reshape(slots // 2, OWN, 2, ROWS - LANES).transpose(0, 2, 1, 3)
     return jnp.concatenate([part[:, :2], rest], axis=-1).reshape(slots, OWN, ROWS)
+
+
+def layer_sum(pair, end):
+    bound = jnp.maximum(pair[0, 0, end, 0] + pair[1, 0, end, 0], 1e-30)
+    power = jnp.floor(jnp.log2(bound)) - 14
+    scaled = (pair[0, :, :end] + pair[1, :, :end]) * jnp.exp2(-power)
+    powers = jnp.full((NL, pair.shape[2] - end, LANES), power, jnp.float32)
+    sent = jnp.concatenate([scaled, powers], axis=1).astype(jnp.float16)
+    got = lax.all_to_all(sent, ("y", "zh"), 0, 0, tiled=False).astype(jnp.float32)
+    return (got[:, :end] * jnp.exp2(got[:, end : end + 1, :1])).sum(0)
 
 
 def per_device(grads, in_factor, out_factor):
@@ -195,9 +210,7 @@
         [p4, p5], [w0, w1, w2, w3], [(0, 1, (0, r), (1, r)) for r in range(NX)], 12, 8, early
     )
     pair = lax.all_to_all(sums, "c", 0, 0, tiled=False)
-    part = pair[0] + pair[1]
-    part = lax.all_to_all(part, ("y", "zh"), 0, 0, tiled=False).sum(0)
-    slots = unpacked(part, 12)
+    slots = unpacked(layer_sum(pair, 12 * PIECE), 12)
     row, two, again, following = slots[:3], slots[3:7], slots[7], slots[8:]
     out = [None] * 9
     out[0], out[4] = row[0], following[0]

time: 158 us -> 148 us (0.937)
  waiting for transfers between devices: 56.1 us -> 44.3 us
    all_to_all x1, waiting for transfers between devices: 32.2 us -> 20.5 us  [layer_sum(): lax.all_to_all(sent, ('y', 'zh'), 0, 0, tiled=False).astype(jnp.float32)]
  transfers between devices with their start and end apart: 11 -> 11, of which waited for: 6 -> 6; matrix products, arithmetic and copies ran while one was open for 0% -> 0% of each run, Pallas kernels for 21% -> 23%
where the time goes in v4:
time: 148 us; the launch traced here: 147 us
  starting transfers between devices  50.1 us (34%)
  waiting for transfers between devices  44.3 us (30%)
  Pallas kernels  38 us (26%)
  local copies, waits for them, and re-layouts  6.55 us (4%)
  blocking collectives  5.21 us (4%)
  between operations  1.91 us (1%)
    ppermute x7, starting transfers between devices, moved(): lax.ppermute(value, axis, [(s, (s + steps) % count) for s in range(count)])  23.8 us
    pallas_call x5, Pallas kernels, weigh(): pl.pallas_call(weigh_kernel, out_shape=(out, jax.ShapeDtypeStruct(rows.sh...  23.8 us
    all_to_all x1, waiting for transfers between devices, layer_sum(): lax.all_to_all(sent, ('y', 'zh'), 0, 0, tiled=False).astype(jnp.float32)  20.5 us
    ppermute x7, waiting for transfers between devices, moved(): lax.ppermute(value, axis, [(s, (s + steps) % count) for s in range(count)])  16.8 us
    all_to_all x1, starting transfers between devices, layer_sum(): lax.all_to_all(sent, ('y', 'zh'), 0, 0, tiled=False).astype(jnp.float32)  13.8 us
    pallas_call x2, Pallas kernels, products(): pl.pallas_call(functools.partial(products_kernel, picks, len(plains), len...  11.2 us
    ppermute x1, waiting for transfers between devices, per_device(): p5 = lax.ppermute(own, 'zl', [(0, 3), (2, 1), (3, 2)])  7.01 us
    ppermute x1, starting transfers between devices, per_device(): p4 = lax.ppermute(p0, 'zl', [(0, 2), (3, 1), (1, 0)])  6.94 us
  transfers between devices with their start and end apart: 11, of which 6 were waited for; matrix products, arithmetic and copies ran while one was open for 0% of the time, Pallas kernels for 23%

profile of v4, /device:TPU:64, one launch (start us, length us, event | category | flops | bytes accessed | tf_op | source)
XLA Modules:
  0.0 147.5 jit_solution(4039810580117546474)
XLA Ops:
  0.0 3.4 %collective-permute-start.2 = (bf16[192,4096]{1,0:T(8,128)(2,1)}, bf16[192,4096]{1,0:T(8,128)(2,1)S(1)}, u32[]{:S(2)}, u32[]{:S(2)}) collective-permute-start(bf16[192,4096]{1,0:T(8,128)(2,1)} %bitcast.16), channel_id=1, source_target_pairs={{0,32},{32,64},{64,96},{96,0},{1,33},{33,65},{65,97},{97,1},{2,34}... | collective-permute-start | bytes 4718600 | tf_op jit(solution)/shard_map/ppermute | solution.py:25
  3.4 3.7 %collective-permute-start.4 = (bf16[192,4096]{1,0:T(8,128)(2,1)}, bf16[192,4096]{1,0:T(8,128)(2,1)S(1)}, u32[]{:S(2)}, u32[]{:S(2)}) collective-permute-start(bf16[192,4096]{1,0:T(8,128)(2,1)} %bitcast.17), channel_id=1, source_target_pairs={{0,96},{32,0},{64,32},{96,64},{1,97},{33,1},{65,33},{97,65},{2,98}... | collective-permute-start | bytes 4718600 | tf_op jit(solution)/shard_map/ppermute | solution.py:25
  7.1 6.9 %collective-permute-start = (bf16[192,4096]{1,0:T(8,128)(2,1)}, bf16[192,4096]{1,0:T(8,128)(2,1)}, u32[]{:S(2)}, u32[]{:S(2)}) collective-permute-start(bf16[192,4096]{1,0:T(8,128)(2,1)} %bitcast.18), channel_id=1, source_target_pairs={{0,256},{384,128},{128,0},{1,257},{385,129},{129,1},{2,258},{386,1... | collective-permute-start | bytes 4718600 | tf_op jit(solution)/shard_map/ppermute | solution.py:189
  14.0 3.0 %shard_map.91 = (bf16[256,768]{1,0:T(8,128)(2,1)}, bf16[256,768]{1,0:T(8,128)(2,1)}) custom-call(f32[64,64]{1,0:T(8,128)} %bitcast.28, f32[64,64]{1,0:T(8,128)} %bitcast.29, f32[256,64]{1,0:T(8,128)} %constant.46.clone.four_ref, f32[256,64]{1,0:T(8,128)} %constant.47.clone.last_ref, f32[256,64]{1,0:T(8,128)} %constant.48.clone.mixed_ref, ...), custom_call_target="tpu_custom_call" | custom-call | flops 10000000000 | bytes 1000000 | tf_op jit(solution)/shard_map/pallas_call | solution.py:68
  17.1 1.4 copy-done
  20.5 5.4 %shard_map.92 = (bf16[4096,192]{1,0:T(8,128)(2,1)S(1)}, bf16[192,4096]{1,0:T(8,128)(2,1)}) custom-call(bf16[192,4096]{1,0:T(8,128)(2,1)S(1)} %bitcast.19, bf16[256,768]{1,0:T(8,128)(2,1)S(1)} %copy-done.4, bf16[256,768]{1,0:T(8,128)(2,1)S(1)} %copy-done.6, bf16[256,256]{1,0:T(8,128)(2,1)S(1)} %copy-done.1), custom_call_target="tpu_custom_call" | custom-call | flops 10000000000 | bytes 1000000 | tf_op jit(solution)/shard_map/pallas_call | solution.py:108
  28.6 10.9 %collective-permute-done.2.p_ref.refs_1_ = bf16[192,4096]{1,0:T(8,128)(2,1)S(1)} collective-permute-done((bf16[192,4096]{1,0:T(8,128)(2,1)}, bf16[192,4096]{1,0:T(8,128)(2,1)S(1)}, u32[]{:S(2)}, u32[]{:S(2)}) %collective-permute-start.2) | collective-permute-done | bytes 1572896 | tf_op jit(solution)/shard_map/ppermute | solution.py:25
  39.5 2.2 %collective-permute-start.3 = (bf16[96,4096]{1,0:T(8,128)(2,1)S(1)}, bf16[96,4096]{1,0:T(8,128)(2,1)S(1)}, u32[]{:S(2)}, u32[]{:S(2)}) collective-permute-start(bf16[96,4096]{1,0:T(8,128)(2,1)S(1)} %slice.157), channel_id=1, source_target_pairs={{0,32},{32,64},{64,96},{96,0},{1,33},{33,65},{65,97},{97,1},{2,34}... | collective-permute-start | bytes 2359304 | tf_op jit(solution)/shard_map/ppermute | solution.py:25
  41.8 5.0 %collective-permute-start.5 = (bf16[96,4096]{1,0:T(8,128)(2,1)S(1)}, bf16[96,4096]{1,0:T(8,128)(2,1)S(1)}, u32[]{:S(2)}, u32[]{:S(2)}) collective-permute-start(bf16[96,4096]{1,0:T(8,128)(2,1)S(1)} %slice.158), channel_id=1, source_target_pairs={{0,96},{32,0},{64,32},{96,64},{1,97},{33,1},{65,33},{97,65},{2,98}... | collective-permute-start | bytes 2359304 | tf_op jit(solution)/shard_map/ppermute | solution.py:25
  46.8 4.2 %shard_map.93.refs_6_.refs_3_ = bf16[4096,192]{1,0:T(8,128)(2,1)S(1)} custom-call(bf16[192,4096]{1,0:T(8,128)(2,1)S(1)} %collective-permute-done.2.p_ref.refs_1_, bf16[256,768]{1,0:T(8,128)(2,1)S(1)} %copy-done.5, bf16[256,768]{1,0:T(8,128)(2,1)S(1)} %copy-done.7, bf16[256,256]{1,0:T(8,128)(2,1)S(1)} %copy-done.1), custom_call_target="tpu_custom_call" | custom-call | flops 10000000000 | bytes 1000000 | tf_op jit(solution)/shard_map/pallas_call | solution.py:108
  51.0 4.2 %shard_map.95.refs_8_.refs_5_ = bf16[4096,192]{1,0:T(8,128)(2,1)S(1)} custom-call(bf16[192,4096]{1,0:T(8,128)(2,1)S(1)} %collective-permute-done.4.p_ref.refs_3_, bf16[256,768]{1,0:T(8,128)(2,1)S(1)} %copy-done.5, bf16[256,768]{1,0:T(8,128)(2,1)S(1)} %copy-done.7, bf16[256,256]{1,0:T(8,128)(2,1)S(1)} %copy-done.1), custom_call_target="tpu_custom_call" | custom-call | flops 10000000000 | bytes 1000000 | tf_op jit(solution)/shard_map/pallas_call | solution.py:108
  55.2 5.6 %shard_map.96.refs_9_ = bf16[4096,192]{1,0:T(8,128)(2,1)S(1)} custom-call(bf16[192,4096]{1,0:T(8,128)(2,1)} %collective-permute-done.p_ref.refs_4_.refs_0_, bf16[256,768]{1,0:T(8,128)(2,1)S(1)} %copy-done.5, bf16[256,768]{1,0:T(8,128)(2,1)S(1)} %copy-done.7, bf16[256,256]{1,0:T(8,128)(2,1)S(1)} %copy-done.1), custom_call_target="tpu_custom_call" | custom-call | flops 10000000000 | bytes 1000000 | tf_op jit(solution)/shard_map/pallas_call | solution.py:108
  62.3 4.4 %shard_map.94.refs_7_.refs_4_ = bf16[4096,192]{1,0:T(8,128)(2,1)S(1)} custom-call(bf16[192,4096]{1,0:T(8,128)(2,1)S(1)} %constant_dynamic-update-slice_fusion.p_ref.refs_2_, bf16[256,768]{1,0:T(8,128)(2,1)S(1)} %copy-done.5, bf16[256,768]{1,0:T(8,128)(2,1)S(1)} %copy-done.7, bf16[256,256]{1,0:T(8,128)(2,1)S(1)} %copy-done.1), custom_call_target="tpu_custom_call" | custom-call | flops 10000000000 | bytes 1000000 | tf_op jit(solution)/shard_map/pallas_call | solution.py:108
  66.8 6.6 %shard_map.97.refs_6_ = f32[2,16,112,128]{3,2,1,0:T(8,128)S(1)} custom-call(s32[2]{0:T(128)S(1)} %pad_add_fusion.place_ref, bf16[192,4096]{1,0:T(8,128)(2,1)} %get-tuple-element.11.refs_0_, bf16[192,4096]{1,0:T(8,128)(2,1)S(1)} %collective-permute-done.2.p_ref.refs_1_, bf16[192,4096]{1,0:T(8,128)(2,1)S(1)} %constant_dynamic-update-slice_fusion.p_ref.refs_2_, ...), custom_call_target="tpu_custom_call" | custom-call | flops 10000000000 | bytes 1000000 | tf_op jit(solution)/shard_map/pallas_call | solution.py:154
  73.4 7.0 %collective-permute-done.1.refs_1_ = bf16[192,4096]{1,0:T(8,128)(2,1)} collective-permute-done((bf16[192,4096]{1,0:T(8,128)(2,1)}, bf16[192,4096]{1,0:T(8,128)(2,1)}, u32[]{:S(2)}, u32[]{:S(2)}) %collective-permute-start.1) | collective-permute-done | bytes 1572896 | tf_op jit(solution)/shard_map/ppermute | solution.py:191
  80.4 4.6 %shard_map.98 = f32[2,16,112,128]{3,2,1,0:T(8,128)S(1)} custom-call(s32[2]{0:T(128)S(1)} %pad_add_fusion.place_ref, bf16[192,4096]{1,0:T(8,128)(2,1)} %collective-permute-done.p_ref.refs_4_.refs_0_, bf16[192,4096]{1,0:T(8,128)(2,1)} %collective-permute-done.1.refs_1_, bf16[4096,192]{1,0:T(8,128)(2,1)S(1)} %copy-done.3, ...), custom_call_target="tpu_custom_call" | custom-call | flops 10000000000 | bytes 1000000 | tf_op jit(solution)/shard_map/pallas_call | solution.py:154
  85.0 5.2 %all_to_all.10 = f32[2,16,112,128]{3,2,1,0:T(8,128)S(1)} all-to-all(f32[2,16,112,128]{3,2,1,0:T(8,128)S(1)} %shard_map.98), channel_id=1, replica_groups=mesh['zl'=4,'x'=4,'y'=8,'zh'=2,'c'=2] {'c'}, dimensions={0} | all-to-all | bytes 3670016 | tf_op jit(solution)/shard_map/all_to_all | solution.py:212
  93.3 13.8 %all-to-all-start.1 = ((f16[16,112,128]{2,1,0:T(8,128)(2,1)}), f16[16,112,128]{2,1,0:T(8,128)(2,1)S(1)}, u32[]{:S(2)}, u32[]{:S(2)}) async-start(f16[16,112,128]{2,1,0:T(8,128)(2,1)} %concatenate.13), calls=%async_computation.1 | async-start | bytes 917504 | tf_op jit(solution)/shard_map/all_to_all | solution.py:178
  107.1 20.5 %all-to-all-done.1 = f16[16,112,128]{2,1,0:T(8,128)(2,1)S(1)} async-done(((f16[16,112,128]{2,1,0:T(8,128)(2,1)}), f16[16,112,128]{2,1,0:T(8,128)(2,1)S(1)}, u32[]{:S(2)}, u32[]{:S(2)}) %all-to-all-start.1) | async-done | bytes 458784 | tf_op jit(solution)/shard_map/all_to_all | solution.py:178
  128.3 4.2 %collective-permute-start.9 = (f32[4,6,192]{2,1,0:T(8,128)S(1)}, f32[4,6,192]{2,1,0:T(8,128)S(1)}, u32[]{:S(2)}, u32[]{:S(2)}) collective-permute-start(f32[4,6,192]{2,1,0:T(8,128)S(1)} %pad_maximum_fusion.1), channel_id=1, source_target_pairs={{128,384},{256,0},{129,385},{257,1},{130,386},{258,2},{131,387},{2... | collective-permute-start | bytes 55304 | tf_op jit(solution)/shard_map/ppermute | solution.py:217
  132.5 2.2 %collective-permute-start.8 = (f32[2,6,192]{2,1,0:T(8,128)S(1)}, f32[2,6,192]{2,1,0:T(8,128)S(1)}, u32[]{:S(2)}, u32[]{:S(2)}) collective-permute-start(f32[2,6,192]{2,1,0:T(8,128)S(1)} %pad_maximum_fusion.4), channel_id=1, source_target_pairs={{0,32},{32,64},{64,96},{96,0},{1,33},{33,65},{65,97},{97,1},{2,34}... | collective-permute-start | bytes 27656 | tf_op jit(solution)/shard_map/ppermute | solution.py:25
  134.7 4.9 %collective-permute-start.6 = (f32[2,6,192]{2,1,0:T(8,128)S(1)}, f32[2,6,192]{2,1,0:T(8,128)S(1)}, u32[]{:S(2)}, u32[]{:S(2)}) collective-permute-start(f32[2,6,192]{2,1,0:T(8,128)S(1)} %pad_maximum_fusion.2), channel_id=1, source_target_pairs={{0,96},{32,0},{64,32},{96,64},{1,97},{33,1},{65,33},{97,65},{2,98}... | collective-permute-start | bytes 27656 | tf_op jit(solution)/shard_map/ppermute | solution.py:25
  139.6 2.5 %collective-permute-start.7 = (f32[2,6,192]{2,1,0:T(8,128)S(1)}, f32[2,6,192]{2,1,0:T(8,128)S(1)}, u32[]{:S(2)}, u32[]{:S(2)}) collective-permute-start(f32[2,6,192]{2,1,0:T(8,128)S(1)} %pad_maximum_fusion.3), channel_id=1, source_target_pairs={{0,64},{32,96},{64,0},{96,32},{1,65},{33,97},{65,1},{97,33},{2,66}... | collective-permute-start | bytes 27656 | tf_op jit(solution)/shard_map/ppermute | solution.py:25
  142.2 4.6 %collective-permute-done.7 = f32[2,6,192]{2,1,0:T(8,128)S(1)} collective-permute-done((f32[2,6,192]{2,1,0:T(8,128)S(1)}, f32[2,6,192]{2,1,0:T(8,128)S(1)}, u32[]{:S(2)}, u32[]{:S(2)}) %collective-permute-start.7) | collective-permute-done | bytes 9248 | tf_op jit(solution)/shard_map/ppermute | solution.py:25
  (56 shorter events, 9.1 us)
Async XLA Ops:
  0.0 39.4 %collective-permute-start.2 = (bf16[192,4096]{1,0:T(8,128)(2,1)}, bf16[192,4096]{1,0:T(8,128)(2,1)S(1)}, u32[]{:S(2)}, u32[]{:S(2)}) collective-permute-start(bf16[192,4096]{1,0:T(8,128)(2,1)} %bitcast.16), channel_id=1, source_target_pairs={{0,32},{32,64},{64,96},{96,0},{1,33},{33,65},{65,97},{97,1},{2,34}... | collective-permute-start | bytes 4718600 | tf_op jit(solution)/shard_map/ppermute | solution.py:25
  3.4 38.3 %collective-permute-start.4 = (bf16[192,4096]{1,0:T(8,128)(2,1)}, bf16[192,4096]{1,0:T(8,128)(2,1)S(1)}, u32[]{:S(2)}, u32[]{:S(2)}) collective-permute-start(bf16[192,4096]{1,0:T(8,128)(2,1)} %bitcast.17), channel_id=1, source_target_pairs={{0,96},{32,0},{64,32},{96,64},{1,97},{33,1},{65,33},{97,65},{2,98}... | collective-permute-start | bytes 4718600 | tf_op jit(solution)/shard_map/ppermute | solution.py:25
  7.1 48.2 %collective-permute-start = (bf16[192,4096]{1,0:T(8,128)(2,1)}, bf16[192,4096]{1,0:T(8,128)(2,1)}, u32[]{:S(2)}, u32[]{:S(2)}) collective-permute-start(bf16[192,4096]{1,0:T(8,128)(2,1)} %bitcast.18), channel_id=1, source_target_pairs={{0,256},{384,128},{128,0},{1,257},{385,129},{129,1},{2,258},{386,1... | collective-permute-start | bytes 4718600 | tf_op jit(solution)/shard_map/ppermute | solution.py:189
  14.0 3.1 %copy-start.1 = (bf16[256,256]{1,0:T(8,128)(2,1)S(1)}, bf16[256,256]{1,0:T(8,128)(2,1)}, u32[]{:S(2)}) copy-start(bf16[256,256]{1,0:T(8,128)(2,1)} %constant.51.clone.order_ref) | copy-start | bytes 393220
  17.1 1.4 copy-start
  18.5 1.0 copy-start.4
  19.5 1.0 copy-start.6
  25.9 1.3 copy-start.2
  27.2 53.2 %collective-permute-start.1 = (bf16[192,4096]{1,0:T(8,128)(2,1)}, bf16[192,4096]{1,0:T(8,128)(2,1)}, u32[]{:S(2)}, u32[]{:S(2)}) collective-permute-start(bf16[192,4096]{1,0:T(8,128)(2,1)} %get-tuple-element.11.refs_0_), channel_id=1, source_target_pairs={{0,384},{256,128},{384,256},{1,385},{257,129},{385,257},{2,386},{2... | collective-permute-start | bytes 4718600 | tf_op jit(solution)/shard_map/ppermute | solution.py:191
  28.6 18.2 %copy-start.5 = (bf16[256,768]{1,0:T(8,128)(2,1)S(1)}, bf16[256,768]{1,0:T(8,128)(2,1)}, u32[]{:S(2)}) copy-start(bf16[256,768]{1,0:T(8,128)(2,1)} %get-tuple-element.9.inner_ref) | copy-start | bytes 1179652
  28.6 18.3 %copy-start.7 = (bf16[256,768]{1,0:T(8,128)(2,1)S(1)}, bf16[256,768]{1,0:T(8,128)(2,1)}, u32[]{:S(2)}) copy-start(bf16[256,768]{1,0:T(8,128)(2,1)} %get-tuple-element.10.outer_ref) | copy-start | bytes 1179652
  39.5 21.5 %collective-permute-start.3 = (bf16[96,4096]{1,0:T(8,128)(2,1)S(1)}, bf16[96,4096]{1,0:T(8,128)(2,1)S(1)}, u32[]{:S(2)}, u32[]{:S(2)}) collective-permute-start(bf16[96,4096]{1,0:T(8,128)(2,1)S(1)} %slice.157), channel_id=1, source_target_pairs={{0,32},{32,64},{64,96},{96,0},{1,33},{33,65},{65,97},{97,1},{2,34}... | collective-permute-start | bytes 2359304 | tf_op jit(solution)/shard_map/ppermute | solution.py:25
  41.8 20.5 %collective-permute-start.5 = (bf16[96,4096]{1,0:T(8,128)(2,1)S(1)}, bf16[96,4096]{1,0:T(8,128)(2,1)S(1)}, u32[]{:S(2)}, u32[]{:S(2)}) collective-permute-start(bf16[96,4096]{1,0:T(8,128)(2,1)S(1)} %slice.158), channel_id=1, source_target_pairs={{0,96},{32,0},{64,32},{96,64},{1,97},{33,1},{65,33},{97,65},{2,98}... | collective-permute-start | bytes 2359304 | tf_op jit(solution)/shard_map/ppermute | solution.py:25
  62.3 4.5 %copy-start.3 = (bf16[4096,192]{1,0:T(8,128)(2,1)S(1)}, bf16[4096,192]{1,0:T(8,128)(2,1)}, u32[]{:S(2)}) copy-start(bf16[4096,192]{1,0:T(8,128)(2,1)} %copy-done.2) | copy-start | bytes 4718596
  93.3 34.4 %all-to-all-start.1 = ((f16[16,112,128]{2,1,0:T(8,128)(2,1)}), f16[16,112,128]{2,1,0:T(8,128)(2,1)S(1)}, u32[]{:S(2)}, u32[]{:S(2)}) async-start(f16[16,112,128]{2,1,0:T(8,128)(2,1)} %concatenate.13), calls=%async_computation.1 | async-start | bytes 917504 | tf_op jit(solution)/shard_map/all_to_all | solution.py:178
  128.3 18.5 %collective-permute-start.9 = (f32[4,6,192]{2,1,0:T(8,128)S(1)}, f32[4,6,192]{2,1,0:T(8,128)S(1)}, u32[]{:S(2)}, u32[]{:S(2)}) collective-permute-start(f32[4,6,192]{2,1,0:T(8,128)S(1)} %pad_maximum_fusion.1), channel_id=1, source_target_pairs={{128,384},{256,0},{129,385},{257,1},{130,386},{258,2},{131,387},{2... | collective-permute-start | bytes 55304 | tf_op jit(solution)/shard_map/ppermute | solution.py:217
  132.5 14.2 %collective-permute-start.8 = (f32[2,6,192]{2,1,0:T(8,128)S(1)}, f32[2,6,192]{2,1,0:T(8,128)S(1)}, u32[]{:S(2)}, u32[]{:S(2)}) collective-permute-start(f32[2,6,192]{2,1,0:T(8,128)S(1)} %pad_maximum_fusion.4), channel_id=1, source_target_pairs={{0,32},{32,64},{64,96},{96,0},{1,33},{33,65},{65,97},{97,1},{2,34}... | collective-permute-start | bytes 27656 | tf_op jit(solution)/shard_map/ppermute | solution.py:25
  134.7 7.4 %collective-permute-start.6 = (f32[2,6,192]{2,1,0:T(8,128)S(1)}, f32[2,6,192]{2,1,0:T(8,128)S(1)}, u32[]{:S(2)}, u32[]{:S(2)}) collective-permute-start(f32[2,6,192]{2,1,0:T(8,128)S(1)} %pad_maximum_fusion.2), channel_id=1, source_target_pairs={{0,96},{32,0},{64,32},{96,64},{1,97},{33,1},{65,33},{97,65},{2,98}... | collective-permute-start | bytes 27656 | tf_op jit(solution)/shard_map/ppermute | solution.py:25
  139.6 7.1 %collective-permute-start.7 = (f32[2,6,192]{2,1,0:T(8,128)S(1)}, f32[2,6,192]{2,1,0:T(8,128)S(1)}, u32[]{:S(2)}, u32[]{:S(2)}) collective-permute-start(f32[2,6,192]{2,1,0:T(8,128)S(1)} %pad_maximum_fusion.3), channel_id=1, source_target_pairs={{0,64},{32,96},{64,0},{96,32},{1,65},{33,97},{65,1},{97,33},{2,66}... | collective-permute-start | bytes 27656 | tf_op jit(solution)/shard_map/ppermute | solution.py:25

commit v5 on v3

--- a/solution.py
+++ b/solution.py
@@ -114,9 +114,9 @@
     )(rows, *tiles)
 
 
-def products_kernel(picks, n_p, n_w, first, place_ref, *refs):
+def products_kernel(picks, n_p, n_w, place_ref, *refs):
     p_refs, w_refs = refs[:n_p], refs[n_p : n_p + n_w]
-    given, (out_ref, total) = refs[n_p + n_w : -2], refs[-2:]
+    out_ref, total = refs[-2:]
 
     def score(slot, p, w):
         total[slot] = dot(p_refs[p][...], w_refs[w][...], NN)
@@ -128,40 +128,59 @@
             here = place_ref[axis]
             pl.when(here < least)(functools.partial(score, slot, *below))
             pl.when(here >= least)(functools.partial(score, slot, *reached))
-    if given:
-        out_ref[:, :, : first * PIECE] = given[0][:, :, : first * PIECE]
+    end = len(picks) * PIECE
+    left = out_ref.shape[2] - end
+    top = jnp.max(jnp.abs(total[...]))
+    out_ref[:, :, end:] = jnp.full((NC, NL, left, LANES), top, jnp.float32)
     for pair in range(len(picks) // 2):
         a, b = total[2 * pair], total[2 * pair + 1]
         rest = jnp.concatenate([a[:, LANES:], b[:, LANES:]], axis=1)
         for n, piece in enumerate((a[:, :LANES], b[:, :LANES], rest)):
-            to = first * PIECE + (3 * pair + n) * OWN
+            to = (3 * pair + n) * OWN
             for chip in range(NL):
                 for core in range(NC):
                     at = (chip * NC + core) * OWN
                     out_ref[core, chip, to : to + OWN] = piece[at : at + OWN]
 
 
-def products(plains, weights, picks, slots, first=0, sums=None):
+def products(plains, weights, picks):
     place = jnp.stack([lax.axis_index("zl"), lax.axis_index("x")]).astype(jnp.int32)
-    given = () if sums is None else (sums,)
     vmem = pl.BlockSpec(memory_space=pltpu.VMEM)
-    height = -(-slots * PIECE // 8) * 8
+    height = (len(picks) * PIECE // 8 + 1) * 8
     return pl.pallas_call(
-        functools.partial(products_kernel, picks, len(plains), len(weights), first),
+        functools.partial(products_kernel, picks, len(plains), len(weights)),
         out_shape=jax.ShapeDtypeStruct((NC, NL, height, LANES), jnp.float32),
-        in_specs=[pl.BlockSpec(memory_space=pltpu.SMEM)]
-        + [vmem] * (len(plains) + len(weights) + len(given)),
+        in_specs=[pl.BlockSpec(memory_space=pltpu.SMEM)] + [vmem] * (len(plains) + len(weights)),
         out_specs=vmem,
         scratch_shapes=[pltpu.VMEM((len(picks), ROWS, ROWS), jnp.float32)],
         compiler_params=pltpu.CompilerParams(vmem_limit_bytes=24 * 2**20),
         cost_estimate=COST,
-    )(place, *plains, *weights, *given)
+    )(place, *plains, *weights)
 
 
 def unpacked(part, slots):
     part = part[: slots * PIECE].reshape(slots // 2, 3, OWN, LANES)
     rest = part[:, 2].reshape(slots // 2, OWN, 2, ROWS - LANES).transpose(0, 2, 1, 3)
     return jnp.concatenate([part[:, :2], rest], axis=-1).reshape(slots, OWN, ROWS)
+
+
+def core_sum(sums, slots):
+    pair = lax.all_to_all(sums, "c", 0, 0, tiled=False)
+    end = slots * PIECE
+    bound = jnp.maximum(pair[0, :, end:] + pair[1, :, end:], 1e-30)
+    power = jnp.floor(jnp.log2(bound)) - 14
+    scaled = (pair[0, :, :end] + pair[1, :, :end]) * jnp.exp2(-power[:, :1])
+    return jnp.concatenate([scaled, power], axis=1).astype(jnp.float16)
+
+
+def chip_sum(got, slots):
+    end = slots * PIECE
+    got = got.astype(jnp.float32)
+    return unpacked((got[:, :end] * jnp.exp2(got[:, end : end + 1])).sum(0), slots)
+
+
+def turned(value, steps):
+    return lax.dynamic_slice_in_dim(jnp.concatenate([value, value]), steps, value.shape[0])
 
 
 def per_device(grads, in_factor, out_factor):
@@ -189,16 +208,15 @@
             (1, 3, (4, 3), (3, 4)),
             (None, 0, None, (0, 4)),
         ],
-        12,
-    )
-    sums = products(
-        [p4, p5], [w0, w1, w2, w3], [(0, 1, (0, r), (1, r)) for r in range(NX)], 12, 8, early
-    )
-    pair = lax.all_to_all(sums, "c", 0, 0, tiled=False)
-    part = pair[0] + pair[1]
-    part = lax.all_to_all(part, ("y", "zh"), 0, 0, tiled=False).sum(0)
-    slots = unpacked(part, 12)
-    row, two, again, following = slots[:3], slots[3:7], slots[7], slots[8:]
+    )
+    late = products([p4, p5], [w0, w1, w2, w3], [(0, 1, (0, r), (1, r)) for r in range(NX)])
+    early, late = core_sum(early, 8), core_sum(late, 4)
+    got = lax.all_to_all(
+        jnp.concatenate([early, late], axis=1), ("y", "zh"), 0, 0, tiled=False
+    )
+    slots = chip_sum(got[:, : early.shape[1]], 8)
+    row, two, again = slots[:3], slots[3:7], slots[7]
+    following = chip_sum(got[:, early.shape[1] :], 4)
     out = [None] * 9
     out[0], out[4] = row[0], following[0]
     across = lax.ppermute(
@@ -206,9 +224,12 @@
     )
     middle = (z == 1) | (z == 2)
     out[8] = jnp.where(middle, two[0], across[0])
+    other = [two[0]] + [jnp.where(x >= r, row[min(r, 2)], two[r]) for r in range(1, NX)]
+    sent = jnp.stack([following, jnp.stack(other)], axis=1)[::-1]
+    got = lax.all_to_all(turned(sent, (NX - 1 - x) % NX), "x", 0, 0, tiled=False)
+    got = turned(got, x)
     for r in range(1, NX):
-        same = row[r] if r < 3 else row[1]
-        back = moved(jnp.stack([following[r], jnp.where(x >= r, same, two[r])]), "x", -r)
+        back = got[r]
         inside = x + r < NX
         near = row[1] if r == 3 else back[1]
         far = jnp.where(middle, back[1], across[NX - r])

time: 158 us -> 145 us (0.918)
  the two profiles are of different devices: /device:TPU:64 before, /device:TPU:8 now
where the time goes in v5:
time: 145 us; the launch traced here: 144 us
  starting transfers between devices  46.1 us (32%)
  waiting for transfers between devices  41.9 us (29%)
  Pallas kernels  38 us (26%)
  blocking collectives  9.05 us (6%)
  local copies, waits for them, and re-layouts  6.78 us (5%)
  other arithmetic  1.8 us (1%)
    pallas_call x5, Pallas kernels, weigh(): pl.pallas_call(weigh_kernel, out_shape=(out, jax.ShapeDtypeStruct(rows.sh...  23.8 us
    all_to_all x1, waiting for transfers between devices, per_device(): lax.all_to_all(jnp.concatenate([early, late], axis=1), ('y', 'zh'), 0, 0,...  20.1 us
    ppermute x4, starting transfers between devices, moved(): lax.ppermute(value, axis, [(s, (s + steps) % count) for s in range(count)])  14.3 us
    all_to_all x1, starting transfers between devices, per_device(): lax.all_to_all(jnp.concatenate([early, late], axis=1), ('y', 'zh'), 0, 0,...  14.2 us
    pallas_call x2, Pallas kernels, products(): pl.pallas_call(functools.partial(products_kernel, picks, len(plains), len...  11.1 us
    all_to_all x2, blocking collectives, core_sum(): pair = lax.all_to_all(sums, 'c', 0, 0, tiled=False)  9.05 us
    ppermute x4, waiting for transfers between devices, moved(): lax.ppermute(value, axis, [(s, (s + steps) % count) for s in range(count)])  9.03 us
    ppermute x1, starting transfers between devices, per_device(): p4 = lax.ppermute(p0, 'zl', [(0, 2), (3, 1), (1, 0)])  6.09 us
  transfers between devices with their start and end apart: 9, of which 7 were waited for; matrix products, arithmetic and copies ran while one was open for 0% of the time, Pallas kernels for 23%

profile of v5, /device:TPU:8, one launch (start us, length us, event | category | flops | bytes accessed | tf_op | source)
XLA Modules:
  0.0 144.0 jit_solution(9589383376773596764)
XLA Ops:
  0.0 3.4 %collective-permute-start = (bf16[192,4096]{1,0:T(8,128)(2,1)}, bf16[192,4096]{1,0:T(8,128)(2,1)S(1)}, u32[]{:S(2)}, u32[]{:S(2)}) collective-permute-start(bf16[192,4096]{1,0:T(8,128)(2,1)} %bitcast.84), channel_id=1, source_target_pairs={{0,32},{32,64},{64,96},{96,0},{1,33},{33,65},{65,97},{97,1},{2,34}... | collective-permute-start | bytes 4718600 | tf_op jit(solution)/shard_map/ppermute | solution.py:25
  3.4 3.7 %collective-permute-start.2 = (bf16[192,4096]{1,0:T(8,128)(2,1)}, bf16[192,4096]{1,0:T(8,128)(2,1)S(1)}, u32[]{:S(2)}, u32[]{:S(2)}) collective-permute-start(bf16[192,4096]{1,0:T(8,128)(2,1)} %bitcast.85), channel_id=1, source_target_pairs={{0,96},{32,0},{64,32},{96,64},{1,97},{33,1},{65,33},{97,65},{2,98}... | collective-permute-start | bytes 4718600 | tf_op jit(solution)/shard_map/ppermute | solution.py:25
  7.1 6.1 %collective-permute-start.4 = (bf16[192,4096]{1,0:T(8,128)(2,1)}, bf16[192,4096]{1,0:T(8,128)(2,1)}, u32[]{:S(2)}, u32[]{:S(2)}) collective-permute-start(bf16[192,4096]{1,0:T(8,128)(2,1)} %bitcast.86), channel_id=1, source_target_pairs={{0,256},{384,128},{128,0},{1,257},{385,129},{129,1},{2,258},{386,1... | collective-permute-start | bytes 4718600 | tf_op jit(solution)/shard_map/ppermute | solution.py:193
  13.2 3.0 %shard_map.91 = (bf16[256,768]{1,0:T(8,128)(2,1)}, bf16[256,768]{1,0:T(8,128)(2,1)}) custom-call(f32[64,64]{1,0:T(8,128)} %bitcast.98, f32[64,64]{1,0:T(8,128)} %bitcast.99, f32[256,64]{1,0:T(8,128)} %constant.60.clone.four_ref, f32[256,64]{1,0:T(8,128)} %constant.61.clone.last_ref, f32[256,64]{1,0:T(8,128)} %constant.62.clone.mixed_ref, ...), custom_call_target="tpu_custom_call" | custom-call | flops 10000000000 | bytes 1000000 | tf_op jit(solution)/shard_map/pallas_call | solution.py:68
  16.2 1.4 copy-done
  19.6 5.4 %shard_map.92 = (bf16[4096,192]{1,0:T(8,128)(2,1)S(1)}, bf16[192,4096]{1,0:T(8,128)(2,1)}) custom-call(bf16[192,4096]{1,0:T(8,128)(2,1)S(1)} %bitcast.87, bf16[256,768]{1,0:T(8,128)(2,1)S(1)} %copy-done.4, bf16[256,768]{1,0:T(8,128)(2,1)S(1)} %copy-done.6, bf16[256,256]{1,0:T(8,128)(2,1)S(1)} %copy-done.1), custom_call_target="tpu_custom_call" | custom-call | flops 10000000000 | bytes 1000000 | tf_op jit(solution)/shard_map/pallas_call | solution.py:108
  26.3 5.3 %collective-permute-start.5 = (bf16[192,4096]{1,0:T(8,128)(2,1)}, bf16[192,4096]{1,0:T(8,128)(2,1)}, u32[]{:S(2)}, u32[]{:S(2)}) collective-permute-start(bf16[192,4096]{1,0:T(8,128)(2,1)} %get-tuple-element.11.refs_0_), channel_id=1, source_target_pairs={{0,384},{256,128},{384,256},{1,385},{257,129},{385,257},{2,386},{2... | collective-permute-start | bytes 4718600 | tf_op jit(solution)/shard_map/ppermute | solution.py:195
  31.8 7.7 %collective-permute-done.p_ref.refs_1_ = bf16[192,4096]{1,0:T(8,128)(2,1)S(1)} collective-permute-done((bf16[192,4096]{1,0:T(8,128)(2,1)}, bf16[192,4096]{1,0:T(8,128)(2,1)S(1)}, u32[]{:S(2)}, u32[]{:S(2)}) %collective-permute-start) | collective-permute-done | bytes 1572896 | tf_op jit(solution)/shard_map/ppermute | solution.py:25
  39.5 2.2 %collective-permute-start.1 = (bf16[96,4096]{1,0:T(8,128)(2,1)S(1)}, bf16[96,4096]{1,0:T(8,128)(2,1)S(1)}, u32[]{:S(2)}, u32[]{:S(2)}) collective-permute-start(bf16[96,4096]{1,0:T(8,128)(2,1)S(1)} %slice.201), channel_id=1, source_target_pairs={{0,32},{32,64},{64,96},{96,0},{1,33},{33,65},{65,97},{97,1},{2,34}... | collective-permute-start | bytes 2359304 | tf_op jit(solution)/shard_map/ppermute | solution.py:25
  41.8 5.0 %collective-permute-start.3 = (bf16[96,4096]{1,0:T(8,128)(2,1)S(1)}, bf16[96,4096]{1,0:T(8,128)(2,1)S(1)}, u32[]{:S(2)}, u32[]{:S(2)}) collective-permute-start(bf16[96,4096]{1,0:T(8,128)(2,1)S(1)} %slice.202), channel_id=1, source_target_pairs={{0,96},{32,0},{64,32},{96,64},{1,97},{33,1},{65,33},{97,65},{2,98}... | collective-permute-start | bytes 2359304 | tf_op jit(solution)/shard_map/ppermute | solution.py:25
  46.8 4.2 %shard_map.93.refs_6_.refs_3_ = bf16[4096,192]{1,0:T(8,128)(2,1)S(1)} custom-call(bf16[192,4096]{1,0:T(8,128)(2,1)S(1)} %collective-permute-done.p_ref.refs_1_, bf16[256,768]{1,0:T(8,128)(2,1)S(1)} %copy-done.5, bf16[256,768]{1,0:T(8,128)(2,1)S(1)} %copy-done.7, bf16[256,256]{1,0:T(8,128)(2,1)S(1)} %copy-done.1), custom_call_target="tpu_custom_call" | custom-call | flops 10000000000 | bytes 1000000 | tf_op jit(solution)/shard_map/pallas_call | solution.py:108
  51.0 4.2 %shard_map.95.refs_8_.refs_5_ = bf16[4096,192]{1,0:T(8,128)(2,1)S(1)} custom-call(bf16[192,4096]{1,0:T(8,128)(2,1)S(1)} %collective-permute-done.2.p_ref.refs_3_, bf16[256,768]{1,0:T(8,128)(2,1)S(1)} %copy-done.5, bf16[256,768]{1,0:T(8,128)(2,1)S(1)} %copy-done.7, bf16[256,256]{1,0:T(8,128)(2,1)S(1)} %copy-done.1), custom_call_target="tpu_custom_call" | custom-call | flops 10000000000 | bytes 1000000 | tf_op jit(solution)/shard_map/pallas_call | solution.py:108
  55.2 5.6 %shard_map.96.refs_9_ = bf16[4096,192]{1,0:T(8,128)(2,1)S(1)} custom-call(bf16[192,4096]{1,0:T(8,128)(2,1)} %collective-permute-done.4.p_ref.refs_4_.refs_0_, bf16[256,768]{1,0:T(8,128)(2,1)S(1)} %copy-done.5, bf16[256,768]{1,0:T(8,128)(2,1)S(1)} %copy-done.7, bf16[256,256]{1,0:T(8,128)(2,1)S(1)} %copy-done.1), custom_call_target="tpu_custom_call" | custom-call | flops 10000000000 | bytes 1000000 | tf_op jit(solution)/shard_map/pallas_call | solution.py:108
  62.3 4.4 %shard_map.94.refs_7_.refs_4_ = bf16[4096,192]{1,0:T(8,128)(2,1)S(1)} custom-call(bf16[192,4096]{1,0:T(8,128)(2,1)S(1)} %constant_dynamic-update-slice_fusion.p_ref.refs_2_, bf16[256,768]{1,0:T(8,128)(2,1)S(1)} %copy-done.5, bf16[256,768]{1,0:T(8,128)(2,1)S(1)} %copy-done.7, bf16[256,256]{1,0:T(8,128)(2,1)S(1)} %copy-done.1), custom_call_target="tpu_custom_call" | custom-call | flops 10000000000 | bytes 1000000 | tf_op jit(solution)/shard_map/pallas_call | solution.py:108
  66.8 6.6 %shard_map.97 = f32[2,16,80,128]{3,2,1,0:T(8,128)S(1)} custom-call(s32[2]{0:T(128)S(1)} %pad_add_fusion.place_ref, bf16[192,4096]{1,0:T(8,128)(2,1)} %get-tuple-element.11.refs_0_, bf16[192,4096]{1,0:T(8,128)(2,1)S(1)} %collective-permute-done.p_ref.refs_1_, bf16[192,4096]{1,0:T(8,128)(2,1)S(1)} %constant_dynamic-update-slice_fusion.p_ref.refs_2_, ...), custom_call_target="tpu_custom_call" | custom-call | flops 10000000000 | bytes 1000000 | tf_op jit(solution)/shard_map/pallas_call | solution.py:150
  73.4 4.8 %all_to_all.20 = f32[2,16,80,128]{3,2,1,0:T(8,128)S(1)} all-to-all(f32[2,16,80,128]{3,2,1,0:T(8,128)S(1)} %shard_map.97), channel_id=1, replica_groups=mesh['zl'=4,'x'=4,'y'=8,'zh'=2,'c'=2] {'c'}, dimensions={0} | all-to-all | bytes 2621440 | tf_op jit(solution)/shard_map/all_to_all | solution.py:168
  78.3 2.0 %collective-permute-done.5.refs_1_ = bf16[192,4096]{1,0:T(8,128)(2,1)} collective-permute-done((bf16[192,4096]{1,0:T(8,128)(2,1)}, bf16[192,4096]{1,0:T(8,128)(2,1)}, u32[]{:S(2)}, u32[]{:S(2)}) %collective-permute-start.5) | collective-permute-done | bytes 1572896 | tf_op jit(solution)/shard_map/ppermute | solution.py:195
  80.3 4.5 %shard_map.98 = f32[2,16,40,128]{3,2,1,0:T(8,128)S(1)} custom-call(s32[2]{0:T(128)S(1)} %pad_add_fusion.place_ref, bf16[192,4096]{1,0:T(8,128)(2,1)} %collective-permute-done.4.p_ref.refs_4_.refs_0_, bf16[192,4096]{1,0:T(8,128)(2,1)} %collective-permute-done.5.refs_1_, bf16[4096,192]{1,0:T(8,128)(2,1)S(1)} %copy-done.3, ...), custom_call_target="tpu_custom_call" | custom-call | flops 10000000000 | bytes 1000000 | tf_op jit(solution)/shard_map/pallas_call | solution.py:150
  84.8 4.3 %all_to_all.21 = f32[2,16,40,128]{3,2,1,0:T(8,128)S(1)} all-to-all(f32[2,16,40,128]{3,2,1,0:T(8,128)S(1)} %shard_map.98), channel_id=1, replica_groups=mesh['zl'=4,'x'=4,'y'=8,'zh'=2,'c'=2] {'c'}, dimensions={0} | all-to-all | bytes 1310720 | tf_op jit(solution)/shard_map/all_to_all | solution.py:168
  90.2 14.2 %all-to-all-start.2 = ((f16[16,120,128]{2,1,0:T(8,128)(2,1)}), f16[16,120,128]{2,1,0:T(8,128)(2,1)S(1)}, u32[]{:S(2)}, u32[]{:S(2)}) async-start(f16[16,120,128]{2,1,0:T(8,128)(2,1)} %pad_maximum_fusion), calls=%async_computation.2 | async-start | bytes 983040 | tf_op jit(solution)/shard_map/all_to_all | solution.py:214
  104.4 20.1 %all-to-all-done.2 = f16[16,120,128]{2,1,0:T(8,128)(2,1)S(1)} async-done(((f16[16,120,128]{2,1,0:T(8,128)(2,1)}), f16[16,120,128]{2,1,0:T(8,128)(2,1)S(1)}, u32[]{:S(2)}, u32[]{:S(2)}) %all-to-all-start.2) | async-done | bytes 491552 | tf_op jit(solution)/shard_map/all_to_all | solution.py:214
  126.5 5.2 %collective-permute-done.6 = f32[4,6,192]{2,0,1:T(4,128)S(1)} collective-permute-done((f32[4,6,192]{2,0,1:T(4,128)S(1)}, f32[4,6,192]{2,0,1:T(4,128)S(1)}, u32[]{:S(2)}, u32[]{:S(2)}) %collective-permute-start.6) | collective-permute-done | bytes 18464 | tf_op jit(solution)/shard_map/ppermute | solution.py:222
  132.7 4.8 %all-to-all-start.3 = ((f32[4,2,6,192]{3,1,2,0:T(2,128)}), f32[4,2,6,192]{3,1,2,0:T(2,128)S(1)}, u32[]{:S(2)}, u32[]{:S(2)}) async-start(f32[4,2,6,192]{3,1,2,0:T(2,128)} %copy.39), calls=%async_computation.3 | async-start | bytes 98304 | tf_op jit(solution)/shard_map/all_to_all | solution.py:229
  137.5 5.5 %all-to-all-done.3 = f32[4,2,6,192]{3,1,2,0:T(2,128)S(1)} async-done(((f32[4,2,6,192]{3,1,2,0:T(2,128)}), f32[4,2,6,192]{3,1,2,0:T(2,128)S(1)}, u32[]{:S(2)}, u32[]{:S(2)}) %all-to-all-start.3) | async-done | bytes 36896 | tf_op jit(solution)/shard_map/all_to_all | solution.py:229
  (71 shorter events, 9.8 us)
Async XLA Ops:
  0.0 39.4 %collective-permute-start = (bf16[192,4096]{1,0:T(8,128)(2,1)}, bf16[192,4096]{1,0:T(8,128)(2,1)S(1)}, u32[]{:S(2)}, u32[]{:S(2)}) collective-permute-start(bf16[192,4096]{1,0:T(8,128)(2,1)} %bitcast.84), channel_id=1, source_target_pairs={{0,32},{32,64},{64,96},{96,0},{1,33},{33,65},{65,97},{97,1},{2,34}... | collective-permute-start | bytes 4718600 | tf_op jit(solution)/shard_map/ppermute | solution.py:25
  3.4 38.3 %collective-permute-start.2 = (bf16[192,4096]{1,0:T(8,128)(2,1)}, bf16[192,4096]{1,0:T(8,128)(2,1)S(1)}, u32[]{:S(2)}, u32[]{:S(2)}) collective-permute-start(bf16[192,4096]{1,0:T(8,128)(2,1)} %bitcast.85), channel_id=1, source_target_pairs={{0,96},{32,0},{64,32},{96,64},{1,97},{33,1},{65,33},{97,65},{2,98}... | collective-permute-start | bytes 4718600 | tf_op jit(solution)/shard_map/ppermute | solution.py:25
  7.1 48.2 %collective-permute-start.4 = (bf16[192,4096]{1,0:T(8,128)(2,1)}, bf16[192,4096]{1,0:T(8,128)(2,1)}, u32[]{:S(2)}, u32[]{:S(2)}) collective-permute-start(bf16[192,4096]{1,0:T(8,128)(2,1)} %bitcast.86), channel_id=1, source_target_pairs={{0,256},{384,128},{128,0},{1,257},{385,129},{129,1},{2,258},{386,1... | collective-permute-start | bytes 4718600 | tf_op jit(solution)/shard_map/ppermute | solution.py:193
  13.2 3.1 %copy-start.1 = (bf16[256,256]{1,0:T(8,128)(2,1)S(1)}, bf16[256,256]{1,0:T(8,128)(2,1)}, u32[]{:S(2)}) copy-start(bf16[256,256]{1,0:T(8,128)(2,1)} %constant.65.clone.order_ref) | copy-start | bytes 393220
  16.2 1.4 copy-start
  17.6 1.0 copy-start.4
  18.6 1.0 copy-start.6
  25.0 1.3 copy-start.2
  26.3 53.9 %collective-permute-start.5 = (bf16[192,4096]{1,0:T(8,128)(2,1)}, bf16[192,4096]{1,0:T(8,128)(2,1)}, u32[]{:S(2)}, u32[]{:S(2)}) collective-permute-start(bf16[192,4096]{1,0:T(8,128)(2,1)} %get-tuple-element.11.refs_0_), channel_id=1, source_target_pairs={{0,384},{256,128},{384,256},{1,385},{257,129},{385,257},{2,386},{2... | collective-permute-start | bytes 4718600 | tf_op jit(solution)/shard_map/ppermute | solution.py:195
  31.8 15.1 %copy-start.5 = (bf16[256,768]{1,0:T(8,128)(2,1)S(1)}, bf16[256,768]{1,0:T(8,128)(2,1)}, u32[]{:S(2)}) copy-start(bf16[256,768]{1,0:T(8,128)(2,1)} %get-tuple-element.9.inner_ref) | copy-start | bytes 1179652
  31.8 15.1 %copy-start.7 = (bf16[256,768]{1,0:T(8,128)(2,1)S(1)}, bf16[256,768]{1,0:T(8,128)(2,1)}, u32[]{:S(2)}) copy-start(bf16[256,768]{1,0:T(8,128)(2,1)} %get-tuple-element.10.outer_ref) | copy-start | bytes 1179652
  39.5 21.5 %collective-permute-start.1 = (bf16[96,4096]{1,0:T(8,128)(2,1)S(1)}, bf16[96,4096]{1,0:T(8,128)(2,1)S(1)}, u32[]{:S(2)}, u32[]{:S(2)}) collective-permute-start(bf16[96,4096]{1,0:T(8,128)(2,1)S(1)} %slice.201), channel_id=1, source_target_pairs={{0,32},{32,64},{64,96},{96,0},{1,33},{33,65},{65,97},{97,1},{2,34}... | collective-permute-start | bytes 2359304 | tf_op jit(solution)/shard_map/ppermute | solution.py:25
  41.8 20.5 %collective-permute-start.3 = (bf16[96,4096]{1,0:T(8,128)(2,1)S(1)}, bf16[96,4096]{1,0:T(8,128)(2,1)S(1)}, u32[]{:S(2)}, u32[]{:S(2)}) collective-permute-start(bf16[96,4096]{1,0:T(8,128)(2,1)S(1)} %slice.202), channel_id=1, source_target_pairs={{0,96},{32,0},{64,32},{96,64},{1,97},{33,1},{65,33},{97,65},{2,98}... | collective-permute-start | bytes 2359304 | tf_op jit(solution)/shard_map/ppermute | solution.py:25
  62.3 4.5 %copy-start.3 = (bf16[4096,192]{1,0:T(8,128)(2,1)S(1)}, bf16[4096,192]{1,0:T(8,128)(2,1)}, u32[]{:S(2)}) copy-start(bf16[4096,192]{1,0:T(8,128)(2,1)} %copy-done.2) | copy-start | bytes 4718596
  90.2 34.3 %all-to-all-start.2 = ((f16[16,120,128]{2,1,0:T(8,128)(2,1)}), f16[16,120,128]{2,1,0:T(8,128)(2,1)S(1)}, u32[]{:S(2)}, u32[]{:S(2)}) async-start(f16[16,120,128]{2,1,0:T(8,128)(2,1)} %pad_maximum_fusion), calls=%async_computation.2 | async-start | bytes 983040 | tf_op jit(solution)/shard_map/all_to_all | solution.py:214
  125.1 6.6 %collective-permute-start.6 = (f32[4,6,192]{2,0,1:T(4,128)S(1)}, f32[4,6,192]{2,0,1:T(4,128)S(1)}, u32[]{:S(2)}, u32[]{:S(2)}) collective-permute-start(f32[4,6,192]{2,0,1:T(4,128)S(1)} %pad_maximum_fusion.4), channel_id=1, source_target_pairs={{128,384},{256,0},{129,385},{257,1},{130,386},{258,2},{131,387},{2... | collective-permute-start | bytes 55304 | tf_op jit(solution)/shard_map/ppermute | solution.py:222
  132.7 10.4 %all-to-all-start.3 = ((f32[4,2,6,192]{3,1,2,0:T(2,128)}), f32[4,2,6,192]{3,1,2,0:T(2,128)S(1)}, u32[]{:S(2)}, u32[]{:S(2)}) async-start(f32[4,2,6,192]{3,1,2,0:T(2,128)} %copy.39), calls=%async_computation.3 | async-start | bytes 98304 | tf_op jit(solution)/shard_map/all_to_all | solution.py:229

commit v6 on v3

--- a/solution.py
+++ b/solution.py
@@ -15,6 +15,7 @@
 OWN = ROWS // (NL * NC)
 LANES = 128
 PIECE = OWN * ROWS // LANES
+GROUP = 40
 TILE = 256
 NN, NT = ((1,), (0,)), ((1,), (1,))
 COST = pl.CostEstimate(flops=10**10, bytes_accessed=10**6, transcendentals=0)
@@ -114,9 +115,9 @@
     )(rows, *tiles)
 
 
-def products_kernel(picks, n_p, n_w, first, place_ref, *refs):
+def products_kernel(picks, groups, n_p, n_w, place_ref, *refs):
     p_refs, w_refs = refs[:n_p], refs[n_p : n_p + n_w]
-    given, (out_ref, total) = refs[n_p + n_w : -2], refs[-2:]
+    out_ref, total = refs[-2:]
 
     def score(slot, p, w):
         total[slot] = dot(p_refs[p][...], w_refs[w][...], NN)
@@ -128,40 +129,59 @@
             here = place_ref[axis]
             pl.when(here < least)(functools.partial(score, slot, *below))
             pl.when(here >= least)(functools.partial(score, slot, *reached))
-    if given:
-        out_ref[:, :, : first * PIECE] = given[0][:, :, : first * PIECE]
-    for pair in range(len(picks) // 2):
-        a, b = total[2 * pair], total[2 * pair + 1]
-        rest = jnp.concatenate([a[:, LANES:], b[:, LANES:]], axis=1)
-        for n, piece in enumerate((a[:, :LANES], b[:, :LANES], rest)):
-            to = first * PIECE + (3 * pair + n) * OWN
-            for chip in range(NL):
-                for core in range(NC):
-                    at = (chip * NC + core) * OWN
-                    out_ref[core, chip, to : to + OWN] = piece[at : at + OWN]
-
-
-def products(plains, weights, picks, slots, first=0, sums=None):
+    top = jnp.full((NC, NL, GROUP - 4 * PIECE, LANES), jnp.max(jnp.abs(total[...])), jnp.float32)
+    for group, slots in enumerate(groups):
+        start = group * GROUP
+        out_ref[:, :, start + 4 * PIECE : start + GROUP] = top
+        for pair in range(2):
+            a, b = total[slots[2 * pair]], total[slots[2 * pair + 1]]
+            rest = jnp.concatenate([a[:, LANES:], b[:, LANES:]], axis=1)
+            for n, piece in enumerate((a[:, :LANES], b[:, :LANES], rest)):
+                to = start + (3 * pair + n) * OWN
+                for chip in range(NL):
+                    for core in range(NC):
+                        at = (chip * NC + core) * OWN
+                        out_ref[core, chip, to : to + OWN] = piece[at : at + OWN]
+
+
+def products(plains, weights, picks, groups):
     place = jnp.stack([lax.axis_index("zl"), lax.axis_index("x")]).astype(jnp.int32)
-    given = () if sums is None else (sums,)
     vmem = pl.BlockSpec(memory_space=pltpu.VMEM)
-    height = -(-slots * PIECE // 8) * 8
+    height = len(groups) * GROUP
     return pl.pallas_call(
-        functools.partial(products_kernel, picks, len(plains), len(weights), first),
+        functools.partial(products_kernel, picks, groups, len(plains), len(weights)),
         out_shape=jax.ShapeDtypeStruct((NC, NL, height, LANES), jnp.float32),
-        in_specs=[pl.BlockSpec(memory_space=pltpu.SMEM)]
-        + [vmem] * (len(plains) + len(weights) + len(given)),
+        in_specs=[pl.BlockSpec(memory_space=pltpu.SMEM)] + [vmem] * (len(plains) + len(weights)),
         out_specs=vmem,
         scratch_shapes=[pltpu.VMEM((len(picks), ROWS, ROWS), jnp.float32)],
         compiler_params=pltpu.CompilerParams(vmem_limit_bytes=24 * 2**20),
         cost_estimate=COST,
-    )(place, *plains, *weights, *given)
-
-
-def unpacked(part, slots):
-    part = part[: slots * PIECE].reshape(slots // 2, 3, OWN, LANES)
-    rest = part[:, 2].reshape(slots // 2, OWN, 2, ROWS - LANES).transpose(0, 2, 1, 3)
-    return jnp.concatenate([part[:, :2], rest], axis=-1).reshape(slots, OWN, ROWS)
+    )(place, *plains, *weights)
+
+
+def core_sum(sums):
+    pair = lax.all_to_all(sums, "c", 0, 0, tiled=False)
+    pair = pair.reshape(NC, NL, -1, GROUP, LANES)
+    end = 4 * PIECE
+    bound = jnp.maximum(pair[0, :, :, end:] + pair[1, :, :, end:], 1e-30)
+    power = jnp.floor(jnp.log2(bound)) - 14
+    scaled = (pair[0, :, :, :end] + pair[1, :, :, :end]) * jnp.exp2(-power[:, :, :1])
+    return jnp.concatenate([scaled, power], axis=2).astype(jnp.float16)
+
+
+def chip_sum(sums):
+    n = sums.shape[1]
+    got = lax.all_to_all(sums.reshape(NY, NH * n * GROUP, LANES), "y", 0, 0, tiled=False)
+    got = got.astype(jnp.float32).reshape(NY, NH, n, GROUP, LANES)
+    end = 4 * PIECE
+    part = (got[..., :end, :] * jnp.exp2(got[..., end : end + 1, :])).sum(0)
+    part = part.reshape(NH, n, 2, 3, OWN, LANES)
+    rest = part[..., 2, :, :].reshape(NH, n, 2, OWN, 2, ROWS - LANES).swapaxes(3, 4)
+    return jnp.concatenate([part[..., :2, :, :], rest], axis=-1).reshape(NH, n, 4, OWN, ROWS)
+
+
+def turned(value, steps):
+    return lax.dynamic_slice_in_dim(jnp.concatenate([value, value]), steps, value.shape[0])
 
 
 def per_device(grads, in_factor, out_factor):
@@ -189,31 +209,46 @@
             (1, 3, (4, 3), (3, 4)),
             (None, 0, None, (0, 4)),
         ],
-        12,
-    )
-    sums = products(
-        [p4, p5], [w0, w1, w2, w3], [(0, 1, (0, r), (1, r)) for r in range(NX)], 12, 8, early
-    )
-    pair = lax.all_to_all(sums, "c", 0, 0, tiled=False)
-    part = pair[0] + pair[1]
-    part = lax.all_to_all(part, ("y", "zh"), 0, 0, tiled=False).sum(0)
-    slots = unpacked(part, 12)
-    row, two, again, following = slots[:3], slots[3:7], slots[7], slots[8:]
+        [(0, 1, 2, 2), (3, 4, 5, 6), (7, 4, 5, 6)],
+    )
+    late = products(
+        [p4, p5],
+        [w0, w1, w2, w3],
+        [(0, 1, (0, r), (1, r)) for r in range(NX)],
+        [tuple(range(NX))],
+    )
+    early = core_sum(early)
+    across = lax.ppermute(early[:, 2], "zl", [(1, 3), (2, 0)])
+    middle = (z == 1) | (z == 2)
+    two = jnp.where(middle, early[:, 1], across)
+    sums = jnp.concatenate([early[:, :1], two[:, None], core_sum(late)], axis=1)
+    sums = chip_sum(sums)
+    row, two, following = sums[:, 0], sums[:, 1], sums[:, 2]
+    own = [row[:, 0], jnp.where(x == 0, row[:, 1], two[:, 1]), two[:, 2], two[:, 3]]
+    sent = [
+        jnp.stack(
+            [
+                following[:, r],
+                jnp.where(x >= r, row[:, min(r, 2)], two[:, r]) if r else two[:, 0],
+                *own,
+            ],
+            axis=1,
+        )
+        for r in reversed(range(NX))
+    ]
+    sent = turned(jnp.stack(sent), (NX - 1 - x) % NX)
+    got = lax.all_to_all(
+        sent.reshape(NX * NH, 6 * OWN, ROWS), ("x", "zh"), 0, 0, tiled=False
+    )
+    got = turned(got.reshape(NX, NH, 6, OWN, ROWS).sum(1), x)
     out = [None] * 9
-    out[0], out[4] = row[0], following[0]
-    across = lax.ppermute(
-        jnp.concatenate([again[None], two[1:]]), "zl", [(1, 3), (2, 0)]
-    )
-    middle = (z == 1) | (z == 2)
-    out[8] = jnp.where(middle, two[0], across[0])
+    out[4], out[8], out[0] = got[0, 0], got[0, 1], got[0, 2]
     for r in range(1, NX):
-        same = row[r] if r < 3 else row[1]
-        back = moved(jnp.stack([following[r], jnp.where(x >= r, same, two[r])]), "x", -r)
         inside = x + r < NX
-        near = row[1] if r == 3 else back[1]
-        far = jnp.where(middle, back[1], across[NX - r])
-        out[r] = jnp.where(inside, near, back[0])
-        out[r + 4] = jnp.where(inside, back[0], far)
+        near = got[0, 3] if r == 3 else got[r, 1]
+        far = jnp.where(middle, got[r, 1], got[0, 6 - r])
+        out[r] = jnp.where(inside, near, got[r, 0])
+        out[r + 4] = jnp.where(inside, got[r, 0], far)
     return (jnp.stack(out) * factor).transpose(2, 0, 1)
 
 

time: 158 us -> 149 us (0.943)
  the two profiles are of different devices: /device:TPU:64 before, /device:TPU:65 now
where the time goes in v6:
time: 149 us; the launch traced here: 148 us
  waiting for transfers between devices  48.2 us (32%)
  starting transfers between devices  39.5 us (27%)
  Pallas kernels  38.1 us (26%)
  blocking collectives  12.2 us (8%)
  local copies, waits for them, and re-layouts  8.52 us (6%)
    pallas_call x5, Pallas kernels, weigh(): pl.pallas_call(weigh_kernel, out_shape=(out, jax.ShapeDtypeStruct(rows.sh...  23.8 us
    all_to_all x1, waiting for transfers between devices, chip_sum(): lax.all_to_all(sums.reshape(NY, NH * n * GROUP, LANES), 'y', 0, 0, tiled=...  17.3 us
    ppermute x4, waiting for transfers between devices, moved(): lax.ppermute(value, axis, [(s, (s + steps) % count) for s in range(count)])  16.2 us
    all_to_all x1, waiting for transfers between devices, per_device(): lax.all_to_all(sent.reshape(NX * NH, 6 * OWN, ROWS), ('x', 'zh'), 0, 0, t...  14.7 us
    ppermute x4, starting transfers between devices, moved(): lax.ppermute(value, axis, [(s, (s + steps) % count) for s in range(count)])  13.2 us
    all_to_all x2, blocking collectives, core_sum(): pair = lax.all_to_all(sums, 'c', 0, 0, tiled=False)  12.2 us
    pallas_call x2, Pallas kernels, products(): pl.pallas_call(functools.partial(products_kernel, picks, groups, len(plai...  11.2 us
    all_to_all x1, starting transfers between devices, per_device(): lax.all_to_all(sent.reshape(NX * NH, 6 * OWN, ROWS), ('x', 'zh'), 0, 0, t...  10.5 us
  transfers between devices with their start and end apart: 9, of which 4 were waited for; matrix products, arithmetic and copies ran while one was open for 1% of the time, Pallas kernels for 26%

profile of v6, /device:TPU:65, one launch (start us, length us, event | category | flops | bytes accessed | tf_op | source)
XLA Modules:
  0.0 148.3 jit_solution(16456351716042621719)
XLA Ops:
  0.0 3.1 %collective-permute-start = (bf16[192,4096]{1,0:T(8,128)(2,1)}, bf16[192,4096]{1,0:T(8,128)(2,1)S(1)}, u32[]{:S(2)}, u32[]{:S(2)}) collective-permute-start(bf16[192,4096]{1,0:T(8,128)(2,1)} %bitcast.139), channel_id=1, source_target_pairs={{0,32},{32,64},{64,96},{96,0},{1,33},{33,65},{65,97},{97,1},{2,34}... | collective-permute-start | bytes 4718600 | tf_op jit(solution)/shard_map/ppermute | solution.py:26
  3.1 3.4 %collective-permute-start.2 = (bf16[192,4096]{1,0:T(8,128)(2,1)}, bf16[192,4096]{1,0:T(8,128)(2,1)S(1)}, u32[]{:S(2)}, u32[]{:S(2)}) collective-permute-start(bf16[192,4096]{1,0:T(8,128)(2,1)} %bitcast.140), channel_id=1, source_target_pairs={{0,96},{32,0},{64,32},{96,64},{1,97},{33,1},{65,33},{97,65},{2,98}... | collective-permute-start | bytes 4718600 | tf_op jit(solution)/shard_map/ppermute | solution.py:26
  6.5 1.9 %collective-permute-start.4 = (bf16[192,4096]{1,0:T(8,128)(2,1)}, bf16[192,4096]{1,0:T(8,128)(2,1)}, u32[]{:S(2)}, u32[]{:S(2)}) collective-permute-start(bf16[192,4096]{1,0:T(8,128)(2,1)} %bitcast.141), channel_id=1, source_target_pairs={{0,256},{384,128},{128,0},{1,257},{385,129},{129,1},{2,258},{386,1... | collective-permute-start | bytes 4718600 | tf_op jit(solution)/shard_map/ppermute | solution.py:194
  8.4 3.1 %shard_map.91 = (bf16[256,768]{1,0:T(8,128)(2,1)}, bf16[256,768]{1,0:T(8,128)(2,1)}) custom-call(f32[64,64]{1,0:T(8,128)} %bitcast.155, f32[64,64]{1,0:T(8,128)} %bitcast.156, f32[256,64]{1,0:T(8,128)} %constant.62.clone.four_ref, f32[256,64]{1,0:T(8,128)} %constant.63.clone.last_ref, f32[256,64]{1,0:T(8,128)} %constant.64.clone.mixed_ref, ...), custom_call_target="tpu_custom_call" | custom-call | flops 10000000000 | bytes 1000000 | tf_op jit(solution)/shard_map/pallas_call | solution.py:69
  11.5 1.4 copy-done
  14.9 5.4 %shard_map.92 = (bf16[4096,192]{1,0:T(8,128)(2,1)S(1)}, bf16[192,4096]{1,0:T(8,128)(2,1)}) custom-call(bf16[192,4096]{1,0:T(8,128)(2,1)S(1)} %bitcast.142, bf16[256,768]{1,0:T(8,128)(2,1)S(1)} %copy-done.4, bf16[256,768]{1,0:T(8,128)(2,1)S(1)} %copy-done.6, bf16[256,256]{1,0:T(8,128)(2,1)S(1)} %copy-done.1), custom_call_target="tpu_custom_call" | custom-call | flops 10000000000 | bytes 1000000 | tf_op jit(solution)/shard_map/pallas_call | solution.py:109
  20.3 1.3 copy-done.2
  21.7 1.3 collective-permute-start.6
  23.0 15.5 %collective-permute-done.p_ref.refs_1_ = bf16[192,4096]{1,0:T(8,128)(2,1)S(1)} collective-permute-done((bf16[192,4096]{1,0:T(8,128)(2,1)}, bf16[192,4096]{1,0:T(8,128)(2,1)S(1)}, u32[]{:S(2)}, u32[]{:S(2)}) %collective-permute-start) | collective-permute-done | bytes 1572896 | tf_op jit(solution)/shard_map/ppermute | solution.py:26
  38.6 2.0 %collective-permute-start.1 = (bf16[96,4096]{1,0:T(8,128)(2,1)S(1)}, bf16[96,4096]{1,0:T(8,128)(2,1)S(1)}, u32[]{:S(2)}, u32[]{:S(2)}) collective-permute-start(bf16[96,4096]{1,0:T(8,128)(2,1)S(1)} %slice.198), channel_id=1, source_target_pairs={{0,32},{32,64},{64,96},{96,0},{1,33},{33,65},{65,97},{97,1},{2,34}... | collective-permute-start | bytes 2359304 | tf_op jit(solution)/shard_map/ppermute | solution.py:26
  40.7 4.7 %collective-permute-start.3 = (bf16[96,4096]{1,0:T(8,128)(2,1)S(1)}, bf16[96,4096]{1,0:T(8,128)(2,1)S(1)}, u32[]{:S(2)}, u32[]{:S(2)}) collective-permute-start(bf16[96,4096]{1,0:T(8,128)(2,1)S(1)} %slice.199), channel_id=1, source_target_pairs={{0,96},{32,0},{64,32},{96,64},{1,97},{33,1},{65,33},{97,65},{2,98}... | collective-permute-start | bytes 2359304 | tf_op jit(solution)/shard_map/ppermute | solution.py:26
  45.4 4.2 %shard_map.93.refs_6_.refs_3_ = bf16[4096,192]{1,0:T(8,128)(2,1)S(1)} custom-call(bf16[192,4096]{1,0:T(8,128)(2,1)S(1)} %collective-permute-done.p_ref.refs_1_, bf16[256,768]{1,0:T(8,128)(2,1)S(1)} %copy-done.5, bf16[256,768]{1,0:T(8,128)(2,1)S(1)} %copy-done.7, bf16[256,256]{1,0:T(8,128)(2,1)S(1)} %copy-done.1), custom_call_target="tpu_custom_call" | custom-call | flops 10000000000 | bytes 1000000 | tf_op jit(solution)/shard_map/pallas_call | solution.py:109
  49.6 4.2 %shard_map.95.refs_8_.refs_5_ = bf16[4096,192]{1,0:T(8,128)(2,1)S(1)} custom-call(bf16[192,4096]{1,0:T(8,128)(2,1)S(1)} %collective-permute-done.2.p_ref.refs_3_, bf16[256,768]{1,0:T(8,128)(2,1)S(1)} %copy-done.5, bf16[256,768]{1,0:T(8,128)(2,1)S(1)} %copy-done.7, bf16[256,256]{1,0:T(8,128)(2,1)S(1)} %copy-done.1), custom_call_target="tpu_custom_call" | custom-call | flops 10000000000 | bytes 1000000 | tf_op jit(solution)/shard_map/pallas_call | solution.py:109
  53.8 5.6 %shard_map.96.refs_9_ = bf16[4096,192]{1,0:T(8,128)(2,1)S(1)} custom-call(bf16[192,4096]{1,0:T(8,128)(2,1)} %collective-permute-done.4.p_ref.refs_4_.refs_0_, bf16[256,768]{1,0:T(8,128)(2,1)S(1)} %copy-done.5, bf16[256,768]{1,0:T(8,128)(2,1)S(1)} %copy-done.7, bf16[256,256]{1,0:T(8,128)(2,1)S(1)} %copy-done.1), custom_call_target="tpu_custom_call" | custom-call | flops 10000000000 | bytes 1000000 | tf_op jit(solution)/shard_map/pallas_call | solution.py:109
  60.3 4.4 %shard_map.94.refs_7_.refs_4_ = bf16[4096,192]{1,0:T(8,128)(2,1)S(1)} custom-call(bf16[192,4096]{1,0:T(8,128)(2,1)S(1)} %constant_dynamic-update-slice_fusion.p_ref.refs_2_, bf16[256,768]{1,0:T(8,128)(2,1)S(1)} %copy-done.5, bf16[256,768]{1,0:T(8,128)(2,1)S(1)} %copy-done.7, bf16[256,256]{1,0:T(8,128)(2,1)S(1)} %copy-done.1), custom_call_target="tpu_custom_call" | custom-call | flops 10000000000 | bytes 1000000 | tf_op jit(solution)/shard_map/pallas_call | solution.py:109
  64.7 6.7 %shard_map.97 = f32[2,16,120,128]{3,2,1,0:T(8,128)S(1)} custom-call(s32[2]{0:T(128)S(1)} %pad_add_fusion.place_ref, bf16[192,4096]{1,0:T(8,128)(2,1)} %get-tuple-element.11.refs_0_, bf16[192,4096]{1,0:T(8,128)(2,1)S(1)} %collective-permute-done.p_ref.refs_1_, bf16[192,4096]{1,0:T(8,128)(2,1)S(1)} %constant_dynamic-update-slice_fusion.p_ref.refs_2_, ...), custom_call_target="tpu_custom_call" | custom-call | flops 10000000000 | bytes 1000000 | tf_op jit(solution)/shard_map/pallas_call | solution.py:151
  71.4 7.7 %all_to_all.20 = f32[2,16,120,128]{3,2,1,0:T(8,128)S(1)} all-to-all(f32[2,16,120,128]{3,2,1,0:T(8,128)S(1)} %shard_map.97), channel_id=1, replica_groups=mesh['zl'=4,'x'=4,'y'=8,'zh'=2,'c'=2] {'c'}, dimensions={0} | all-to-all | bytes 3932160 | tf_op jit(solution)/shard_map/all_to_all | solution.py:163
  79.7 5.8 %collective-permute-start.5 = (f16[16,40,128]{2,1,0:T(8,128)(2,1)S(1)}, f16[16,40,128]{2,1,0:T(8,128)(2,1)S(1)}, u32[]{:S(2)}, u32[]{:S(2)}) collective-permute-start(f16[16,40,128]{2,1,0:T(8,128)(2,1)S(1)} %get-tuple-element.24), channel_id=1, source_target_pairs={{128,384},{256,0},{129,385},{257,1},{130,386},{258,2},{131,387},{2... | collective-permute-start | bytes 491528 | tf_op jit(solution)/shard_map/ppermute | solution.py:221
  85.5 4.5 %shard_map.98 = f32[2,16,40,128]{3,2,1,0:T(8,128)S(1)} custom-call(s32[2]{0:T(128)S(1)} %pad_add_fusion.place_ref, bf16[192,4096]{1,0:T(8,128)(2,1)} %collective-permute-done.4.p_ref.refs_4_.refs_0_, bf16[192,4096]{1,0:T(8,128)(2,1)} %collective-permute-done.6.refs_1_, bf16[4096,192]{1,0:T(8,128)(2,1)S(1)} %copy-done.3, ...), custom_call_target="tpu_custom_call" | custom-call | flops 10000000000 | bytes 1000000 | tf_op jit(solution)/shard_map/pallas_call | solution.py:151
  90.0 4.5 %all_to_all.21 = f32[2,16,40,128]{3,2,1,0:T(8,128)S(1)} all-to-all(f32[2,16,40,128]{3,2,1,0:T(8,128)S(1)} %shard_map.98), channel_id=1, replica_groups=mesh['zl'=4,'x'=4,'y'=8,'zh'=2,'c'=2] {'c'}, dimensions={0} | all-to-all | bytes 1310720 | tf_op jit(solution)/shard_map/all_to_all | solution.py:163
  95.9 6.9 %all-to-all-start.2 = ((f16[8,240,128]{2,1,0:T(8,128)(2,1)}), f16[8,240,128]{2,1,0:T(8,128)(2,1)S(1)}, u32[]{:S(2)}, u32[]{:S(2)}) async-start(f16[8,240,128]{2,1,0:T(8,128)(2,1)} %bitcast.18), calls=%async_computation.2 | async-start | bytes 983040 | tf_op jit(solution)/shard_map/all_to_all | solution.py:174
  102.7 17.3 %all-to-all-done.2 = f16[8,240,128]{2,1,0:T(8,128)(2,1)S(1)} async-done(((f16[8,240,128]{2,1,0:T(8,128)(2,1)}), f16[8,240,128]{2,1,0:T(8,128)(2,1)S(1)}, u32[]{:S(2)}, u32[]{:S(2)}) %all-to-all-start.2) | async-done | bytes 491552 | tf_op jit(solution)/shard_map/all_to_all | solution.py:174
  122.1 10.5 %all-to-all-start.3 = ((f32[8,36,192]{2,1,0:T(8,128)}), f32[8,36,192]{2,1,0:T(8,128)S(1)}, u32[]{:S(2)}, u32[]{:S(2)}) async-start(f32[8,36,192]{2,1,0:T(8,128)} %copy.44), calls=%async_computation.3 | async-start | bytes 655360 | tf_op jit(solution)/shard_map/all_to_all | solution.py:240
  132.6 14.7 %all-to-all-done.3 = f32[8,36,192]{2,1,0:T(8,128)S(1)} async-done(((f32[8,36,192]{2,1,0:T(8,128)}), f32[8,36,192]{2,1,0:T(8,128)S(1)}, u32[]{:S(2)}, u32[]{:S(2)}) %all-to-all-start.3) | async-done | bytes 221216 | tf_op jit(solution)/shard_map/all_to_all | solution.py:240
  (75 shorter events, 7.8 us)
Async XLA Ops:
  0.0 38.6 %collective-permute-start = (bf16[192,4096]{1,0:T(8,128)(2,1)}, bf16[192,4096]{1,0:T(8,128)(2,1)S(1)}, u32[]{:S(2)}, u32[]{:S(2)}) collective-permute-start(bf16[192,4096]{1,0:T(8,128)(2,1)} %bitcast.139), channel_id=1, source_target_pairs={{0,32},{32,64},{64,96},{96,0},{1,33},{33,65},{65,97},{97,1},{2,34}... | collective-permute-start | bytes 4718600 | tf_op jit(solution)/shard_map/ppermute | solution.py:26
  3.1 37.5 %collective-permute-start.2 = (bf16[192,4096]{1,0:T(8,128)(2,1)}, bf16[192,4096]{1,0:T(8,128)(2,1)S(1)}, u32[]{:S(2)}, u32[]{:S(2)}) collective-permute-start(bf16[192,4096]{1,0:T(8,128)(2,1)} %bitcast.140), channel_id=1, source_target_pairs={{0,96},{32,0},{64,32},{96,64},{1,97},{33,1},{65,33},{97,65},{2,98}... | collective-permute-start | bytes 4718600 | tf_op jit(solution)/shard_map/ppermute | solution.py:26
  6.5 47.3 %collective-permute-start.4 = (bf16[192,4096]{1,0:T(8,128)(2,1)}, bf16[192,4096]{1,0:T(8,128)(2,1)}, u32[]{:S(2)}, u32[]{:S(2)}) collective-permute-start(bf16[192,4096]{1,0:T(8,128)(2,1)} %bitcast.141), channel_id=1, source_target_pairs={{0,256},{384,128},{128,0},{1,257},{385,129},{129,1},{2,258},{386,1... | collective-permute-start | bytes 4718600 | tf_op jit(solution)/shard_map/ppermute | solution.py:194
  8.4 3.1 %copy-start.1 = (bf16[256,256]{1,0:T(8,128)(2,1)S(1)}, bf16[256,256]{1,0:T(8,128)(2,1)}, u32[]{:S(2)}) copy-start(bf16[256,256]{1,0:T(8,128)(2,1)} %constant.67.clone.order_ref) | copy-start | bytes 393220
  11.5 1.4 copy-start
  12.9 1.0 copy-start.4
  13.9 1.0 copy-start.6
  20.3 1.3 copy-start.2
  21.7 63.8 %collective-permute-start.6 = (bf16[192,4096]{1,0:T(8,128)(2,1)}, bf16[192,4096]{1,0:T(8,128)(2,1)}, u32[]{:S(2)}, u32[]{:S(2)}) collective-permute-start(bf16[192,4096]{1,0:T(8,128)(2,1)} %get-tuple-element.11.refs_0_), channel_id=1, source_target_pairs={{0,384},{256,128},{384,256},{1,385},{257,129},{385,257},{2,386},{2... | collective-permute-start | bytes 4718600 | tf_op jit(solution)/shard_map/ppermute | solution.py:196
  23.0 22.4 %copy-start.5 = (bf16[256,768]{1,0:T(8,128)(2,1)S(1)}, bf16[256,768]{1,0:T(8,128)(2,1)}, u32[]{:S(2)}) copy-start(bf16[256,768]{1,0:T(8,128)(2,1)} %get-tuple-element.9.inner_ref) | copy-start | bytes 1179652
  23.0 22.4 %copy-start.7 = (bf16[256,768]{1,0:T(8,128)(2,1)S(1)}, bf16[256,768]{1,0:T(8,128)(2,1)}, u32[]{:S(2)}) copy-start(bf16[256,768]{1,0:T(8,128)(2,1)} %get-tuple-element.10.outer_ref) | copy-start | bytes 1179652
  38.6 20.8 %collective-permute-start.1 = (bf16[96,4096]{1,0:T(8,128)(2,1)S(1)}, bf16[96,4096]{1,0:T(8,128)(2,1)S(1)}, u32[]{:S(2)}, u32[]{:S(2)}) collective-permute-start(bf16[96,4096]{1,0:T(8,128)(2,1)S(1)} %slice.198), channel_id=1, source_target_pairs={{0,32},{32,64},{64,96},{96,0},{1,33},{33,65},{65,97},{97,1},{2,34}... | collective-permute-start | bytes 2359304 | tf_op jit(solution)/shard_map/ppermute | solution.py:26
  40.7 19.5 %collective-permute-start.3 = (bf16[96,4096]{1,0:T(8,128)(2,1)S(1)}, bf16[96,4096]{1,0:T(8,128)(2,1)S(1)}, u32[]{:S(2)}, u32[]{:S(2)}) collective-permute-start(bf16[96,4096]{1,0:T(8,128)(2,1)S(1)} %slice.199), channel_id=1, source_target_pairs={{0,96},{32,0},{64,32},{96,64},{1,97},{33,1},{65,33},{97,65},{2,98}... | collective-permute-start | bytes 2359304 | tf_op jit(solution)/shard_map/ppermute | solution.py:26
  60.2 4.5 %copy-start.3 = (bf16[4096,192]{1,0:T(8,128)(2,1)S(1)}, bf16[4096,192]{1,0:T(8,128)(2,1)}, u32[]{:S(2)}) copy-start(bf16[4096,192]{1,0:T(8,128)(2,1)} %copy-done.2) | copy-start | bytes 4718596
  79.7 15.0 %collective-permute-start.5 = (f16[16,40,128]{2,1,0:T(8,128)(2,1)S(1)}, f16[16,40,128]{2,1,0:T(8,128)(2,1)S(1)}, u32[]{:S(2)}, u32[]{:S(2)}) collective-permute-start(f16[16,40,128]{2,1,0:T(8,128)(2,1)S(1)} %get-tuple-element.24), channel_id=1, source_target_pairs={{128,384},{256,0},{129,385},{257,1},{130,386},{258,2},{131,387},{2... | collective-permute-start | bytes 491528 | tf_op jit(solution)/shard_map/ppermute | solution.py:221
  95.9 24.1 %all-to-all-start.2 = ((f16[8,240,128]{2,1,0:T(8,128)(2,1)}), f16[8,240,128]{2,1,0:T(8,128)(2,1)S(1)}, u32[]{:S(2)}, u32[]{:S(2)}) async-start(f16[8,240,128]{2,1,0:T(8,128)(2,1)} %bitcast.18), calls=%async_computation.2 | async-start | bytes 983040 | tf_op jit(solution)/shard_map/all_to_all | solution.py:174
  122.1 25.2 %all-to-all-start.3 = ((f32[8,36,192]{2,1,0:T(8,128)}), f32[8,36,192]{2,1,0:T(8,128)S(1)}, u32[]{:S(2)}, u32[]{:S(2)}) async-start(f32[8,36,192]{2,1,0:T(8,128)} %copy.44), calls=%async_computation.3 | async-start | bytes 655360 | tf_op jit(solution)/shard_map/all_to_all | solution.py:240

commit v7 on v6

--- a/solution.py
+++ b/solution.py
@@ -171,13 +171,14 @@
 
 def chip_sum(sums):
     n = sums.shape[1]
-    got = lax.all_to_all(sums.reshape(NY, NH * n * GROUP, LANES), "y", 0, 0, tiled=False)
-    got = got.astype(jnp.float32).reshape(NY, NH, n, GROUP, LANES)
+    sums = sums.reshape(NL, n * GROUP, LANES)
+    got = lax.all_to_all(sums, ("y", "zh"), 0, 0, tiled=False)
+    got = got.astype(jnp.float32).reshape(NL, n, GROUP, LANES)
     end = 4 * PIECE
     part = (got[..., :end, :] * jnp.exp2(got[..., end : end + 1, :])).sum(0)
-    part = part.reshape(NH, n, 2, 3, OWN, LANES)
-    rest = part[..., 2, :, :].reshape(NH, n, 2, OWN, 2, ROWS - LANES).swapaxes(3, 4)
-    return jnp.concatenate([part[..., :2, :, :], rest], axis=-1).reshape(NH, n, 4, OWN, ROWS)
+    part = part.reshape(n, 2, 3, OWN, LANES)
+    rest = part[:, :, 2].reshape(n, 2, OWN, 2, ROWS - LANES).swapaxes(2, 3)
+    return jnp.concatenate([part[:, :, :2], rest], axis=-1).reshape(n, 4, OWN, ROWS)
 
 
 def turned(value, steps):
@@ -222,31 +223,16 @@
     middle = (z == 1) | (z == 2)
     two = jnp.where(middle, early[:, 1], across)
     sums = jnp.concatenate([early[:, :1], two[:, None], core_sum(late)], axis=1)
-    sums = chip_sum(sums)
-    row, two, following = sums[:, 0], sums[:, 1], sums[:, 2]
-    own = [row[:, 0], jnp.where(x == 0, row[:, 1], two[:, 1]), two[:, 2], two[:, 3]]
-    sent = [
-        jnp.stack(
-            [
-                following[:, r],
-                jnp.where(x >= r, row[:, min(r, 2)], two[:, r]) if r else two[:, 0],
-                *own,
-            ],
-            axis=1,
-        )
-        for r in reversed(range(NX))
-    ]
-    sent = turned(jnp.stack(sent), (NX - 1 - x) % NX)
-    got = lax.all_to_all(
-        sent.reshape(NX * NH, 6 * OWN, ROWS), ("x", "zh"), 0, 0, tiled=False
-    )
-    got = turned(got.reshape(NX, NH, 6, OWN, ROWS).sum(1), x)
+    row, two, following = chip_sum(sums)
+    other = [two[0]] + [jnp.where(x >= r, row[min(r, 2)], two[r]) for r in range(1, NX)]
+    sent = turned(jnp.stack([following, jnp.stack(other)], axis=1)[::-1], (NX - 1 - x) % NX)
+    got = turned(lax.all_to_all(sent, "x", 0, 0, tiled=False), x)
     out = [None] * 9
-    out[4], out[8], out[0] = got[0, 0], got[0, 1], got[0, 2]
+    out[0], out[4], out[8] = row[0], following[0], two[0]
     for r in range(1, NX):
         inside = x + r < NX
-        near = got[0, 3] if r == 3 else got[r, 1]
-        far = jnp.where(middle, got[r, 1], got[0, 6 - r])
+        near = row[1] if r == 3 else got[r, 1]
+        far = jnp.where(middle, got[r, 1], two[NX - r])
         out[r] = jnp.where(inside, near, got[r, 0])
         out[r + 4] = jnp.where(inside, got[r, 0], far)
     return (jnp.stack(out) * factor).transpose(2, 0, 1)

time: 149 us -> 143 us (0.960)
  the two profiles are of different devices: /device:TPU:65 before, /device:TPU:64 now
where the time goes in v7:
time: 143 us
  starting transfers between devices  46.6 us (33%)
  waiting for transfers between devices  38.8 us (27%)
  Pallas kernels  38.1 us (27%)
  blocking collectives  9.57 us (7%)
  local copies, waits for them, and re-layouts  7.77 us (5%)
    pallas_call x5, Pallas kernels, weigh(): pl.pallas_call(weigh_kernel, out_shape=(out, jax.ShapeDtypeStruct(rows.sh...  23.8 us
    all_to_all x1, waiting for transfers between devices, chip_sum(): got = lax.all_to_all(sums, ('y', 'zh'), 0, 0, tiled=False)  21.1 us
    ppermute x4, starting transfers between devices, moved(): lax.ppermute(value, axis, [(s, (s + steps) % count) for s in range(count)])  14.3 us
    all_to_all x1, starting transfers between devices, chip_sum(): got = lax.all_to_all(sums, ('y', 'zh'), 0, 0, tiled=False)  13 us
    ppermute x4, waiting for transfers between devices, moved(): lax.ppermute(value, axis, [(s, (s + steps) % count) for s in range(count)])  12.2 us
    pallas_call x2, Pallas kernels, products(): pl.pallas_call(functools.partial(products_kernel, picks, groups, len(plai...  11.2 us
    all_to_all x2, blocking collectives, core_sum(): pair = lax.all_to_all(sums, 'c', 0, 0, tiled=False)  9.57 us
    ppermute x1, starting transfers between devices, per_device(): p4 = lax.ppermute(p0, 'zl', [(0, 2), (3, 1), (1, 0)])  6.94 us
  transfers between devices with their start and end apart: 9, of which 5 were waited for; matrix products, arithmetic and copies ran while one was open for 1% of the time, Pallas kernels for 27%

profile of v7, /device:TPU:64, one launch (start us, length us, event | category | flops | bytes accessed | tf_op | source)
XLA Modules:
  0.0 142.6 jit_solution(17964461396025882948)
XLA Ops:
  0.0 3.4 %collective-permute-start = (bf16[192,4096]{1,0:T(8,128)(2,1)}, bf16[192,4096]{1,0:T(8,128)(2,1)S(1)}, u32[]{:S(2)}, u32[]{:S(2)}) collective-permute-start(bf16[192,4096]{1,0:T(8,128)(2,1)} %bitcast.101), channel_id=1, source_target_pairs={{0,32},{32,64},{64,96},{96,0},{1,33},{33,65},{65,97},{97,1},{2,34}... | collective-permute-start | bytes 4718600 | tf_op jit(solution)/shard_map/ppermute | solution.py:26
  3.4 3.7 %collective-permute-start.2 = (bf16[192,4096]{1,0:T(8,128)(2,1)}, bf16[192,4096]{1,0:T(8,128)(2,1)S(1)}, u32[]{:S(2)}, u32[]{:S(2)}) collective-permute-start(bf16[192,4096]{1,0:T(8,128)(2,1)} %bitcast.102), channel_id=1, source_target_pairs={{0,96},{32,0},{64,32},{96,64},{1,97},{33,1},{65,33},{97,65},{2,98}... | collective-permute-start | bytes 4718600 | tf_op jit(solution)/shard_map/ppermute | solution.py:26
  7.1 6.9 %collective-permute-start.4 = (bf16[192,4096]{1,0:T(8,128)(2,1)}, bf16[192,4096]{1,0:T(8,128)(2,1)}, u32[]{:S(2)}, u32[]{:S(2)}) collective-permute-start(bf16[192,4096]{1,0:T(8,128)(2,1)} %bitcast.103), channel_id=1, source_target_pairs={{0,256},{384,128},{128,0},{1,257},{385,129},{129,1},{2,258},{386,1... | collective-permute-start | bytes 4718600 | tf_op jit(solution)/shard_map/ppermute | solution.py:195
  14.0 3.1 %shard_map.91 = (bf16[256,768]{1,0:T(8,128)(2,1)}, bf16[256,768]{1,0:T(8,128)(2,1)}) custom-call(f32[64,64]{1,0:T(8,128)} %bitcast.118, f32[64,64]{1,0:T(8,128)} %bitcast.119, f32[256,64]{1,0:T(8,128)} %constant.61.clone.four_ref, f32[256,64]{1,0:T(8,128)} %constant.62.clone.last_ref, f32[256,64]{1,0:T(8,128)} %constant.63.clone.mixed_ref, ...), custom_call_target="tpu_custom_call" | custom-call | flops 10000000000 | bytes 1000000 | tf_op jit(solution)/shard_map/pallas_call | solution.py:69
  17.1 1.4 copy-done
  20.5 5.4 %shard_map.92 = (bf16[4096,192]{1,0:T(8,128)(2,1)S(1)}, bf16[192,4096]{1,0:T(8,128)(2,1)}) custom-call(bf16[192,4096]{1,0:T(8,128)(2,1)S(1)} %bitcast.104, bf16[256,768]{1,0:T(8,128)(2,1)S(1)} %copy-done.4, bf16[256,768]{1,0:T(8,128)(2,1)S(1)} %copy-done.6, bf16[256,256]{1,0:T(8,128)(2,1)S(1)} %copy-done.1), custom_call_target="tpu_custom_call" | custom-call | flops 10000000000 | bytes 1000000 | tf_op jit(solution)/shard_map/pallas_call | solution.py:109
  25.9 1.3 copy-done.2
  27.2 1.3 collective-permute-start.6
  28.6 10.8 %collective-permute-done.p_ref.refs_1_ = bf16[192,4096]{1,0:T(8,128)(2,1)S(1)} collective-permute-done((bf16[192,4096]{1,0:T(8,128)(2,1)}, bf16[192,4096]{1,0:T(8,128)(2,1)S(1)}, u32[]{:S(2)}, u32[]{:S(2)}) %collective-permute-start) | collective-permute-done | bytes 1572896 | tf_op jit(solution)/shard_map/ppermute | solution.py:26
  39.5 2.2 %collective-permute-start.1 = (bf16[96,4096]{1,0:T(8,128)(2,1)S(1)}, bf16[96,4096]{1,0:T(8,128)(2,1)S(1)}, u32[]{:S(2)}, u32[]{:S(2)}) collective-permute-start(bf16[96,4096]{1,0:T(8,128)(2,1)S(1)} %slice.146), channel_id=1, source_target_pairs={{0,32},{32,64},{64,96},{96,0},{1,33},{33,65},{65,97},{97,1},{2,34}... | collective-permute-start | bytes 2359304 | tf_op jit(solution)/shard_map/ppermute | solution.py:26
  41.8 5.0 %collective-permute-start.3 = (bf16[96,4096]{1,0:T(8,128)(2,1)S(1)}, bf16[96,4096]{1,0:T(8,128)(2,1)S(1)}, u32[]{:S(2)}, u32[]{:S(2)}) collective-permute-start(bf16[96,4096]{1,0:T(8,128)(2,1)S(1)} %slice.147), channel_id=1, source_target_pairs={{0,96},{32,0},{64,32},{96,64},{1,97},{33,1},{65,33},{97,65},{2,98}... | collective-permute-start | bytes 2359304 | tf_op jit(solution)/shard_map/ppermute | solution.py:26
  46.8 4.2 %shard_map.93.refs_6_.refs_3_ = bf16[4096,192]{1,0:T(8,128)(2,1)S(1)} custom-call(bf16[192,4096]{1,0:T(8,128)(2,1)S(1)} %collective-permute-done.p_ref.refs_1_, bf16[256,768]{1,0:T(8,128)(2,1)S(1)} %copy-done.5, bf16[256,768]{1,0:T(8,128)(2,1)S(1)} %copy-done.7, bf16[256,256]{1,0:T(8,128)(2,1)S(1)} %copy-done.1), custom_call_target="tpu_custom_call" | custom-call | flops 10000000000 | bytes 1000000 | tf_op jit(solution)/shard_map/pallas_call | solution.py:109
  51.0 4.2 %shard_map.95.refs_8_.refs_5_ = bf16[4096,192]{1,0:T(8,128)(2,1)S(1)} custom-call(bf16[192,4096]{1,0:T(8,128)(2,1)S(1)} %collective-permute-done.2.p_ref.refs_3_, bf16[256,768]{1,0:T(8,128)(2,1)S(1)} %copy-done.5, bf16[256,768]{1,0:T(8,128)(2,1)S(1)} %copy-done.7, bf16[256,256]{1,0:T(8,128)(2,1)S(1)} %copy-done.1), custom_call_target="tpu_custom_call" | custom-call | flops 10000000000 | bytes 1000000 | tf_op jit(solution)/shard_map/pallas_call | solution.py:109
  55.2 5.6 %shard_map.96.refs_9_ = bf16[4096,192]{1,0:T(8,128)(2,1)S(1)} custom-call(bf16[192,4096]{1,0:T(8,128)(2,1)} %collective-permute-done.4.p_ref.refs_4_.refs_0_, bf16[256,768]{1,0:T(8,128)(2,1)S(1)} %copy-done.5, bf16[256,768]{1,0:T(8,128)(2,1)S(1)} %copy-done.7, bf16[256,256]{1,0:T(8,128)(2,1)S(1)} %copy-done.1), custom_call_target="tpu_custom_call" | custom-call | flops 10000000000 | bytes 1000000 | tf_op jit(solution)/shard_map/pallas_call | solution.py:109
  62.3 4.4 %shard_map.94.refs_7_.refs_4_ = bf16[4096,192]{1,0:T(8,128)(2,1)S(1)} custom-call(bf16[192,4096]{1,0:T(8,128)(2,1)S(1)} %constant_dynamic-update-slice_fusion.p_ref.refs_2_, bf16[256,768]{1,0:T(8,128)(2,1)S(1)} %copy-done.5, bf16[256,768]{1,0:T(8,128)(2,1)S(1)} %copy-done.7, bf16[256,256]{1,0:T(8,128)(2,1)S(1)} %copy-done.1), custom_call_target="tpu_custom_call" | custom-call | flops 10000000000 | bytes 1000000 | tf_op jit(solution)/shard_map/pallas_call | solution.py:109
  66.8 6.7 %shard_map.97 = f32[2,16,120,128]{3,2,1,0:T(8,128)S(1)} custom-call(s32[2]{0:T(128)S(1)} %pad_add_fusion.place_ref, bf16[192,4096]{1,0:T(8,128)(2,1)} %get-tuple-element.11.refs_0_, bf16[192,4096]{1,0:T(8,128)(2,1)S(1)} %collective-permute-done.p_ref.refs_1_, bf16[192,4096]{1,0:T(8,128)(2,1)S(1)} %constant_dynamic-update-slice_fusion.p_ref.refs_2_, ...), custom_call_target="tpu_custom_call" | custom-call | flops 10000000000 | bytes 1000000 | tf_op jit(solution)/shard_map/pallas_call | solution.py:151
  73.5 5.3 %all_to_all.20 = f32[2,16,120,128]{3,2,1,0:T(8,128)S(1)} all-to-all(f32[2,16,120,128]{3,2,1,0:T(8,128)S(1)} %shard_map.97), channel_id=1, replica_groups=mesh['zl'=4,'x'=4,'y'=8,'zh'=2,'c'=2] {'c'}, dimensions={0} | all-to-all | bytes 3932160 | tf_op jit(solution)/shard_map/all_to_all | solution.py:163
  79.4 6.1 %collective-permute-start.5 = (f16[16,40,128]{2,1,0:T(8,128)(2,1)S(1)}, f16[16,40,128]{2,1,0:T(8,128)(2,1)S(1)}, u32[]{:S(2)}, u32[]{:S(2)}) collective-permute-start(f16[16,40,128]{2,1,0:T(8,128)(2,1)S(1)} %get-tuple-element.22), channel_id=1, source_target_pairs={{128,384},{256,0},{129,385},{257,1},{130,386},{258,2},{131,387},{2... | collective-permute-start | bytes 491528 | tf_op jit(solution)/shard_map/ppermute | solution.py:222
  85.5 4.5 %shard_map.98 = f32[2,16,40,128]{3,2,1,0:T(8,128)S(1)} custom-call(s32[2]{0:T(128)S(1)} %pad_add_fusion.place_ref, bf16[192,4096]{1,0:T(8,128)(2,1)} %collective-permute-done.4.p_ref.refs_4_.refs_0_, bf16[192,4096]{1,0:T(8,128)(2,1)} %collective-permute-done.6.refs_1_, bf16[4096,192]{1,0:T(8,128)(2,1)S(1)} %copy-done.3, ...), custom_call_target="tpu_custom_call" | custom-call | flops 10000000000 | bytes 1000000 | tf_op jit(solution)/shard_map/pallas_call | solution.py:151
  90.0 4.3 %all_to_all.21 = f32[2,16,40,128]{3,2,1,0:T(8,128)S(1)} all-to-all(f32[2,16,40,128]{3,2,1,0:T(8,128)S(1)} %shard_map.98), channel_id=1, replica_groups=mesh['zl'=4,'x'=4,'y'=8,'zh'=2,'c'=2] {'c'}, dimensions={0} | all-to-all | bytes 1310720 | tf_op jit(solution)/shard_map/all_to_all | solution.py:163
  95.5 13.0 %all-to-all-start.2 = ((f16[16,120,128]{2,1,0:T(8,128)(2,1)}), f16[16,120,128]{2,1,0:T(8,128)(2,1)S(1)}, u32[]{:S(2)}, u32[]{:S(2)}) async-start(f16[16,120,128]{2,1,0:T(8,128)(2,1)} %bitcast.18), calls=%async_computation.2 | async-start | bytes 983040 | tf_op jit(solution)/shard_map/all_to_all | solution.py:175
  108.6 21.1 %all-to-all-done.2 = f16[16,120,128]{2,1,0:T(8,128)(2,1)S(1)} async-done(((f16[16,120,128]{2,1,0:T(8,128)(2,1)}), f16[16,120,128]{2,1,0:T(8,128)(2,1)S(1)}, u32[]{:S(2)}, u32[]{:S(2)}) %all-to-all-start.2) | async-done | bytes 491552 | tf_op jit(solution)/shard_map/all_to_all | solution.py:175
  131.1 5.0 %all-to-all-start.3 = ((f32[4,2,6,192]{3,1,2,0:T(2,128)}), f32[4,2,6,192]{3,1,2,0:T(2,128)S(1)}, u32[]{:S(2)}, u32[]{:S(2)}) async-start(f32[4,2,6,192]{3,1,2,0:T(2,128)} %copy.58), calls=%async_computation.3 | async-start | bytes 98304 | tf_op jit(solution)/shard_map/all_to_all | solution.py:229
  136.2 5.5 %all-to-all-done.3 = f32[4,2,6,192]{3,1,2,0:T(2,128)S(1)} async-done(((f32[4,2,6,192]{3,1,2,0:T(2,128)}), f32[4,2,6,192]{3,1,2,0:T(2,128)S(1)}, u32[]{:S(2)}, u32[]{:S(2)}) %all-to-all-start.3) | async-done | bytes 36896 | tf_op jit(solution)/shard_map/all_to_all | solution.py:229
  (65 shorter events, 7.7 us)
Async XLA Ops:
  0.0 39.4 %collective-permute-start = (bf16[192,4096]{1,0:T(8,128)(2,1)}, bf16[192,4096]{1,0:T(8,128)(2,1)S(1)}, u32[]{:S(2)}, u32[]{:S(2)}) collective-permute-start(bf16[192,4096]{1,0:T(8,128)(2,1)} %bitcast.101), channel_id=1, source_target_pairs={{0,32},{32,64},{64,96},{96,0},{1,33},{33,65},{65,97},{97,1},{2,34}... | collective-permute-start | bytes 4718600 | tf_op jit(solution)/shard_map/ppermute | solution.py:26
  3.4 38.3 %collective-permute-start.2 = (bf16[192,4096]{1,0:T(8,128)(2,1)}, bf16[192,4096]{1,0:T(8,128)(2,1)S(1)}, u32[]{:S(2)}, u32[]{:S(2)}) collective-permute-start(bf16[192,4096]{1,0:T(8,128)(2,1)} %bitcast.102), channel_id=1, source_target_pairs={{0,96},{32,0},{64,32},{96,64},{1,97},{33,1},{65,33},{97,65},{2,98}... | collective-permute-start | bytes 4718600 | tf_op jit(solution)/shard_map/ppermute | solution.py:26
  7.1 48.2 %collective-permute-start.4 = (bf16[192,4096]{1,0:T(8,128)(2,1)}, bf16[192,4096]{1,0:T(8,128)(2,1)}, u32[]{:S(2)}, u32[]{:S(2)}) collective-permute-start(bf16[192,4096]{1,0:T(8,128)(2,1)} %bitcast.103), channel_id=1, source_target_pairs={{0,256},{384,128},{128,0},{1,257},{385,129},{129,1},{2,258},{386,1... | collective-permute-start | bytes 4718600 | tf_op jit(solution)/shard_map/ppermute | solution.py:195
  14.0 3.1 %copy-start.1 = (bf16[256,256]{1,0:T(8,128)(2,1)S(1)}, bf16[256,256]{1,0:T(8,128)(2,1)}, u32[]{:S(2)}) copy-start(bf16[256,256]{1,0:T(8,128)(2,1)} %constant.66.clone.order_ref) | copy-start | bytes 393220
  17.1 1.4 copy-start
  18.5 1.0 copy-start.4
  19.5 1.0 copy-start.6
  25.9 1.3 copy-start.2
  27.2 58.3 %collective-permute-start.6 = (bf16[192,4096]{1,0:T(8,128)(2,1)}, bf16[192,4096]{1,0:T(8,128)(2,1)}, u32[]{:S(2)}, u32[]{:S(2)}) collective-permute-start(bf16[192,4096]{1,0:T(8,128)(2,1)} %get-tuple-element.11.refs_0_), channel_id=1, source_target_pairs={{0,384},{256,128},{384,256},{1,385},{257,129},{385,257},{2,386},{2... | collective-permute-start | bytes 4718600 | tf_op jit(solution)/shard_map/ppermute | solution.py:197
  28.6 18.2 %copy-start.5 = (bf16[256,768]{1,0:T(8,128)(2,1)S(1)}, bf16[256,768]{1,0:T(8,128)(2,1)}, u32[]{:S(2)}) copy-start(bf16[256,768]{1,0:T(8,128)(2,1)} %get-tuple-element.9.inner_ref) | copy-start | bytes 1179652
  28.6 18.2 %copy-start.7 = (bf16[256,768]{1,0:T(8,128)(2,1)S(1)}, bf16[256,768]{1,0:T(8,128)(2,1)}, u32[]{:S(2)}) copy-start(bf16[256,768]{1,0:T(8,128)(2,1)} %get-tuple-element.10.outer_ref) | copy-start | bytes 1179652
  39.5 21.5 %collective-permute-start.1 = (bf16[96,4096]{1,0:T(8,128)(2,1)S(1)}, bf16[96,4096]{1,0:T(8,128)(2,1)S(1)}, u32[]{:S(2)}, u32[]{:S(2)}) collective-permute-start(bf16[96,4096]{1,0:T(8,128)(2,1)S(1)} %slice.146), channel_id=1, source_target_pairs={{0,32},{32,64},{64,96},{96,0},{1,33},{33,65},{65,97},{97,1},{2,34}... | collective-permute-start | bytes 2359304 | tf_op jit(solution)/shard_map/ppermute | solution.py:26
  41.8 20.5 %collective-permute-start.3 = (bf16[96,4096]{1,0:T(8,128)(2,1)S(1)}, bf16[96,4096]{1,0:T(8,128)(2,1)S(1)}, u32[]{:S(2)}, u32[]{:S(2)}) collective-permute-start(bf16[96,4096]{1,0:T(8,128)(2,1)S(1)} %slice.147), channel_id=1, source_target_pairs={{0,96},{32,0},{64,32},{96,64},{1,97},{33,1},{65,33},{97,65},{2,98}... | collective-permute-start | bytes 2359304 | tf_op jit(solution)/shard_map/ppermute | solution.py:26
  62.3 4.5 %copy-start.3 = (bf16[4096,192]{1,0:T(8,128)(2,1)S(1)}, bf16[4096,192]{1,0:T(8,128)(2,1)}, u32[]{:S(2)}) copy-start(bf16[4096,192]{1,0:T(8,128)(2,1)} %copy-done.2) | copy-start | bytes 4718596
  79.4 15.0 %collective-permute-start.5 = (f16[16,40,128]{2,1,0:T(8,128)(2,1)S(1)}, f16[16,40,128]{2,1,0:T(8,128)(2,1)S(1)}, u32[]{:S(2)}, u32[]{:S(2)}) collective-permute-start(f16[16,40,128]{2,1,0:T(8,128)(2,1)S(1)} %get-tuple-element.22), channel_id=1, source_target_pairs={{128,384},{256,0},{129,385},{257,1},{130,386},{258,2},{131,387},{2... | collective-permute-start | bytes 491528 | tf_op jit(solution)/shard_map/ppermute | solution.py:222
  95.5 34.1 %all-to-all-start.2 = ((f16[16,120,128]{2,1,0:T(8,128)(2,1)}), f16[16,120,128]{2,1,0:T(8,128)(2,1)S(1)}, u32[]{:S(2)}, u32[]{:S(2)}) async-start(f16[16,120,128]{2,1,0:T(8,128)(2,1)} %bitcast.18), calls=%async_computation.2 | async-start | bytes 983040 | tf_op jit(solution)/shard_map/all_to_all | solution.py:175
  131.1 10.6 %all-to-all-start.3 = ((f32[4,2,6,192]{3,1,2,0:T(2,128)}), f32[4,2,6,192]{3,1,2,0:T(2,128)S(1)}, u32[]{:S(2)}, u32[]{:S(2)}) async-start(f32[4,2,6,192]{3,1,2,0:T(2,128)} %copy.58), calls=%async_computation.3 | async-start | bytes 98304 | tf_op jit(solution)/shard_map/all_to_all | solution.py:229

commit v8 on v7

--- a/solution.py
+++ b/solution.py
@@ -117,7 +117,11 @@
 
 def products_kernel(picks, groups, n_p, n_w, place_ref, *refs):
     p_refs, w_refs = refs[:n_p], refs[n_p : n_p + n_w]
-    out_ref, total = refs[-2:]
+    given, (out_ref, total) = refs[n_p + n_w : -2], refs[-2:]
+    first = 0
+    if given:
+        first = given[0].shape[2]
+        out_ref[:, :, :first] = given[0][...]
 
     def score(slot, p, w):
         total[slot] = dot(p_refs[p][...], w_refs[w][...], NN)
@@ -131,7 +135,7 @@
             pl.when(here >= least)(functools.partial(score, slot, *reached))
     top = jnp.full((NC, NL, GROUP - 4 * PIECE, LANES), jnp.max(jnp.abs(total[...])), jnp.float32)
     for group, slots in enumerate(groups):
-        start = group * GROUP
+        start = first + group * GROUP
         out_ref[:, :, start + 4 * PIECE : start + GROUP] = top
         for pair in range(2):
             a, b = total[slots[2 * pair]], total[slots[2 * pair + 1]]
@@ -144,19 +148,20 @@
                         out_ref[core, chip, to : to + OWN] = piece[at : at + OWN]
 
 
-def products(plains, weights, picks, groups):
+def products(plains, weights, picks, groups, sums=None):
     place = jnp.stack([lax.axis_index("zl"), lax.axis_index("x")]).astype(jnp.int32)
     vmem = pl.BlockSpec(memory_space=pltpu.VMEM)
-    height = len(groups) * GROUP
+    given = () if sums is None else (sums,)
+    height = sum(v.shape[2] for v in given) + len(groups) * GROUP
     return pl.pallas_call(
         functools.partial(products_kernel, picks, groups, len(plains), len(weights)),
         out_shape=jax.ShapeDtypeStruct((NC, NL, height, LANES), jnp.float32),
-        in_specs=[pl.BlockSpec(memory_space=pltpu.SMEM)] + [vmem] * (len(plains) + len(weights)),
+        in_specs=[pl.BlockSpec(memory_space=pltpu.SMEM)] + [vmem] * (len(plains) + len(weights) + len(given)),
         out_specs=vmem,
         scratch_shapes=[pltpu.VMEM((len(picks), ROWS, ROWS), jnp.float32)],
         compiler_params=pltpu.CompilerParams(vmem_limit_bytes=24 * 2**20),
         cost_estimate=COST,
-    )(place, *plains, *weights)
+    )(place, *plains, *weights, *given)
 
 
 def core_sum(sums):
@@ -210,23 +215,25 @@
             (1, 3, (4, 3), (3, 4)),
             (None, 0, None, (0, 4)),
         ],
-        [(0, 1, 2, 2), (3, 4, 5, 6), (7, 4, 5, 6)],
-    )
-    late = products(
+        [(0, 1, 2, 7), (3, 4, 5, 6)],
+    )
+    sums = products(
         [p4, p5],
         [w0, w1, w2, w3],
         [(0, 1, (0, r), (1, r)) for r in range(NX)],
         [tuple(range(NX))],
-    )
-    early = core_sum(early)
-    across = lax.ppermute(early[:, 2], "zl", [(1, 3), (2, 0)])
+        early,
+    )
+    row, two, following = chip_sum(core_sum(sums))
+    across = lax.ppermute(jnp.concatenate([row[3:], two[1:]]), "zl", [(1, 3), (2, 0)])
     middle = (z == 1) | (z == 2)
-    two = jnp.where(middle, early[:, 1], across)
-    sums = jnp.concatenate([early[:, :1], two[:, None], core_sum(late)], axis=1)
-    row, two, following = chip_sum(sums)
     other = [two[0]] + [jnp.where(x >= r, row[min(r, 2)], two[r]) for r in range(1, NX)]
     sent = turned(jnp.stack([following, jnp.stack(other)], axis=1)[::-1], (NX - 1 - x) % NX)
-    got = turned(lax.all_to_all(sent, "x", 0, 0, tiled=False), x)
+    sent, row, two, following = lax.optimization_barrier((sent, row, two, following))
+    got = lax.all_to_all(sent, "x", 0, 0, tiled=False)
+    got, across = lax.optimization_barrier((got, across))
+    got = turned(got, x)
+    two = jnp.where(middle, two, across)
     out = [None] * 9
     out[0], out[4], out[8] = row[0], following[0], two[0]
     for r in range(1, NX):

time: 143 us -> 140 us (0.979)
  the two profiles are of different devices: /device:TPU:64 before, /device:TPU:2 now
where the time goes in v8:
time: 140 us
  starting transfers between devices  43.5 us (31%)
  waiting for transfers between devices  43.3 us (31%)
  Pallas kernels  38.1 us (27%)
  local copies, waits for them, and re-layouts  7.01 us (5%)
  blocking collectives  5.31 us (4%)
  other arithmetic  1.8 us (1%)
    pallas_call x5, Pallas kernels, weigh(): pl.pallas_call(weigh_kernel, out_shape=(out, jax.ShapeDtypeStruct(rows.sh...  23.8 us
    all_to_all x1, waiting for transfers between devices, chip_sum(): got = lax.all_to_all(sums, ('y', 'zh'), 0, 0, tiled=False)  21.1 us
    ppermute x4, starting transfers between devices, moved(): lax.ppermute(value, axis, [(s, (s + steps) % count) for s in range(count)])  15.8 us
    all_to_all x1, starting transfers between devices, chip_sum(): got = lax.all_to_all(sums, ('y', 'zh'), 0, 0, tiled=False)  13.8 us
    pallas_call x2, Pallas kernels, products(): pl.pallas_call(functools.partial(products_kernel, picks, groups, len(plai...  11.3 us
    ppermute x4, waiting for transfers between devices, moved(): lax.ppermute(value, axis, [(s, (s + steps) % count) for s in range(count)])  11 us
    ppermute x1, waiting for transfers between devices, per_device(): p5 = lax.ppermute(own, 'zl', [(0, 3), (2, 1), (3, 2)])  5.94 us
    ppermute x1, starting transfers between devices, per_device(): p5 = lax.ppermute(own, 'zl', [(0, 3), (2, 1), (3, 2)])  5.39 us
  transfers between devices with their start and end apart: 9, of which 5 were waited for; matrix products, arithmetic and copies ran while one was open for 0% of the time, Pallas kernels for 24%

profile of v8, /device:TPU:2, one launch (start us, length us, event | category | flops | bytes accessed | tf_op | source)
XLA Modules:
  0.0 139.5 jit_solution(2838937357228236094)
XLA Ops:
  0.0 3.4 %collective-permute-start.2 = (bf16[192,4096]{1,0:T(8,128)(2,1)}, bf16[192,4096]{1,0:T(8,128)(2,1)S(1)}, u32[]{:S(2)}, u32[]{:S(2)}) collective-permute-start(bf16[192,4096]{1,0:T(8,128)(2,1)} %bitcast.76), channel_id=1, source_target_pairs={{0,32},{32,64},{64,96},{96,0},{1,33},{33,65},{65,97},{97,1},{2,34}... | collective-permute-start | bytes 4718600 | tf_op jit(solution)/shard_map/ppermute | solution.py:26
  3.4 6.3 %collective-permute-start.4 = (bf16[192,4096]{1,0:T(8,128)(2,1)}, bf16[192,4096]{1,0:T(8,128)(2,1)S(1)}, u32[]{:S(2)}, u32[]{:S(2)}) collective-permute-start(bf16[192,4096]{1,0:T(8,128)(2,1)} %bitcast.77), channel_id=1, source_target_pairs={{0,96},{32,0},{64,32},{96,64},{1,97},{33,1},{65,33},{97,65},{2,98}... | collective-permute-start | bytes 4718600 | tf_op jit(solution)/shard_map/ppermute | solution.py:26
  9.7 2.2 %collective-permute-start = (bf16[192,4096]{1,0:T(8,128)(2,1)}, bf16[192,4096]{1,0:T(8,128)(2,1)}, u32[]{:S(2)}, u32[]{:S(2)}) collective-permute-start(bf16[192,4096]{1,0:T(8,128)(2,1)} %bitcast.78), channel_id=1, source_target_pairs={{0,256},{384,128},{128,0},{1,257},{385,129},{129,1},{2,258},{386,1... | collective-permute-start | bytes 4718600 | tf_op jit(solution)/shard_map/ppermute | solution.py:200
  12.0 3.1 %shard_map.91 = (bf16[256,768]{1,0:T(8,128)(2,1)}, bf16[256,768]{1,0:T(8,128)(2,1)}) custom-call(f32[64,64]{1,0:T(8,128)} %bitcast.92, f32[64,64]{1,0:T(8,128)} %bitcast.93, f32[256,64]{1,0:T(8,128)} %constant.56.clone.four_ref, f32[256,64]{1,0:T(8,128)} %constant.57.clone.last_ref, f32[256,64]{1,0:T(8,128)} %constant.58.clone.mixed_ref, ...), custom_call_target="tpu_custom_call" | custom-call | flops 10000000000 | bytes 1000000 | tf_op jit(solution)/shard_map/pallas_call | solution.py:69
  15.0 1.4 %copy-done = bf16[1,192,4096]{2,1,0:T(8,128)(2,1)S(1)} copy-done((bf16[1,192,4096]{2,1,0:T(8,128)(2,1)S(1)}, bf16[1,192,4096]{2,1,0:T(8,128)(2,1)}, u32[]{:S(2)}) %copy-start) | copy-done | bytes 1572888
  18.4 5.4 %shard_map.92 = (bf16[4096,192]{1,0:T(8,128)(2,1)S(1)}, bf16[192,4096]{1,0:T(8,128)(2,1)}) custom-call(bf16[192,4096]{1,0:T(8,128)(2,1)S(1)} %bitcast.79, bf16[256,768]{1,0:T(8,128)(2,1)S(1)} %copy-done.4, bf16[256,768]{1,0:T(8,128)(2,1)S(1)} %copy-done.6, bf16[256,256]{1,0:T(8,128)(2,1)S(1)} %copy-done.1), custom_call_target="tpu_custom_call" | custom-call | flops 10000000000 | bytes 1000000 | tf_op jit(solution)/shard_map/pallas_call | solution.py:109
  23.8 1.3 copy-done.2
  25.2 5.4 %collective-permute-start.1 = (bf16[192,4096]{1,0:T(8,128)(2,1)}, bf16[192,4096]{1,0:T(8,128)(2,1)}, u32[]{:S(2)}, u32[]{:S(2)}) collective-permute-start(bf16[192,4096]{1,0:T(8,128)(2,1)} %get-tuple-element.17.refs_0_), channel_id=1, source_target_pairs={{0,384},{256,128},{384,256},{1,385},{257,129},{385,257},{2,386},{2... | collective-permute-start | bytes 4718600 | tf_op jit(solution)/shard_map/ppermute | solution.py:202
  30.6 7.6 %collective-permute-done.2.p_ref.refs_1_ = bf16[192,4096]{1,0:T(8,128)(2,1)S(1)} collective-permute-done((bf16[192,4096]{1,0:T(8,128)(2,1)}, bf16[192,4096]{1,0:T(8,128)(2,1)S(1)}, u32[]{:S(2)}, u32[]{:S(2)}) %collective-permute-start.2) | collective-permute-done | bytes 1572896 | tf_op jit(solution)/shard_map/ppermute | solution.py:26
  38.3 3.4 %collective-permute-start.3 = (bf16[96,4096]{1,0:T(8,128)(2,1)S(1)}, bf16[96,4096]{1,0:T(8,128)(2,1)S(1)}, u32[]{:S(2)}, u32[]{:S(2)}) collective-permute-start(bf16[96,4096]{1,0:T(8,128)(2,1)S(1)} %slice.137), channel_id=1, source_target_pairs={{0,32},{32,64},{64,96},{96,0},{1,33},{33,65},{65,97},{97,1},{2,34}... | collective-permute-start | bytes 2359304 | tf_op jit(solution)/shard_map/ppermute | solution.py:26
  41.8 2.6 %collective-permute-start.5 = (bf16[96,4096]{1,0:T(8,128)(2,1)S(1)}, bf16[96,4096]{1,0:T(8,128)(2,1)S(1)}, u32[]{:S(2)}, u32[]{:S(2)}) collective-permute-start(bf16[96,4096]{1,0:T(8,128)(2,1)S(1)} %slice.138), channel_id=1, source_target_pairs={{0,96},{32,0},{64,32},{96,64},{1,97},{33,1},{65,33},{97,65},{2,98}... | collective-permute-start | bytes 2359304 | tf_op jit(solution)/shard_map/ppermute | solution.py:26
  44.4 4.2 %shard_map.93.refs_6_.refs_3_ = bf16[4096,192]{1,0:T(8,128)(2,1)S(1)} custom-call(bf16[192,4096]{1,0:T(8,128)(2,1)S(1)} %collective-permute-done.2.p_ref.refs_1_, bf16[256,768]{1,0:T(8,128)(2,1)S(1)} %copy-done.5, bf16[256,768]{1,0:T(8,128)(2,1)S(1)} %copy-done.7, bf16[256,256]{1,0:T(8,128)(2,1)S(1)} %copy-done.1), custom_call_target="tpu_custom_call" | custom-call | flops 10000000000 | bytes 1000000 | tf_op jit(solution)/shard_map/pallas_call | solution.py:109
  48.6 4.2 %shard_map.95.refs_8_.refs_5_ = bf16[4096,192]{1,0:T(8,128)(2,1)S(1)} custom-call(bf16[192,4096]{1,0:T(8,128)(2,1)S(1)} %collective-permute-done.4.p_ref.refs_3_, bf16[256,768]{1,0:T(8,128)(2,1)S(1)} %copy-done.5, bf16[256,768]{1,0:T(8,128)(2,1)S(1)} %copy-done.7, bf16[256,256]{1,0:T(8,128)(2,1)S(1)} %copy-done.1), custom_call_target="tpu_custom_call" | custom-call | flops 10000000000 | bytes 1000000 | tf_op jit(solution)/shard_map/pallas_call | solution.py:109
  52.8 5.6 %shard_map.96.refs_9_ = bf16[4096,192]{1,0:T(8,128)(2,1)S(1)} custom-call(bf16[192,4096]{1,0:T(8,128)(2,1)} %collective-permute-done.p_ref.refs_4_.refs_0_, bf16[256,768]{1,0:T(8,128)(2,1)S(1)} %copy-done.5, bf16[256,768]{1,0:T(8,128)(2,1)S(1)} %copy-done.7, bf16[256,256]{1,0:T(8,128)(2,1)S(1)} %copy-done.1), custom_call_target="tpu_custom_call" | custom-call | flops 10000000000 | bytes 1000000 | tf_op jit(solution)/shard_map/pallas_call | solution.py:109
  58.5 3.4 %collective-permute-done.5 = bf16[96,4096]{1,0:T(8,128)(2,1)S(1)} collective-permute-done((bf16[96,4096]{1,0:T(8,128)(2,1)S(1)}, bf16[96,4096]{1,0:T(8,128)(2,1)S(1)}, u32[]{:S(2)}, u32[]{:S(2)}) %collective-permute-start.5) | collective-permute-done | bytes 786464 | tf_op jit(solution)/shard_map/ppermute | solution.py:26
  62.0 4.4 %shard_map.94.refs_7_.refs_4_ = bf16[4096,192]{1,0:T(8,128)(2,1)S(1)} custom-call(bf16[192,4096]{1,0:T(8,128)(2,1)S(1)} %constant_dynamic-update-slice_fusion.p_ref.refs_2_, bf16[256,768]{1,0:T(8,128)(2,1)S(1)} %copy-done.5, bf16[256,768]{1,0:T(8,128)(2,1)S(1)} %copy-done.7, bf16[256,256]{1,0:T(8,128)(2,1)S(1)} %copy-done.1), custom_call_target="tpu_custom_call" | custom-call | flops 10000000000 | bytes 1000000 | tf_op jit(solution)/shard_map/pallas_call | solution.py:109
  66.4 6.7 %shard_map.97.refs_6_ = f32[2,16,80,128]{3,2,1,0:T(8,128)S(1)} custom-call(s32[2]{0:T(128)S(1)} %pad_add_fusion.place_ref, bf16[192,4096]{1,0:T(8,128)(2,1)} %get-tuple-element.17.refs_0_, bf16[192,4096]{1,0:T(8,128)(2,1)S(1)} %collective-permute-done.2.p_ref.refs_1_, bf16[192,4096]{1,0:T(8,128)(2,1)S(1)} %constant_dynamic-update-slice_fusion.p_ref.refs_2_, ...), custom_call_target="tpu_custom_call" | custom-call | flops 10000000000 | bytes 1000000 | tf_op jit(solution)/shard_map/pallas_call | solution.py:156
  73.1 5.9 %collective-permute-done.1.refs_1_ = bf16[192,4096]{1,0:T(8,128)(2,1)} collective-permute-done((bf16[192,4096]{1,0:T(8,128)(2,1)}, bf16[192,4096]{1,0:T(8,128)(2,1)}, u32[]{:S(2)}, u32[]{:S(2)}) %collective-permute-start.1) | collective-permute-done | bytes 1572896 | tf_op jit(solution)/shard_map/ppermute | solution.py:202
  79.0 4.6 %shard_map.98 = f32[2,16,120,128]{3,2,1,0:T(8,128)S(1)} custom-call(s32[2]{0:T(128)S(1)} %pad_add_fusion.place_ref, bf16[192,4096]{1,0:T(8,128)(2,1)} %collective-permute-done.p_ref.refs_4_.refs_0_, bf16[192,4096]{1,0:T(8,128)(2,1)} %collective-permute-done.1.refs_1_, bf16[4096,192]{1,0:T(8,128)(2,1)S(1)} %copy-done.3, ...), custom_call_target="tpu_custom_call" | custom-call | flops 10000000000 | bytes 1000000 | tf_op jit(solution)/shard_map/pallas_call | solution.py:156
  83.6 5.3 %all_to_all.15 = f32[2,16,120,128]{3,2,1,0:T(8,128)S(1)} all-to-all(f32[2,16,120,128]{3,2,1,0:T(8,128)S(1)} %shard_map.98), channel_id=1, replica_groups=mesh['zl'=4,'x'=4,'y'=8,'zh'=2,'c'=2] {'c'}, dimensions={0} | all-to-all | bytes 3932160 | tf_op jit(solution)/shard_map/all_to_all | solution.py:168
  90.2 13.8 %all-to-all-start.1 = ((f16[16,120,128]{2,1,0:T(8,128)(2,1)}), f16[16,120,128]{2,1,0:T(8,128)(2,1)S(1)}, u32[]{:S(2)}, u32[]{:S(2)}) async-start(f16[16,120,128]{2,1,0:T(8,128)(2,1)} %bitcast.9), calls=%async_computation.1 | async-start | bytes 983040 | tf_op jit(solution)/shard_map/all_to_all | solution.py:180
  104.1 21.1 %all-to-all-done.1 = f16[16,120,128]{2,1,0:T(8,128)(2,1)S(1)} async-done(((f16[16,120,128]{2,1,0:T(8,128)(2,1)}), f16[16,120,128]{2,1,0:T(8,128)(2,1)S(1)}, u32[]{:S(2)}, u32[]{:S(2)}) %all-to-all-start.1) | async-done | bytes 491552 | tf_op jit(solution)/shard_map/all_to_all | solution.py:180
  127.0 5.0 %all-to-all-start.2 = ((f32[4,2,6,192]{3,1,2,0:T(2,128)}), f32[4,2,6,192]{3,1,2,0:T(2,128)S(1)}, u32[]{:S(2)}, u32[]{:S(2)}) async-start(f32[4,2,6,192]{3,1,2,0:T(2,128)} %copy.48), calls=%async_computation.2 | async-start | bytes 98304 | tf_op jit(solution)/shard_map/all_to_all | solution.py:233
  133.4 5.2 %collective-permute-done.6 = f32[4,6,192]{2,0,1:T(4,128)S(1)} collective-permute-done((f32[4,6,192]{2,0,1:T(4,128)S(1)}, f32[4,6,192]{2,0,1:T(4,128)S(1)}, u32[]{:S(2)}, u32[]{:S(2)}) %collective-permute-start.6) | collective-permute-done | bytes 18464 | tf_op jit(solution)/shard_map/ppermute | solution.py:228
  (66 shorter events, 7.4 us)
Async XLA Ops:
  0.0 38.2 %collective-permute-start.2 = (bf16[192,4096]{1,0:T(8,128)(2,1)}, bf16[192,4096]{1,0:T(8,128)(2,1)S(1)}, u32[]{:S(2)}, u32[]{:S(2)}) collective-permute-start(bf16[192,4096]{1,0:T(8,128)(2,1)} %bitcast.76), channel_id=1, source_target_pairs={{0,32},{32,64},{64,96},{96,0},{1,33},{33,65},{65,97},{97,1},{2,34}... | collective-permute-start | bytes 4718600 | tf_op jit(solution)/shard_map/ppermute | solution.py:26
  3.4 38.3 %collective-permute-start.4 = (bf16[192,4096]{1,0:T(8,128)(2,1)}, bf16[192,4096]{1,0:T(8,128)(2,1)S(1)}, u32[]{:S(2)}, u32[]{:S(2)}) collective-permute-start(bf16[192,4096]{1,0:T(8,128)(2,1)} %bitcast.77), channel_id=1, source_target_pairs={{0,96},{32,0},{64,32},{96,64},{1,97},{33,1},{65,33},{97,65},{2,98}... | collective-permute-start | bytes 4718600 | tf_op jit(solution)/shard_map/ppermute | solution.py:26
  9.7 43.1 %collective-permute-start = (bf16[192,4096]{1,0:T(8,128)(2,1)}, bf16[192,4096]{1,0:T(8,128)(2,1)}, u32[]{:S(2)}, u32[]{:S(2)}) collective-permute-start(bf16[192,4096]{1,0:T(8,128)(2,1)} %bitcast.78), channel_id=1, source_target_pairs={{0,256},{384,128},{128,0},{1,257},{385,129},{129,1},{2,258},{386,1... | collective-permute-start | bytes 4718600 | tf_op jit(solution)/shard_map/ppermute | solution.py:200
  12.0 3.1 %copy-start.1 = (bf16[256,256]{1,0:T(8,128)(2,1)S(1)}, bf16[256,256]{1,0:T(8,128)(2,1)}, u32[]{:S(2)}) copy-start(bf16[256,256]{1,0:T(8,128)(2,1)} %constant.61.clone.order_ref) | copy-start | bytes 393220
  15.0 1.4 %copy-start = (bf16[1,192,4096]{2,1,0:T(8,128)(2,1)S(1)}, bf16[1,192,4096]{2,1,0:T(8,128)(2,1)}, u32[]{:S(2)}) copy-start(bf16[1,192,4096]{2,1,0:T(8,128)(2,1)} %param.9) | copy-start | bytes 4718596
  16.4 1.0 copy-start.4
  17.4 1.0 copy-start.6
  23.8 1.3 copy-start.2
  25.2 53.9 %collective-permute-start.1 = (bf16[192,4096]{1,0:T(8,128)(2,1)}, bf16[192,4096]{1,0:T(8,128)(2,1)}, u32[]{:S(2)}, u32[]{:S(2)}) collective-permute-start(bf16[192,4096]{1,0:T(8,128)(2,1)} %get-tuple-element.17.refs_0_), channel_id=1, source_target_pairs={{0,384},{256,128},{384,256},{1,385},{257,129},{385,257},{2,386},{2... | collective-permute-start | bytes 4718600 | tf_op jit(solution)/shard_map/ppermute | solution.py:202
  30.6 13.8 %copy-start.5 = (bf16[256,768]{1,0:T(8,128)(2,1)S(1)}, bf16[256,768]{1,0:T(8,128)(2,1)}, u32[]{:S(2)}) copy-start(bf16[256,768]{1,0:T(8,128)(2,1)} %get-tuple-element.15.inner_ref) | copy-start | bytes 1179652
  30.6 13.8 %copy-start.7 = (bf16[256,768]{1,0:T(8,128)(2,1)S(1)}, bf16[256,768]{1,0:T(8,128)(2,1)}, u32[]{:S(2)}) copy-start(bf16[256,768]{1,0:T(8,128)(2,1)} %get-tuple-element.16.outer_ref) | copy-start | bytes 1179652
  38.3 20.1 %collective-permute-start.3 = (bf16[96,4096]{1,0:T(8,128)(2,1)S(1)}, bf16[96,4096]{1,0:T(8,128)(2,1)S(1)}, u32[]{:S(2)}, u32[]{:S(2)}) collective-permute-start(bf16[96,4096]{1,0:T(8,128)(2,1)S(1)} %slice.137), channel_id=1, source_target_pairs={{0,32},{32,64},{64,96},{96,0},{1,33},{33,65},{65,97},{97,1},{2,34}... | collective-permute-start | bytes 2359304 | tf_op jit(solution)/shard_map/ppermute | solution.py:26
  41.8 20.1 %collective-permute-start.5 = (bf16[96,4096]{1,0:T(8,128)(2,1)S(1)}, bf16[96,4096]{1,0:T(8,128)(2,1)S(1)}, u32[]{:S(2)}, u32[]{:S(2)}) collective-permute-start(bf16[96,4096]{1,0:T(8,128)(2,1)S(1)} %slice.138), channel_id=1, source_target_pairs={{0,96},{32,0},{64,32},{96,64},{1,97},{33,1},{65,33},{97,65},{2,98}... | collective-permute-start | bytes 2359304 | tf_op jit(solution)/shard_map/ppermute | solution.py:26
  62.0 4.5 %copy-start.3 = (bf16[4096,192]{1,0:T(8,128)(2,1)S(1)}, bf16[4096,192]{1,0:T(8,128)(2,1)}, u32[]{:S(2)}) copy-start(bf16[4096,192]{1,0:T(8,128)(2,1)} %copy-done.2) | copy-start | bytes 4718596
  90.2 35.0 %all-to-all-start.1 = ((f16[16,120,128]{2,1,0:T(8,128)(2,1)}), f16[16,120,128]{2,1,0:T(8,128)(2,1)S(1)}, u32[]{:S(2)}, u32[]{:S(2)}) async-start(f16[16,120,128]{2,1,0:T(8,128)(2,1)} %bitcast.9), calls=%async_computation.1 | async-start | bytes 983040 | tf_op jit(solution)/shard_map/all_to_all | solution.py:180
  127.0 11.6 %all-to-all-start.2 = ((f32[4,2,6,192]{3,1,2,0:T(2,128)}), f32[4,2,6,192]{3,1,2,0:T(2,128)S(1)}, u32[]{:S(2)}, u32[]{:S(2)}) async-start(f32[4,2,6,192]{3,1,2,0:T(2,128)} %copy.48), calls=%async_computation.2 | async-start | bytes 98304 | tf_op jit(solution)/shard_map/all_to_all | solution.py:233
  132.0 6.6 %collective-permute-start.6 = (f32[4,6,192]{2,0,1:T(4,128)S(1)}, f32[4,6,192]{2,0,1:T(4,128)S(1)}, u32[]{:S(2)}, u32[]{:S(2)}) collective-permute-start(f32[4,6,192]{2,0,1:T(4,128)S(1)} %pad_maximum_fusion.3), channel_id=1, source_target_pairs={{128,384},{256,0},{129,385},{257,1},{130,386},{258,2},{131,387},{2... | collective-permute-start | bytes 55304 | tf_op jit(solution)/shard_map/ppermute | solution.py:228

commit v9 on v7

--- a/solution.py
+++ b/solution.py
@@ -210,7 +210,7 @@
             (1, 3, (4, 3), (3, 4)),
             (None, 0, None, (0, 4)),
         ],
-        [(0, 1, 2, 2), (3, 4, 5, 6), (7, 4, 5, 6)],
+        [(0, 1, 2, 7), (3, 4, 5, 6)],
     )
     late = products(
         [p4, p5],
@@ -218,15 +218,17 @@
         [(0, 1, (0, r), (1, r)) for r in range(NX)],
         [tuple(range(NX))],
     )
-    early = core_sum(early)
-    across = lax.ppermute(early[:, 2], "zl", [(1, 3), (2, 0)])
+    sums = jnp.concatenate([core_sum(early), core_sum(late)], axis=1)
+    row, two, following = chip_sum(sums)
+    across = lax.ppermute(jnp.concatenate([row[3:], two[1:]]), "zl", [(1, 3), (2, 0)])
     middle = (z == 1) | (z == 2)
-    two = jnp.where(middle, early[:, 1], across)
-    sums = jnp.concatenate([early[:, :1], two[:, None], core_sum(late)], axis=1)
-    row, two, following = chip_sum(sums)
     other = [two[0]] + [jnp.where(x >= r, row[min(r, 2)], two[r]) for r in range(1, NX)]
     sent = turned(jnp.stack([following, jnp.stack(other)], axis=1)[::-1], (NX - 1 - x) % NX)
-    got = turned(lax.all_to_all(sent, "x", 0, 0, tiled=False), x)
+    sent, row, two, following = lax.optimization_barrier((sent, row, two, following))
+    got = lax.all_to_all(sent, "x", 0, 0, tiled=False)
+    got, across = lax.optimization_barrier((got, across))
+    got = turned(got, x)
+    two = jnp.where(middle, two, across)
     out = [None] * 9
     out[0], out[4], out[8] = row[0], following[0], two[0]
     for r in range(1, NX):

time: 143 us -> 141 us (0.986)
  the two profiles are of different devices: /device:TPU:64 before, /device:TPU:2 now
where the time goes in v9:
time: 141 us; the launch traced here: 140 us
  starting transfers between devices  45.3 us (32%)
  waiting for transfers between devices  38.3 us (27%)
  Pallas kernels  38.1 us (27%)
  blocking collectives  9.05 us (6%)
  local copies, waits for them, and re-layouts  6.92 us (5%)
  other arithmetic  1.97 us (1%)
    pallas_call x5, Pallas kernels, weigh(): pl.pallas_call(weigh_kernel, out_shape=(out, jax.ShapeDtypeStruct(rows.sh...  23.8 us
    all_to_all x1, waiting for transfers between devices, chip_sum(): got = lax.all_to_all(sums, ('y', 'zh'), 0, 0, tiled=False)  21.1 us
    ppermute x4, starting transfers between devices, moved(): lax.ppermute(value, axis, [(s, (s + steps) % count) for s in range(count)])  15.8 us
    all_to_all x1, starting transfers between devices, chip_sum(): got = lax.all_to_all(sums, ('y', 'zh'), 0, 0, tiled=False)  14.7 us
    pallas_call x2, Pallas kernels, products(): pl.pallas_call(functools.partial(products_kernel, picks, groups, len(plai...  11.2 us
    ppermute x4, waiting for transfers between devices, moved(): lax.ppermute(value, axis, [(s, (s + steps) % count) for s in range(count)])  11 us
    all_to_all x2, blocking collectives, core_sum(): pair = lax.all_to_all(sums, 'c', 0, 0, tiled=False)  9.05 us
    all_to_all x1, starting transfers between devices, per_device(): got = lax.all_to_all(sent, 'x', 0, 0, tiled=False)  5.92 us
  transfers between devices with their start and end apart: 9, of which 5 were waited for; matrix products, arithmetic and copies ran while one was open for 0% of the time, Pallas kernels for 24%

profile of v9, /device:TPU:2, one launch (start us, length us, event | category | flops | bytes accessed | tf_op | source)
XLA Modules:
  0.0 140.1 jit_solution(9907845392156368249)
XLA Ops:
  0.0 3.4 %collective-permute-start = (bf16[192,4096]{1,0:T(8,128)(2,1)}, bf16[192,4096]{1,0:T(8,128)(2,1)S(1)}, u32[]{:S(2)}, u32[]{:S(2)}) collective-permute-start(bf16[192,4096]{1,0:T(8,128)(2,1)} %bitcast.93), channel_id=1, source_target_pairs={{0,32},{32,64},{64,96},{96,0},{1,33},{33,65},{65,97},{97,1},{2,34}... | collective-permute-start | bytes 4718600 | tf_op jit(solution)/shard_map/ppermute | solution.py:26
  3.4 6.3 %collective-permute-start.2 = (bf16[192,4096]{1,0:T(8,128)(2,1)}, bf16[192,4096]{1,0:T(8,128)(2,1)S(1)}, u32[]{:S(2)}, u32[]{:S(2)}) collective-permute-start(bf16[192,4096]{1,0:T(8,128)(2,1)} %bitcast.94), channel_id=1, source_target_pairs={{0,96},{32,0},{64,32},{96,64},{1,97},{33,1},{65,33},{97,65},{2,98}... | collective-permute-start | bytes 4718600 | tf_op jit(solution)/shard_map/ppermute | solution.py:26
  9.7 2.2 %collective-permute-start.4 = (bf16[192,4096]{1,0:T(8,128)(2,1)}, bf16[192,4096]{1,0:T(8,128)(2,1)}, u32[]{:S(2)}, u32[]{:S(2)}) collective-permute-start(bf16[192,4096]{1,0:T(8,128)(2,1)} %bitcast.95), channel_id=1, source_target_pairs={{0,256},{384,128},{128,0},{1,257},{385,129},{129,1},{2,258},{386,1... | collective-permute-start | bytes 4718600 | tf_op jit(solution)/shard_map/ppermute | solution.py:195
  12.0 3.1 %shard_map.91 = (bf16[256,768]{1,0:T(8,128)(2,1)}, bf16[256,768]{1,0:T(8,128)(2,1)}) custom-call(f32[64,64]{1,0:T(8,128)} %bitcast.113, f32[64,64]{1,0:T(8,128)} %bitcast.114, f32[256,64]{1,0:T(8,128)} %constant.62.clone.four_ref, f32[256,64]{1,0:T(8,128)} %constant.63.clone.last_ref, f32[256,64]{1,0:T(8,128)} %constant.64.clone.mixed_ref, ...), custom_call_target="tpu_custom_call" | custom-call | flops 10000000000 | bytes 1000000 | tf_op jit(solution)/shard_map/pallas_call | solution.py:69
  15.0 1.4 %copy-done = bf16[1,192,4096]{2,1,0:T(8,128)(2,1)S(1)} copy-done((bf16[1,192,4096]{2,1,0:T(8,128)(2,1)S(1)}, bf16[1,192,4096]{2,1,0:T(8,128)(2,1)}, u32[]{:S(2)}) %copy-start) | copy-done | bytes 1572888
  18.4 5.4 %shard_map.92 = (bf16[4096,192]{1,0:T(8,128)(2,1)S(1)}, bf16[192,4096]{1,0:T(8,128)(2,1)}) custom-call(bf16[192,4096]{1,0:T(8,128)(2,1)S(1)} %bitcast.96, bf16[256,768]{1,0:T(8,128)(2,1)S(1)} %copy-done.4, bf16[256,768]{1,0:T(8,128)(2,1)S(1)} %copy-done.6, bf16[256,256]{1,0:T(8,128)(2,1)S(1)} %copy-done.1), custom_call_target="tpu_custom_call" | custom-call | flops 10000000000 | bytes 1000000 | tf_op jit(solution)/shard_map/pallas_call | solution.py:109
  23.8 1.3 copy-done.2
  25.2 5.4 %collective-permute-start.5 = (bf16[192,4096]{1,0:T(8,128)(2,1)}, bf16[192,4096]{1,0:T(8,128)(2,1)}, u32[]{:S(2)}, u32[]{:S(2)}) collective-permute-start(bf16[192,4096]{1,0:T(8,128)(2,1)} %get-tuple-element.17.refs_0_), channel_id=1, source_target_pairs={{0,384},{256,128},{384,256},{1,385},{257,129},{385,257},{2,386},{2... | collective-permute-start | bytes 4718600 | tf_op jit(solution)/shard_map/ppermute | solution.py:197
  30.6 7.6 %collective-permute-done.p_ref.refs_1_ = bf16[192,4096]{1,0:T(8,128)(2,1)S(1)} collective-permute-done((bf16[192,4096]{1,0:T(8,128)(2,1)}, bf16[192,4096]{1,0:T(8,128)(2,1)S(1)}, u32[]{:S(2)}, u32[]{:S(2)}) %collective-permute-start) | collective-permute-done | bytes 1572896 | tf_op jit(solution)/shard_map/ppermute | solution.py:26
  38.3 3.4 %collective-permute-start.1 = (bf16[96,4096]{1,0:T(8,128)(2,1)S(1)}, bf16[96,4096]{1,0:T(8,128)(2,1)S(1)}, u32[]{:S(2)}, u32[]{:S(2)}) collective-permute-start(bf16[96,4096]{1,0:T(8,128)(2,1)S(1)} %slice.157), channel_id=1, source_target_pairs={{0,32},{32,64},{64,96},{96,0},{1,33},{33,65},{65,97},{97,1},{2,34}... | collective-permute-start | bytes 2359304 | tf_op jit(solution)/shard_map/ppermute | solution.py:26
  41.8 2.6 %collective-permute-start.3 = (bf16[96,4096]{1,0:T(8,128)(2,1)S(1)}, bf16[96,4096]{1,0:T(8,128)(2,1)S(1)}, u32[]{:S(2)}, u32[]{:S(2)}) collective-permute-start(bf16[96,4096]{1,0:T(8,128)(2,1)S(1)} %slice.158), channel_id=1, source_target_pairs={{0,96},{32,0},{64,32},{96,64},{1,97},{33,1},{65,33},{97,65},{2,98}... | collective-permute-start | bytes 2359304 | tf_op jit(solution)/shard_map/ppermute | solution.py:26
  44.4 4.2 %shard_map.93.refs_6_.refs_3_ = bf16[4096,192]{1,0:T(8,128)(2,1)S(1)} custom-call(bf16[192,4096]{1,0:T(8,128)(2,1)S(1)} %collective-permute-done.p_ref.refs_1_, bf16[256,768]{1,0:T(8,128)(2,1)S(1)} %copy-done.5, bf16[256,768]{1,0:T(8,128)(2,1)S(1)} %copy-done.7, bf16[256,256]{1,0:T(8,128)(2,1)S(1)} %copy-done.1), custom_call_target="tpu_custom_call" | custom-call | flops 10000000000 | bytes 1000000 | tf_op jit(solution)/shard_map/pallas_call | solution.py:109
  48.6 4.2 %shard_map.95.refs_8_.refs_5_ = bf16[4096,192]{1,0:T(8,128)(2,1)S(1)} custom-call(bf16[192,4096]{1,0:T(8,128)(2,1)S(1)} %collective-permute-done.2.p_ref.refs_3_, bf16[256,768]{1,0:T(8,128)(2,1)S(1)} %copy-done.5, bf16[256,768]{1,0:T(8,128)(2,1)S(1)} %copy-done.7, bf16[256,256]{1,0:T(8,128)(2,1)S(1)} %copy-done.1), custom_call_target="tpu_custom_call" | custom-call | flops 10000000000 | bytes 1000000 | tf_op jit(solution)/shard_map/pallas_call | solution.py:109
  52.8 5.6 %shard_map.96.refs_9_ = bf16[4096,192]{1,0:T(8,128)(2,1)S(1)} custom-call(bf16[192,4096]{1,0:T(8,128)(2,1)} %collective-permute-done.4.p_ref.refs_4_.refs_0_, bf16[256,768]{1,0:T(8,128)(2,1)S(1)} %copy-done.5, bf16[256,768]{1,0:T(8,128)(2,1)S(1)} %copy-done.7, bf16[256,256]{1,0:T(8,128)(2,1)S(1)} %copy-done.1), custom_call_target="tpu_custom_call" | custom-call | flops 10000000000 | bytes 1000000 | tf_op jit(solution)/shard_map/pallas_call | solution.py:109
  58.5 3.4 %collective-permute-done.3 = bf16[96,4096]{1,0:T(8,128)(2,1)S(1)} collective-permute-done((bf16[96,4096]{1,0:T(8,128)(2,1)S(1)}, bf16[96,4096]{1,0:T(8,128)(2,1)S(1)}, u32[]{:S(2)}, u32[]{:S(2)}) %collective-permute-start.3) | collective-permute-done | bytes 786464 | tf_op jit(solution)/shard_map/ppermute | solution.py:26
  62.0 4.4 %shard_map.94.refs_7_.refs_4_ = bf16[4096,192]{1,0:T(8,128)(2,1)S(1)} custom-call(bf16[192,4096]{1,0:T(8,128)(2,1)S(1)} %constant_dynamic-update-slice_fusion.p_ref.refs_2_, bf16[256,768]{1,0:T(8,128)(2,1)S(1)} %copy-done.5, bf16[256,768]{1,0:T(8,128)(2,1)S(1)} %copy-done.7, bf16[256,256]{1,0:T(8,128)(2,1)S(1)} %copy-done.1), custom_call_target="tpu_custom_call" | custom-call | flops 10000000000 | bytes 1000000 | tf_op jit(solution)/shard_map/pallas_call | solution.py:109
  66.4 6.7 %shard_map.97 = f32[2,16,80,128]{3,2,1,0:T(8,128)S(1)} custom-call(s32[2]{0:T(128)S(1)} %pad_add_fusion.place_ref, bf16[192,4096]{1,0:T(8,128)(2,1)} %get-tuple-element.17.refs_0_, bf16[192,4096]{1,0:T(8,128)(2,1)S(1)} %collective-permute-done.p_ref.refs_1_, bf16[192,4096]{1,0:T(8,128)(2,1)S(1)} %constant_dynamic-update-slice_fusion.p_ref.refs_2_, ...), custom_call_target="tpu_custom_call" | custom-call | flops 10000000000 | bytes 1000000 | tf_op jit(solution)/shard_map/pallas_call | solution.py:151
  73.1 4.8 %all_to_all.20 = f32[2,16,80,128]{3,2,1,0:T(8,128)S(1)} all-to-all(f32[2,16,80,128]{3,2,1,0:T(8,128)S(1)} %shard_map.97), channel_id=1, replica_groups=mesh['zl'=4,'x'=4,'y'=8,'zh'=2,'c'=2] {'c'}, dimensions={0} | all-to-all | bytes 2621440 | tf_op jit(solution)/shard_map/all_to_all | solution.py:163
  79.0 4.5 %shard_map.98 = f32[2,16,40,128]{3,2,1,0:T(8,128)S(1)} custom-call(s32[2]{0:T(128)S(1)} %pad_add_fusion.place_ref, bf16[192,4096]{1,0:T(8,128)(2,1)} %collective-permute-done.4.p_ref.refs_4_.refs_0_, bf16[192,4096]{1,0:T(8,128)(2,1)} %collective-permute-done.5.refs_1_, bf16[4096,192]{1,0:T(8,128)(2,1)S(1)} %copy-done.3, ...), custom_call_target="tpu_custom_call" | custom-call | flops 10000000000 | bytes 1000000 | tf_op jit(solution)/shard_map/pallas_call | solution.py:151
  83.5 4.3 %all_to_all.21 = f32[2,16,40,128]{3,2,1,0:T(8,128)S(1)} all-to-all(f32[2,16,40,128]{3,2,1,0:T(8,128)S(1)} %shard_map.98), channel_id=1, replica_groups=mesh['zl'=4,'x'=4,'y'=8,'zh'=2,'c'=2] {'c'}, dimensions={0} | all-to-all | bytes 1310720 | tf_op jit(solution)/shard_map/all_to_all | solution.py:163
  89.0 14.7 %all-to-all-start.2 = ((f16[16,120,128]{2,1,0:T(8,128)(2,1)}), f16[16,120,128]{2,1,0:T(8,128)(2,1)S(1)}, u32[]{:S(2)}, u32[]{:S(2)}) async-start(f16[16,120,128]{2,1,0:T(8,128)(2,1)} %bitcast.16), calls=%async_computation.2 | async-start | bytes 983040 | tf_op jit(solution)/shard_map/all_to_all | solution.py:175
  103.7 21.1 %all-to-all-done.2 = f16[16,120,128]{2,1,0:T(8,128)(2,1)S(1)} async-done(((f16[16,120,128]{2,1,0:T(8,128)(2,1)}), f16[16,120,128]{2,1,0:T(8,128)(2,1)S(1)}, u32[]{:S(2)}, u32[]{:S(2)}) %all-to-all-start.2) | async-done | bytes 491552 | tf_op jit(solution)/shard_map/all_to_all | solution.py:175
  126.6 5.9 %all-to-all-start.3 = ((f32[4,2,6,192]{3,1,2,0:T(2,128)}), f32[4,2,6,192]{3,1,2,0:T(2,128)S(1)}, u32[]{:S(2)}, u32[]{:S(2)}) async-start(f32[4,2,6,192]{3,1,2,0:T(2,128)} %copy.40), calls=%async_computation.3 | async-start | bytes 98304 | tf_op jit(solution)/shard_map/all_to_all | solution.py:228
  133.9 5.2 %collective-permute-done.6 = f32[4,6,192]{2,0,1:T(4,128)S(1)} collective-permute-done((f32[4,6,192]{2,0,1:T(4,128)S(1)}, f32[4,6,192]{2,0,1:T(4,128)S(1)}, u32[]{:S(2)}, u32[]{:S(2)}) %collective-permute-start.6) | collective-permute-done | bytes 18464 | tf_op jit(solution)/shard_map/ppermute | solution.py:223
  (68 shorter events, 8.4 us)
Async XLA Ops:
  0.0 38.2 %collective-permute-start = (bf16[192,4096]{1,0:T(8,128)(2,1)}, bf16[192,4096]{1,0:T(8,128)(2,1)S(1)}, u32[]{:S(2)}, u32[]{:S(2)}) collective-permute-start(bf16[192,4096]{1,0:T(8,128)(2,1)} %bitcast.93), channel_id=1, source_target_pairs={{0,32},{32,64},{64,96},{96,0},{1,33},{33,65},{65,97},{97,1},{2,34}... | collective-permute-start | bytes 4718600 | tf_op jit(solution)/shard_map/ppermute | solution.py:26
  3.4 38.3 %collective-permute-start.2 = (bf16[192,4096]{1,0:T(8,128)(2,1)}, bf16[192,4096]{1,0:T(8,128)(2,1)S(1)}, u32[]{:S(2)}, u32[]{:S(2)}) collective-permute-start(bf16[192,4096]{1,0:T(8,128)(2,1)} %bitcast.94), channel_id=1, source_target_pairs={{0,96},{32,0},{64,32},{96,64},{1,97},{33,1},{65,33},{97,65},{2,98}... | collective-permute-start | bytes 4718600 | tf_op jit(solution)/shard_map/ppermute | solution.py:26
  9.7 43.1 %collective-permute-start.4 = (bf16[192,4096]{1,0:T(8,128)(2,1)}, bf16[192,4096]{1,0:T(8,128)(2,1)}, u32[]{:S(2)}, u32[]{:S(2)}) collective-permute-start(bf16[192,4096]{1,0:T(8,128)(2,1)} %bitcast.95), channel_id=1, source_target_pairs={{0,256},{384,128},{128,0},{1,257},{385,129},{129,1},{2,258},{386,1... | collective-permute-start | bytes 4718600 | tf_op jit(solution)/shard_map/ppermute | solution.py:195
  12.0 3.1 %copy-start.1 = (bf16[256,256]{1,0:T(8,128)(2,1)S(1)}, bf16[256,256]{1,0:T(8,128)(2,1)}, u32[]{:S(2)}) copy-start(bf16[256,256]{1,0:T(8,128)(2,1)} %constant.67.clone.order_ref) | copy-start | bytes 393220
  15.0 1.4 %copy-start = (bf16[1,192,4096]{2,1,0:T(8,128)(2,1)S(1)}, bf16[1,192,4096]{2,1,0:T(8,128)(2,1)}, u32[]{:S(2)}) copy-start(bf16[1,192,4096]{2,1,0:T(8,128)(2,1)} %param.9) | copy-start | bytes 4718596
  16.4 1.0 copy-start.4
  17.4 1.0 copy-start.6
  23.8 1.3 copy-start.2
  25.2 53.9 %collective-permute-start.5 = (bf16[192,4096]{1,0:T(8,128)(2,1)}, bf16[192,4096]{1,0:T(8,128)(2,1)}, u32[]{:S(2)}, u32[]{:S(2)}) collective-permute-start(bf16[192,4096]{1,0:T(8,128)(2,1)} %get-tuple-element.17.refs_0_), channel_id=1, source_target_pairs={{0,384},{256,128},{384,256},{1,385},{257,129},{385,257},{2,386},{2... | collective-permute-start | bytes 4718600 | tf_op jit(solution)/shard_map/ppermute | solution.py:197
  30.6 13.8 %copy-start.5 = (bf16[256,768]{1,0:T(8,128)(2,1)S(1)}, bf16[256,768]{1,0:T(8,128)(2,1)}, u32[]{:S(2)}) copy-start(bf16[256,768]{1,0:T(8,128)(2,1)} %get-tuple-element.15.inner_ref) | copy-start | bytes 1179652
  30.6 13.8 %copy-start.7 = (bf16[256,768]{1,0:T(8,128)(2,1)S(1)}, bf16[256,768]{1,0:T(8,128)(2,1)}, u32[]{:S(2)}) copy-start(bf16[256,768]{1,0:T(8,128)(2,1)} %get-tuple-element.16.outer_ref) | copy-start | bytes 1179652
  38.3 20.1 %collective-permute-start.1 = (bf16[96,4096]{1,0:T(8,128)(2,1)S(1)}, bf16[96,4096]{1,0:T(8,128)(2,1)S(1)}, u32[]{:S(2)}, u32[]{:S(2)}) collective-permute-start(bf16[96,4096]{1,0:T(8,128)(2,1)S(1)} %slice.157), channel_id=1, source_target_pairs={{0,32},{32,64},{64,96},{96,0},{1,33},{33,65},{65,97},{97,1},{2,34}... | collective-permute-start | bytes 2359304 | tf_op jit(solution)/shard_map/ppermute | solution.py:26
  41.8 20.1 %collective-permute-start.3 = (bf16[96,4096]{1,0:T(8,128)(2,1)S(1)}, bf16[96,4096]{1,0:T(8,128)(2,1)S(1)}, u32[]{:S(2)}, u32[]{:S(2)}) collective-permute-start(bf16[96,4096]{1,0:T(8,128)(2,1)S(1)} %slice.158), channel_id=1, source_target_pairs={{0,96},{32,0},{64,32},{96,64},{1,97},{33,1},{65,33},{97,65},{2,98}... | collective-permute-start | bytes 2359304 | tf_op jit(solution)/shard_map/ppermute | solution.py:26
  62.0 4.5 %copy-start.3 = (bf16[4096,192]{1,0:T(8,128)(2,1)S(1)}, bf16[4096,192]{1,0:T(8,128)(2,1)}, u32[]{:S(2)}) copy-start(bf16[4096,192]{1,0:T(8,128)(2,1)} %copy-done.2) | copy-start | bytes 4718596
  89.0 35.9 %all-to-all-start.2 = ((f16[16,120,128]{2,1,0:T(8,128)(2,1)}), f16[16,120,128]{2,1,0:T(8,128)(2,1)S(1)}, u32[]{:S(2)}, u32[]{:S(2)}) async-start(f16[16,120,128]{2,1,0:T(8,128)(2,1)} %bitcast.16), calls=%async_computation.2 | async-start | bytes 983040 | tf_op jit(solution)/shard_map/all_to_all | solution.py:175
  126.6 12.6 %all-to-all-start.3 = ((f32[4,2,6,192]{3,1,2,0:T(2,128)}), f32[4,2,6,192]{3,1,2,0:T(2,128)S(1)}, u32[]{:S(2)}, u32[]{:S(2)}) async-start(f32[4,2,6,192]{3,1,2,0:T(2,128)} %copy.40), calls=%async_computation.3 | async-start | bytes 98304 | tf_op jit(solution)/shard_map/all_to_all | solution.py:228
  132.5 6.6 %collective-permute-start.6 = (f32[4,6,192]{2,0,1:T(4,128)S(1)}, f32[4,6,192]{2,0,1:T(4,128)S(1)}, u32[]{:S(2)}, u32[]{:S(2)}) collective-permute-start(f32[4,6,192]{2,0,1:T(4,128)S(1)} %pad_maximum_fusion.3), channel_id=1, source_target_pairs={{128,384},{256,0},{129,385},{257,1},{130,386},{258,2},{131,387},{2... | collective-permute-start | bytes 55304 | tf_op jit(solution)/shard_map/ppermute | solution.py:223

commit v10 on v8

--- a/solution.py
+++ b/solution.py
@@ -76,8 +76,8 @@
     return lax.dot_general(a, b, (dims, ((), ())), preferred_element_type=jnp.float32)
 
 
-def weigh_kernel(p_ref, inner_ref, outer_ref, order_ref, w_ref, *rest):
-    *copies, t_ref = rest
+def weigh_kernel(unused, p_ref, inner_ref, outer_ref, order_ref, *rest):
+    w_ref, *copies, t_ref = rest[unused:]
     tiles = p_ref.shape[1] // TILE
     for copy in copies:
         copy[...] = p_ref[...]
@@ -103,16 +103,18 @@
         w_ref[pl.ds(pl.multiple_of(b * TILE, TILE), TILE), :] = y.astype(jnp.bfloat16)
 
 
-def weigh(rows, tiles, copied=False):
+def weigh(rows, tiles, copied=False, later=()):
     width = rows.shape[1]
     out = jax.ShapeDtypeStruct((width, ROWS), jnp.bfloat16)
     return pl.pallas_call(
-        weigh_kernel,
+        functools.partial(weigh_kernel, len(later)),
         out_shape=(out, jax.ShapeDtypeStruct(rows.shape, rows.dtype)) if copied else out,
+        in_specs=[pl.BlockSpec(memory_space=pltpu.VMEM)] * (1 + len(tiles))
+        + [pl.BlockSpec(memory_space=pl.ANY)] * len(later),
         scratch_shapes=[pltpu.VMEM((width // TILE, TILE, ROWS), jnp.float32)],
         compiler_params=pltpu.CompilerParams(vmem_limit_bytes=24 * 2**20),
         cost_estimate=COST,
-    )(rows, *tiles)
+    )(rows, *tiles, *later)
 
 
 def products_kernel(picks, groups, n_p, n_w, place_ref, *refs):
@@ -201,7 +203,9 @@
     w0, own = weigh(p0, tiles, copied=True)
     p5 = lax.ppermute(own, "zl", [(0, 3), (2, 1), (3, 2)])
     p2 = jnp.concatenate([moved(p1[:half], "x", 1), moved(p3[half:], "x", -1)])
-    w1, w2, w3, w4 = (weigh(p, tiles) for p in (p1, p2, p3, p4))
+    w4 = weigh(p4, tiles)
+    w1, w3 = (weigh(p, tiles, later=(w4,)) for p in (p1, p3))
+    w2 = weigh(p2, tiles)
     early = products(
         [own, p1, p2, p3, p4],
         [w0, w1, w2, w3, w4],

time: 140 us -> 141 us (level)
    ppermute x1, waiting for transfers between devices: 5.94 us -> 0.01 us  [per_device(): p5 = lax.ppermute(own, 'zl', [(0, 3), (2, 1), (3, 2)])]
    ppermute x4, waiting for transfers between devices: 11 us -> 16.4 us  [moved(): lax.ppermute(value, axis, [(s, (s + steps) % count) for s in range(count)])]
    ppermute x4, starting transfers between devices: 15.8 us -> 11.9 us  [moved(): lax.ppermute(value, axis, [(s, (s + steps) % count) for s in range(count)])]
    ppermute x1, starting transfers between devices: 2.2 us -> 6.08 us  [per_device(): p4 = lax.ppermute(p0, 'zl', [(0, 2), (3, 1), (1, 0)])]
  transfers between devices with their start and end apart: 9 -> 9, of which waited for: 5 -> 4; matrix products, arithmetic and copies ran while one was open for 0% -> 0% of each run, Pallas kernels for 24% -> 24%
where the time goes in v10:
time: 141 us; the launch traced here: 140 us
  starting transfers between devices  44.4 us (31%)
  waiting for transfers between devices  42.8 us (30%)
  Pallas kernels  38.2 us (27%)
  local copies, waits for them, and re-layouts  7.01 us (5%)
  blocking collectives  5.31 us (4%)
  other arithmetic  1.8 us (1%)
    pallas_call x5, Pallas kernels, weigh(): pl.pallas_call(functools.partial(weigh_kernel, len(later)), out_shape=(ou...  23.8 us
    all_to_all x1, waiting for transfers between devices, chip_sum(): got = lax.all_to_all(sums, ('y', 'zh'), 0, 0, tiled=False)  21.1 us
    ppermute x4, waiting for transfers between devices, moved(): lax.ppermute(value, axis, [(s, (s + steps) % count) for s in range(count)])  16.4 us
    all_to_all x1, starting transfers between devices, chip_sum(): got = lax.all_to_all(sums, ('y', 'zh'), 0, 0, tiled=False)  13.9 us
    ppermute x4, starting transfers between devices, moved(): lax.ppermute(value, axis, [(s, (s + steps) % count) for s in range(count)])  11.9 us
    pallas_call x2, Pallas kernels, products(): pl.pallas_call(functools.partial(products_kernel, picks, groups, len(plai...  11.3 us
    ppermute x1, starting transfers between devices, per_device(): p4 = lax.ppermute(p0, 'zl', [(0, 2), (3, 1), (1, 0)])  6.08 us
    all_to_all x1, starting transfers between devices, per_device(): got = lax.all_to_all(sent, 'x', 0, 0, tiled=False)  5.93 us
  transfers between devices with their start and end apart: 9, of which 4 were waited for; matrix products, arithmetic and copies ran while one was open for 0% of the time, Pallas kernels for 24%

profile of v10, /device:TPU:2, one launch (start us, length us, event | category | flops | bytes accessed | tf_op | source)
XLA Modules:
  0.0 140.0 jit_solution(16890468141471940508)
XLA Ops:
  0.0 6.1 %collective-permute-start = (bf16[192,4096]{1,0:T(8,128)(2,1)}, bf16[192,4096]{1,0:T(8,128)(2,1)}, u32[]{:S(2)}, u32[]{:S(2)}) collective-permute-start(bf16[192,4096]{1,0:T(8,128)(2,1)} %bitcast.76), channel_id=1, source_target_pairs={{0,256},{384,128},{128,0},{1,257},{385,129},{129,1},{2,258},{386,1... | collective-permute-start | bytes 4718600 | tf_op jit(solution)/shard_map/ppermute | solution.py:202
  6.1 3.4 %collective-permute-start.2 = (bf16[192,4096]{1,0:T(8,128)(2,1)}, bf16[192,4096]{1,0:T(8,128)(2,1)S(1)}, u32[]{:S(2)}, u32[]{:S(2)}) collective-permute-start(bf16[192,4096]{1,0:T(8,128)(2,1)} %bitcast.77), channel_id=1, source_target_pairs={{0,32},{32,64},{64,96},{96,0},{1,33},{33,65},{65,97},{97,1},{2,34}... | collective-permute-start | bytes 4718600 | tf_op jit(solution)/shard_map/ppermute | solution.py:26
  9.5 2.4 %collective-permute-start.4 = (bf16[192,4096]{1,0:T(8,128)(2,1)}, bf16[192,4096]{1,0:T(8,128)(2,1)S(1)}, u32[]{:S(2)}, u32[]{:S(2)}) collective-permute-start(bf16[192,4096]{1,0:T(8,128)(2,1)} %bitcast.78), channel_id=1, source_target_pairs={{0,96},{32,0},{64,32},{96,64},{1,97},{33,1},{65,33},{97,65},{2,98}... | collective-permute-start | bytes 4718600 | tf_op jit(solution)/shard_map/ppermute | solution.py:26
  12.0 3.1 %shard_map.91 = (bf16[256,768]{1,0:T(8,128)(2,1)}, bf16[256,768]{1,0:T(8,128)(2,1)}) custom-call(f32[64,64]{1,0:T(8,128)} %bitcast.92, f32[64,64]{1,0:T(8,128)} %bitcast.93, f32[256,64]{1,0:T(8,128)} %constant.56.clone.four_ref, f32[256,64]{1,0:T(8,128)} %constant.57.clone.last_ref, f32[256,64]{1,0:T(8,128)} %constant.58.clone.mixed_ref, ...), custom_call_target="tpu_custom_call" | custom-call | flops 10000000000 | bytes 1000000 | tf_op jit(solution)/shard_map/pallas_call | solution.py:69
  15.0 1.4 %copy-done = bf16[1,192,4096]{2,1,0:T(8,128)(2,1)S(1)} copy-done((bf16[1,192,4096]{2,1,0:T(8,128)(2,1)S(1)}, bf16[1,192,4096]{2,1,0:T(8,128)(2,1)}, u32[]{:S(2)}) %copy-start) | copy-done | bytes 1572888
  18.4 5.4 %shard_map.92 = (bf16[4096,192]{1,0:T(8,128)(2,1)S(1)}, bf16[192,4096]{1,0:T(8,128)(2,1)}) custom-call(bf16[192,4096]{1,0:T(8,128)(2,1)S(1)} %bitcast.79, bf16[256,768]{1,0:T(8,128)(2,1)S(1)} %copy-done.4, bf16[256,768]{1,0:T(8,128)(2,1)S(1)} %copy-done.6, bf16[256,256]{1,0:T(8,128)(2,1)S(1)} %copy-done.1), custom_call_target="tpu_custom_call" | custom-call | flops 10000000000 | bytes 1000000 | tf_op jit(solution)/shard_map/pallas_call | solution.py:109
  23.8 1.3 copy-done.2
  25.2 5.4 %collective-permute-start.1 = (bf16[192,4096]{1,0:T(8,128)(2,1)}, bf16[192,4096]{1,0:T(8,128)(2,1)}, u32[]{:S(2)}, u32[]{:S(2)}) collective-permute-start(bf16[192,4096]{1,0:T(8,128)(2,1)} %get-tuple-element.17.refs_0_), channel_id=1, source_target_pairs={{0,384},{256,128},{384,256},{1,385},{257,129},{385,257},{2,386},{2... | collective-permute-start | bytes 4718600 | tf_op jit(solution)/shard_map/ppermute | solution.py:204
  30.6 13.4 %collective-permute-done.2.p_ref.refs_1_ = bf16[192,4096]{1,0:T(8,128)(2,1)S(1)} collective-permute-done((bf16[192,4096]{1,0:T(8,128)(2,1)}, bf16[192,4096]{1,0:T(8,128)(2,1)S(1)}, u32[]{:S(2)}, u32[]{:S(2)}) %collective-permute-start.2) | collective-permute-done | bytes 1572896 | tf_op jit(solution)/shard_map/ppermute | solution.py:26
  44.1 3.4 %collective-permute-start.3 = (bf16[96,4096]{1,0:T(8,128)(2,1)S(1)}, bf16[96,4096]{1,0:T(8,128)(2,1)S(1)}, u32[]{:S(2)}, u32[]{:S(2)}) collective-permute-start(bf16[96,4096]{1,0:T(8,128)(2,1)S(1)} %slice.137), channel_id=1, source_target_pairs={{0,32},{32,64},{64,96},{96,0},{1,33},{33,65},{65,97},{97,1},{2,34}... | collective-permute-start | bytes 2359304 | tf_op jit(solution)/shard_map/ppermute | solution.py:26
  47.6 2.6 %collective-permute-start.5 = (bf16[96,4096]{1,0:T(8,128)(2,1)S(1)}, bf16[96,4096]{1,0:T(8,128)(2,1)S(1)}, u32[]{:S(2)}, u32[]{:S(2)}) collective-permute-start(bf16[96,4096]{1,0:T(8,128)(2,1)S(1)} %slice.138), channel_id=1, source_target_pairs={{0,96},{32,0},{64,32},{96,64},{1,97},{33,1},{65,33},{97,65},{2,98}... | collective-permute-start | bytes 2359304 | tf_op jit(solution)/shard_map/ppermute | solution.py:26
  50.2 5.6 %shard_map.93.rest_0_.refs_9_ = bf16[4096,192]{1,0:T(8,128)(2,1)S(1)} custom-call(bf16[192,4096]{1,0:T(8,128)(2,1)} %collective-permute-done.p_ref.refs_4_.refs_0_, bf16[256,768]{1,0:T(8,128)(2,1)S(1)} %copy-done.5, bf16[256,768]{1,0:T(8,128)(2,1)S(1)} %copy-done.7, bf16[256,256]{1,0:T(8,128)(2,1)S(1)} %copy-done.1), custom_call_target="tpu_custom_call" | custom-call | flops 10000000000 | bytes 1000000 | tf_op jit(solution)/shard_map/pallas_call | solution.py:109
  55.9 4.2 %shard_map.94.refs_6_.refs_3_ = bf16[4096,192]{1,0:T(8,128)(2,1)S(1)} custom-call(bf16[192,4096]{1,0:T(8,128)(2,1)S(1)} %collective-permute-done.2.p_ref.refs_1_, bf16[256,768]{1,0:T(8,128)(2,1)S(1)} %copy-done.5, bf16[256,768]{1,0:T(8,128)(2,1)S(1)} %copy-done.7, bf16[256,256]{1,0:T(8,128)(2,1)S(1)} %copy-done.1, ...), custom_call_target="tpu_custom_call" | custom-call | flops 10000000000 | bytes 1000000 | tf_op jit(solution)/shard_map/pallas_call | solution.py:109
  60.0 4.2 %shard_map.96.refs_8_.refs_5_ = bf16[4096,192]{1,0:T(8,128)(2,1)S(1)} custom-call(bf16[192,4096]{1,0:T(8,128)(2,1)S(1)} %collective-permute-done.4.p_ref.refs_3_, bf16[256,768]{1,0:T(8,128)(2,1)S(1)} %copy-done.5, bf16[256,768]{1,0:T(8,128)(2,1)S(1)} %copy-done.7, bf16[256,256]{1,0:T(8,128)(2,1)S(1)} %copy-done.1, ...), custom_call_target="tpu_custom_call" | custom-call | flops 10000000000 | bytes 1000000 | tf_op jit(solution)/shard_map/pallas_call | solution.py:109
  64.3 3.0 %collective-permute-done.5 = bf16[96,4096]{1,0:T(8,128)(2,1)S(1)} collective-permute-done((bf16[96,4096]{1,0:T(8,128)(2,1)S(1)}, bf16[96,4096]{1,0:T(8,128)(2,1)S(1)}, u32[]{:S(2)}, u32[]{:S(2)}) %collective-permute-start.5) | collective-permute-done | bytes 786464 | tf_op jit(solution)/shard_map/ppermute | solution.py:26
  67.4 4.4 %shard_map.95.refs_7_.refs_4_ = bf16[4096,192]{1,0:T(8,128)(2,1)S(1)} custom-call(bf16[192,4096]{1,0:T(8,128)(2,1)S(1)} %constant_dynamic-update-slice_fusion.p_ref.refs_2_, bf16[256,768]{1,0:T(8,128)(2,1)S(1)} %copy-done.5, bf16[256,768]{1,0:T(8,128)(2,1)S(1)} %copy-done.7, bf16[256,256]{1,0:T(8,128)(2,1)S(1)} %copy-done.1), custom_call_target="tpu_custom_call" | custom-call | flops 10000000000 | bytes 1000000 | tf_op jit(solution)/shard_map/pallas_call | solution.py:109
  71.8 6.7 %shard_map.97.refs_6_ = f32[2,16,80,128]{3,2,1,0:T(8,128)S(1)} custom-call(s32[2]{0:T(128)S(1)} %pad_add_fusion.place_ref, bf16[192,4096]{1,0:T(8,128)(2,1)} %get-tuple-element.17.refs_0_, bf16[192,4096]{1,0:T(8,128)(2,1)S(1)} %collective-permute-done.2.p_ref.refs_1_, bf16[192,4096]{1,0:T(8,128)(2,1)S(1)} %constant_dynamic-update-slice_fusion.p_ref.refs_2_, ...), custom_call_target="tpu_custom_call" | custom-call | flops 10000000000 | bytes 1000000 | tf_op jit(solution)/shard_map/pallas_call | solution.py:158
  78.6 4.6 %shard_map.98 = f32[2,16,120,128]{3,2,1,0:T(8,128)S(1)} custom-call(s32[2]{0:T(128)S(1)} %pad_add_fusion.place_ref, bf16[192,4096]{1,0:T(8,128)(2,1)} %collective-permute-done.p_ref.refs_4_.refs_0_, bf16[192,4096]{1,0:T(8,128)(2,1)} %collective-permute-done.1.refs_1_, bf16[4096,192]{1,0:T(8,128)(2,1)S(1)} %copy-done.3, ...), custom_call_target="tpu_custom_call" | custom-call | flops 10000000000 | bytes 1000000 | tf_op jit(solution)/shard_map/pallas_call | solution.py:158
  83.2 5.3 %all_to_all.15 = f32[2,16,120,128]{3,2,1,0:T(8,128)S(1)} all-to-all(f32[2,16,120,128]{3,2,1,0:T(8,128)S(1)} %shard_map.98), channel_id=1, replica_groups=mesh['zl'=4,'x'=4,'y'=8,'zh'=2,'c'=2] {'c'}, dimensions={0} | all-to-all | bytes 3932160 | tf_op jit(solution)/shard_map/all_to_all | solution.py:170
  89.8 13.9 %all-to-all-start.1 = ((f16[16,120,128]{2,1,0:T(8,128)(2,1)}), f16[16,120,128]{2,1,0:T(8,128)(2,1)S(1)}, u32[]{:S(2)}, u32[]{:S(2)}) async-start(f16[16,120,128]{2,1,0:T(8,128)(2,1)} %bitcast.9), calls=%async_computation.1 | async-start | bytes 983040 | tf_op jit(solution)/shard_map/all_to_all | solution.py:182
  103.7 21.1 %all-to-all-done.1 = f16[16,120,128]{2,1,0:T(8,128)(2,1)S(1)} async-done(((f16[16,120,128]{2,1,0:T(8,128)(2,1)}), f16[16,120,128]{2,1,0:T(8,128)(2,1)S(1)}, u32[]{:S(2)}, u32[]{:S(2)}) %all-to-all-start.1) | async-done | bytes 491552 | tf_op jit(solution)/shard_map/all_to_all | solution.py:182
  126.5 5.9 %all-to-all-start.2 = ((f32[4,2,6,192]{3,1,2,0:T(2,128)}), f32[4,2,6,192]{3,1,2,0:T(2,128)S(1)}, u32[]{:S(2)}, u32[]{:S(2)}) async-start(f32[4,2,6,192]{3,1,2,0:T(2,128)} %copy.48), calls=%async_computation.2 | async-start | bytes 98304 | tf_op jit(solution)/shard_map/all_to_all | solution.py:237
  132.5 1.3 collective-permute-start.6
  133.8 5.2 %collective-permute-done.6 = f32[4,6,192]{2,0,1:T(4,128)S(1)} collective-permute-done((f32[4,6,192]{2,0,1:T(4,128)S(1)}, f32[4,6,192]{2,0,1:T(4,128)S(1)}, u32[]{:S(2)}, u32[]{:S(2)}) %collective-permute-start.6) | collective-permute-done | bytes 18464 | tf_op jit(solution)/shard_map/ppermute | solution.py:232
  (66 shorter events, 6.1 us)
Async XLA Ops:
  0.0 50.2 %collective-permute-start = (bf16[192,4096]{1,0:T(8,128)(2,1)}, bf16[192,4096]{1,0:T(8,128)(2,1)}, u32[]{:S(2)}, u32[]{:S(2)}) collective-permute-start(bf16[192,4096]{1,0:T(8,128)(2,1)} %bitcast.76), channel_id=1, source_target_pairs={{0,256},{384,128},{128,0},{1,257},{385,129},{129,1},{2,258},{386,1... | collective-permute-start | bytes 4718600 | tf_op jit(solution)/shard_map/ppermute | solution.py:202
  6.1 38.0 %collective-permute-start.2 = (bf16[192,4096]{1,0:T(8,128)(2,1)}, bf16[192,4096]{1,0:T(8,128)(2,1)S(1)}, u32[]{:S(2)}, u32[]{:S(2)}) collective-permute-start(bf16[192,4096]{1,0:T(8,128)(2,1)} %bitcast.77), channel_id=1, source_target_pairs={{0,32},{32,64},{64,96},{96,0},{1,33},{33,65},{65,97},{97,1},{2,34}... | collective-permute-start | bytes 4718600 | tf_op jit(solution)/shard_map/ppermute | solution.py:26
  9.5 38.0 %collective-permute-start.4 = (bf16[192,4096]{1,0:T(8,128)(2,1)}, bf16[192,4096]{1,0:T(8,128)(2,1)S(1)}, u32[]{:S(2)}, u32[]{:S(2)}) collective-permute-start(bf16[192,4096]{1,0:T(8,128)(2,1)} %bitcast.78), channel_id=1, source_target_pairs={{0,96},{32,0},{64,32},{96,64},{1,97},{33,1},{65,33},{97,65},{2,98}... | collective-permute-start | bytes 4718600 | tf_op jit(solution)/shard_map/ppermute | solution.py:26
  12.0 3.1 %copy-start.1 = (bf16[256,256]{1,0:T(8,128)(2,1)S(1)}, bf16[256,256]{1,0:T(8,128)(2,1)}, u32[]{:S(2)}) copy-start(bf16[256,256]{1,0:T(8,128)(2,1)} %constant.61.clone.order_ref) | copy-start | bytes 393220
  15.0 1.4 %copy-start = (bf16[1,192,4096]{2,1,0:T(8,128)(2,1)S(1)}, bf16[1,192,4096]{2,1,0:T(8,128)(2,1)}, u32[]{:S(2)}) copy-start(bf16[1,192,4096]{2,1,0:T(8,128)(2,1)} %param.9) | copy-start | bytes 4718596
  16.4 1.0 copy-start.4
  17.4 1.0 copy-start.6
  23.8 1.3 copy-start.2
  25.2 53.4 %collective-permute-start.1 = (bf16[192,4096]{1,0:T(8,128)(2,1)}, bf16[192,4096]{1,0:T(8,128)(2,1)}, u32[]{:S(2)}, u32[]{:S(2)}) collective-permute-start(bf16[192,4096]{1,0:T(8,128)(2,1)} %get-tuple-element.17.refs_0_), channel_id=1, source_target_pairs={{0,384},{256,128},{384,256},{1,385},{257,129},{385,257},{2,386},{2... | collective-permute-start | bytes 4718600 | tf_op jit(solution)/shard_map/ppermute | solution.py:204
  30.6 19.6 %copy-start.5 = (bf16[256,768]{1,0:T(8,128)(2,1)S(1)}, bf16[256,768]{1,0:T(8,128)(2,1)}, u32[]{:S(2)}) copy-start(bf16[256,768]{1,0:T(8,128)(2,1)} %get-tuple-element.15.inner_ref) | copy-start | bytes 1179652
  30.6 19.6 %copy-start.7 = (bf16[256,768]{1,0:T(8,128)(2,1)S(1)}, bf16[256,768]{1,0:T(8,128)(2,1)}, u32[]{:S(2)}) copy-start(bf16[256,768]{1,0:T(8,128)(2,1)} %get-tuple-element.16.outer_ref) | copy-start | bytes 1179652
  44.1 20.1 %collective-permute-start.3 = (bf16[96,4096]{1,0:T(8,128)(2,1)S(1)}, bf16[96,4096]{1,0:T(8,128)(2,1)S(1)}, u32[]{:S(2)}, u32[]{:S(2)}) collective-permute-start(bf16[96,4096]{1,0:T(8,128)(2,1)S(1)} %slice.137), channel_id=1, source_target_pairs={{0,32},{32,64},{64,96},{96,0},{1,33},{33,65},{65,97},{97,1},{2,34}... | collective-permute-start | bytes 2359304 | tf_op jit(solution)/shard_map/ppermute | solution.py:26
  47.6 19.7 %collective-permute-start.5 = (bf16[96,4096]{1,0:T(8,128)(2,1)S(1)}, bf16[96,4096]{1,0:T(8,128)(2,1)S(1)}, u32[]{:S(2)}, u32[]{:S(2)}) collective-permute-start(bf16[96,4096]{1,0:T(8,128)(2,1)S(1)} %slice.138), channel_id=1, source_target_pairs={{0,96},{32,0},{64,32},{96,64},{1,97},{33,1},{65,33},{97,65},{2,98}... | collective-permute-start | bytes 2359304 | tf_op jit(solution)/shard_map/ppermute | solution.py:26
  67.3 4.5 %copy-start.3 = (bf16[4096,192]{1,0:T(8,128)(2,1)S(1)}, bf16[4096,192]{1,0:T(8,128)(2,1)}, u32[]{:S(2)}) copy-start(bf16[4096,192]{1,0:T(8,128)(2,1)} %copy-done.2) | copy-start | bytes 4718596
  89.8 35.0 %all-to-all-start.1 = ((f16[16,120,128]{2,1,0:T(8,128)(2,1)}), f16[16,120,128]{2,1,0:T(8,128)(2,1)S(1)}, u32[]{:S(2)}, u32[]{:S(2)}) async-start(f16[16,120,128]{2,1,0:T(8,128)(2,1)} %bitcast.9), calls=%async_computation.1 | async-start | bytes 983040 | tf_op jit(solution)/shard_map/all_to_all | solution.py:182
  126.5 12.6 %all-to-all-start.2 = ((f32[4,2,6,192]{3,1,2,0:T(2,128)}), f32[4,2,6,192]{3,1,2,0:T(2,128)S(1)}, u32[]{:S(2)}, u32[]{:S(2)}) async-start(f32[4,2,6,192]{3,1,2,0:T(2,128)} %copy.48), calls=%async_computation.2 | async-start | bytes 98304 | tf_op jit(solution)/shard_map/all_to_all | solution.py:237
  132.5 6.6 %collective-permute-start.6 = (f32[4,6,192]{2,0,1:T(4,128)S(1)}, f32[4,6,192]{2,0,1:T(4,128)S(1)}, u32[]{:S(2)}, u32[]{:S(2)}) collective-permute-start(f32[4,6,192]{2,0,1:T(4,128)S(1)} %pad_maximum_fusion.3), channel_id=1, source_target_pairs={{128,384},{256,0},{129,385},{257,1},{130,386},{258,2},{131,387},{2... | collective-permute-start | bytes 55304 | tf_op jit(solution)/shard_map/ppermute | solution.py:232
